TPU v7x, 32 devices: a whole 2x2x4 slice. The times are simulated.
32 devices in a mesh: ctx: 2 (over core), fsdp: 16 (over z, y, x).
Axes of the slice: x: 2, y: 2, z: 4, core: 2. Of those that a mesh axis runs over, the one named last changes fastest.
Arguments:
- tokens: bfloat16 [64, 1024, 1024], P('fsdp', 'ctx'), may hold values from -6 to 6
- cotangent: bfloat16 [64, 1024, 1024], P('fsdp', 'ctx'), may hold values from -6 to 6
- lengths: int32 [64], P('fsdp'), may hold values from 256 to 1024, as said below
- norm_gain: bfloat16 [1024], P('fsdp'), may hold values from 0.099609375 to 1.8984375
- query_weight: bfloat16 [1024, 1024], P('fsdp'), may hold values from -0.078125 to 0.078125
- key_weight: bfloat16 [1024, 1024], P('fsdp'), may hold values from -0.078125 to 0.078125
- value_weight: bfloat16 [1024, 1024], P('fsdp'), may hold values from -0.1875 to 0.1875
- output_weight: bfloat16 [1024, 1024], P('fsdp'), may hold values from -1.5 to 1.5
- ffn_gain: bfloat16 [1024], P('fsdp'), may hold values from 0.099609375 to 1.8984375
- inner_weight: bfloat16 [1024, 4096], P('fsdp'), may hold values from -0.1875 to 0.1875
- outer_weight: bfloat16 [4096, 1024], P('fsdp'), may hold values from -0.09375 to 0.09375
- bias_table: bfloat16 [32, 16], P('fsdp'), may hold values from -4 to 4
Outputs:
- layer_out: bfloat16 [64, 1024, 1024], P('fsdp', 'ctx')
- token_grad: float32 [64, 1024, 1024], P('fsdp', 'ctx')
- norm_gain_grad: float32 [1024], P('fsdp')
- query_grad: float32 [1024, 1024], P('fsdp')
- key_grad: float32 [1024, 1024], P('fsdp')
- value_grad: float32 [1024, 1024], P('fsdp')
- output_grad: float32 [1024, 1024], P('fsdp')
- ffn_gain_grad: float32 [1024], P('fsdp')
- inner_grad: float32 [1024, 4096], P('fsdp')
- outer_grad: float32 [4096, 1024], P('fsdp')
- table_grad: float32 [32, 16], P('fsdp')
Inputs may be any that keep to these rules, and one draw needn't show every extreme that they name: The first lengths[s] positions of sequence s are live; one sequence of each index of fsdp has all 1024.
All inputs are finite; a program needn't handle non-finite values.
Results may differ from a plain program's by a relative error of at most 0.023.
Values may be sent and summed in bfloat16 or wider, within the bound.
A program may use at most 472 MiB of HBM per device.

v0:
```python
import jax
import jax.numpy as jnp
import numpy as np
from jax import lax
from jax.sharding import PartitionSpec as P

MB = 4


eps_norm = 1e-06
neg_large = -1e30
gelu_coef = 0.7978845608028654


def bucket_edges():
    distance = np.arange(1, 512)
    scaled = 8 + np.floor(np.log(distance / 8.0) / np.log(16.0) * 8.0)
    bucket_level = np.where(distance < 8, distance, np.minimum(15, scaled))
    return np.array([distance[bucket_level >= target][0] for target in range(1, 16)], np.int32)


def bucket_onehot(query_pos, key_pos, bucket_count):
    offset = key_pos[None, :] - query_pos[:, None]
    magnitude = jnp.abs(offset)
    bucket_bound = jnp.asarray(bucket_edges())
    bucket_level = jnp.sum((magnitude[:, :, None] >= bucket_bound).astype(jnp.int32), axis=2)
    bucket_level = bucket_level + 16 * (offset > 0).astype(jnp.int32)
    return (bucket_level[:, :, None] == jnp.arange(bucket_count, dtype=jnp.int32)).astype(
        jnp.bfloat16
    )


def root_norm(row_values, gain_values):
    inv_root = lax.rsqrt(jnp.mean(row_values * row_values, axis=-1, keepdims=True) + eps_norm)
    return row_values * inv_root * gain_values


def smooth_gelu(row_values):
    return (
        0.5
        * row_values
        * (
            1.0
            + jnp.tanh(gelu_coef * (row_values + 0.044715 * row_values * row_values * row_values))
        )
    )


def fetch_each(
    norm_gain,
    query_weight,
    key_weight,
    value_weight,
    output_weight,
    ffn_gain,
    inner_weight,
    outer_weight,
    bias_table,
):
    return (
        lax.all_gather(norm_gain, "fsdp", axis=0, tiled=True),
        lax.all_gather(query_weight, "fsdp", axis=0, tiled=True),
        lax.all_gather(key_weight, "fsdp", axis=0, tiled=True),
        lax.all_gather(value_weight, "fsdp", axis=0, tiled=True),
        lax.all_gather(output_weight, "fsdp", axis=0, tiled=True),
        lax.all_gather(ffn_gain, "fsdp", axis=0, tiled=True),
        lax.all_gather(inner_weight, "fsdp", axis=0, tiled=True),
        lax.all_gather(outer_weight, "fsdp", axis=0, tiled=True),
        lax.all_gather(bias_table, "fsdp", axis=0, tiled=True),
    )


def position_bias(onehot, table_rows):
    return jnp.einsum("ijb,bh->hij", onehot, table_rows, preferred_element_type=jnp.float32)


def attend_stats(query_low, key_all, bias_rows, live_keys, head_count):
    seq_count, block_len, model_width = query_low.shape
    seq_len = key_all.shape[1]
    head_dim = model_width // head_count
    query_four = query_low.reshape(seq_count, block_len, head_count, head_dim)
    key_four = key_all.reshape(seq_count, seq_len, head_count, head_dim)
    raw_scores = jnp.einsum(
        "sihd,sjhd->shij", query_four, key_four, preferred_element_type=jnp.float32
    )
    scores = jnp.where(live_keys[:, None, None, :], raw_scores + bias_rows[None], neg_large)
    row_max = jnp.max(scores, axis=-1, keepdims=True)
    exp_scores = jnp.exp(scores - row_max)
    row_total = jnp.sum(exp_scores, axis=-1, keepdims=True)
    return (exp_scores / row_total, row_max[..., 0], row_total[..., 0])


def per_device(
    tokens,
    cotangent,
    lengths,
    norm_gain,
    query_weight,
    key_weight,
    value_weight,
    output_weight,
    ffn_gain,
    inner_weight,
    outer_weight,
    bias_table,
):
    groups, block_len, model_width = tokens.shape
    seq_len = block_len * lax.axis_size("ctx")
    fsdp_count = lax.axis_size("fsdp")
    head_count = bias_table.shape[1]
    head_dim = model_width // head_count
    bucket_count = bias_table.shape[0] * fsdp_count
    per_micro = groups // MB
    query_pos = lax.axis_index("ctx") * block_len + jnp.arange(block_len, dtype=jnp.int32)
    key_pos = jnp.arange(seq_len, dtype=jnp.int32)
    onehot = bucket_onehot(query_pos, key_pos, bucket_count)
    totals = [
        jnp.zeros((piece.shape[0] * fsdp_count,) + piece.shape[1:], jnp.float32)
        for piece in (
            norm_gain,
            query_weight,
            key_weight,
            value_weight,
            output_weight,
            ffn_gain,
            inner_weight,
            outer_weight,
            bias_table,
        )
    ]
    layer_parts = []
    grad_parts = []
    for micro_index in range(MB):
        first_seq = micro_index * per_micro
        end_seq = first_seq + per_micro
        fetched = fetch_each(
            norm_gain,
            query_weight,
            key_weight,
            value_weight,
            output_weight,
            ffn_gain,
            inner_weight,
            outer_weight,
            bias_table,
        )
        (
            gain_one,
            weight_query,
            weight_key,
            weight_value,
            weight_output,
            gain_two,
            weight_inner,
            weight_outer,
            table_rows,
        ) = fetched
        token_rows = tokens[first_seq:end_seq].astype(jnp.float32).reshape(-1, model_width)
        length_micro = lengths[first_seq:end_seq]
        normed, norm_pull = jax.vjp(root_norm, token_rows, gain_one.astype(jnp.float32))
        normed_low = normed.astype(jnp.bfloat16)
        query_low = jnp.dot(normed_low, weight_query, preferred_element_type=jnp.float32).astype(
            jnp.bfloat16
        )
        key_low = jnp.dot(normed_low, weight_key, preferred_element_type=jnp.float32).astype(
            jnp.bfloat16
        )
        value_low = jnp.dot(normed_low, weight_value, preferred_element_type=jnp.float32).astype(
            jnp.bfloat16
        )
        key_blocks = key_low.reshape(per_micro, block_len, model_width)
        value_blocks = value_low.reshape(per_micro, block_len, model_width)
        key_all, value_all = (
            lax.all_gather(key_blocks, "ctx", axis=1, tiled=True),
            lax.all_gather(value_blocks, "ctx", axis=1, tiled=True),
        )
        bias_rows = position_bias(onehot, table_rows)
        live_keys = key_pos[None, :] < length_micro[:, None]
        query_three = query_low.reshape(per_micro, block_len, model_width)
        attn_probs, row_max, row_total = attend_stats(
            query_three, key_all, bias_rows, live_keys, head_count
        )
        probs_low = attn_probs.astype(jnp.bfloat16)
        value_four = value_all.reshape(per_micro, seq_len, head_count, head_dim)
        mixed = jnp.einsum(
            "shij,sjhd->sihd", probs_low, value_four, preferred_element_type=jnp.float32
        )
        mixed_low = mixed.reshape(-1, model_width).astype(jnp.bfloat16)
        residual = token_rows + jnp.dot(
            mixed_low, weight_output, preferred_element_type=jnp.float32
        )
        normed_ffn, ffn_pull = jax.vjp(root_norm, residual, gain_two.astype(jnp.float32))
        normed_ffn_low = normed_ffn.astype(jnp.bfloat16)
        inner_act = jnp.dot(normed_ffn_low, weight_inner, preferred_element_type=jnp.float32)
        hidden, gelu_pull = jax.vjp(smooth_gelu, inner_act)
        hidden_low = hidden.astype(jnp.bfloat16)
        layer_rows = residual + jnp.dot(
            hidden_low, weight_outer, preferred_element_type=jnp.float32
        )
        layer_parts.append(
            layer_rows.astype(jnp.bfloat16).reshape(per_micro, block_len, model_width)
        )
        fetched = fetch_each(
            norm_gain,
            query_weight,
            key_weight,
            value_weight,
            output_weight,
            ffn_gain,
            inner_weight,
            outer_weight,
            bias_table,
        )
        (
            gain_one,
            weight_query,
            weight_key,
            weight_value,
            weight_output,
            gain_two,
            weight_inner,
            weight_outer,
            table_rows,
        ) = fetched
        live_rows = (query_pos[None, :] < length_micro[:, None]).astype(jnp.float32).reshape(-1, 1)
        grad_out = (
            cotangent[first_seq:end_seq].astype(jnp.float32).reshape(-1, model_width) * live_rows
        )
        grad_out_low = grad_out.astype(jnp.bfloat16)
        totals[7] = totals[7] + jnp.einsum(
            "rf,rd->fd", hidden_low, grad_out_low, preferred_element_type=jnp.float32
        )
        grad_hidden = jnp.einsum(
            "rd,fd->rf", grad_out_low, weight_outer, preferred_element_type=jnp.float32
        )
        grad_inner = gelu_pull(grad_hidden)[0].astype(jnp.bfloat16)
        totals[6] = totals[6] + jnp.einsum(
            "rd,rf->df", normed_ffn_low, grad_inner, preferred_element_type=jnp.float32
        )
        grad_normed_ffn = jnp.einsum(
            "rf,df->rd", grad_inner, weight_inner, preferred_element_type=jnp.float32
        )
        grad_residual_part, grad_gain_two = ffn_pull(grad_normed_ffn)
        totals[5] = totals[5] + grad_gain_two
        grad_residual = grad_out + grad_residual_part
        grad_residual_low = grad_residual.astype(jnp.bfloat16)
        totals[4] = totals[4] + jnp.einsum(
            "rd,re->de", mixed_low, grad_residual_low, preferred_element_type=jnp.float32
        )
        grad_mixed = jnp.einsum(
            "re,de->rd", grad_residual_low, weight_output, preferred_element_type=jnp.float32
        ).astype(jnp.bfloat16)
        key_all, value_all = (
            lax.all_gather(key_blocks, "ctx", axis=1, tiled=True),
            lax.all_gather(value_blocks, "ctx", axis=1, tiled=True),
        )
        bias_rows = position_bias(onehot, table_rows)
        attn_probs, row_max, row_total = attend_stats(
            query_three, key_all, bias_rows, live_keys, head_count
        )
        probs_low = attn_probs.astype(jnp.bfloat16)
        key_four = key_all.reshape(per_micro, seq_len, head_count, head_dim)
        value_four = value_all.reshape(per_micro, seq_len, head_count, head_dim)
        query_four = query_low.reshape(per_micro, block_len, head_count, head_dim)
        grad_mixed_four = grad_mixed.reshape(per_micro, block_len, head_count, head_dim)
        grad_probs = jnp.einsum(
            "sihd,sjhd->shij", grad_mixed_four, value_four, preferred_element_type=jnp.float32
        )
        prob_dot = jnp.sum(attn_probs * grad_probs, axis=-1, keepdims=True)
        grad_scores = attn_probs * (grad_probs - prob_dot)
        scores_low = grad_scores.astype(jnp.bfloat16)
        totals[8] = totals[8] + jnp.einsum(
            "shij,ijb->bh", scores_low, onehot, preferred_element_type=jnp.float32
        )
        grad_queries = (
            jnp.einsum("shij,sjhd->sihd", scores_low, key_four, preferred_element_type=jnp.float32)
            .reshape(-1, model_width)
            .astype(jnp.bfloat16)
        )
        key_term = jnp.einsum(
            "shij,sihd->sjhd", scores_low, query_four, preferred_element_type=jnp.float32
        ).reshape(per_micro, seq_len, model_width)
        value_term = jnp.einsum(
            "shij,sihd->sjhd", probs_low, grad_mixed_four, preferred_element_type=jnp.float32
        ).reshape(per_micro, seq_len, model_width)
        key_sum, value_sum = (
            lax.psum_scatter(
                key_term.astype(jnp.bfloat16), "ctx", scatter_dimension=1, tiled=True
            ).astype(jnp.float32),
            lax.psum_scatter(
                value_term.astype(jnp.bfloat16), "ctx", scatter_dimension=1, tiled=True
            ).astype(jnp.float32),
        )
        grad_keys = key_sum.reshape(-1, model_width).astype(jnp.bfloat16)
        grad_values = value_sum.reshape(-1, model_width).astype(jnp.bfloat16)
        totals[1] = totals[1] + jnp.einsum(
            "rd,re->de", normed_low, grad_queries, preferred_element_type=jnp.float32
        )
        totals[2] = totals[2] + jnp.einsum(
            "rd,re->de", normed_low, grad_keys, preferred_element_type=jnp.float32
        )
        totals[3] = totals[3] + jnp.einsum(
            "rd,re->de", normed_low, grad_values, preferred_element_type=jnp.float32
        )
        grad_normed = jnp.einsum(
            "re,de->rd", grad_queries, weight_query, preferred_element_type=jnp.float32
        )
        grad_normed = grad_normed + jnp.einsum(
            "re,de->rd", grad_keys, weight_key, preferred_element_type=jnp.float32
        )
        grad_normed = grad_normed + jnp.einsum(
            "re,de->rd", grad_values, weight_value, preferred_element_type=jnp.float32
        )
        grad_token_part, grad_gain_one = norm_pull(grad_normed)
        totals[0] = totals[0] + grad_gain_one
        grad_parts.append(
            (grad_residual + grad_token_part).reshape(per_micro, block_len, model_width)
        )
    owned = (
        lax.psum_scatter(
            totals[0].astype(jnp.bfloat16), "fsdp", scatter_dimension=0, tiled=True
        ).astype(jnp.float32),
        lax.psum_scatter(
            totals[1].astype(jnp.bfloat16), "fsdp", scatter_dimension=0, tiled=True
        ).astype(jnp.float32),
        lax.psum_scatter(
            totals[2].astype(jnp.bfloat16), "fsdp", scatter_dimension=0, tiled=True
        ).astype(jnp.float32),
        lax.psum_scatter(
            totals[3].astype(jnp.bfloat16), "fsdp", scatter_dimension=0, tiled=True
        ).astype(jnp.float32),
        lax.psum_scatter(
            totals[4].astype(jnp.bfloat16), "fsdp", scatter_dimension=0, tiled=True
        ).astype(jnp.float32),
        lax.psum_scatter(
            totals[5].astype(jnp.bfloat16), "fsdp", scatter_dimension=0, tiled=True
        ).astype(jnp.float32),
        lax.psum_scatter(
            totals[6].astype(jnp.bfloat16), "fsdp", scatter_dimension=0, tiled=True
        ).astype(jnp.float32),
        lax.psum_scatter(
            totals[7].astype(jnp.bfloat16), "fsdp", scatter_dimension=0, tiled=True
        ).astype(jnp.float32),
        lax.psum_scatter(
            totals[8].astype(jnp.bfloat16), "fsdp", scatter_dimension=0, tiled=True
        ).astype(jnp.float32),
    )
    summed = (
        lax.psum(owned[0].astype(jnp.bfloat16), "ctx").astype(jnp.float32),
        lax.psum(owned[1].astype(jnp.bfloat16), "ctx").astype(jnp.float32),
        lax.psum(owned[2].astype(jnp.bfloat16), "ctx").astype(jnp.float32),
        lax.psum(owned[3].astype(jnp.bfloat16), "ctx").astype(jnp.float32),
        lax.psum(owned[4].astype(jnp.bfloat16), "ctx").astype(jnp.float32),
        lax.psum(owned[5].astype(jnp.bfloat16), "ctx").astype(jnp.float32),
        lax.psum(owned[6].astype(jnp.bfloat16), "ctx").astype(jnp.float32),
        lax.psum(owned[7].astype(jnp.bfloat16), "ctx").astype(jnp.float32),
        lax.psum(owned[8].astype(jnp.bfloat16), "ctx").astype(jnp.float32),
    )
    layer_out = jnp.concatenate(layer_parts, axis=0)
    token_grad = jnp.concatenate(grad_parts, axis=0)
    return (
        layer_out,
        token_grad,
        summed[0],
        summed[1],
        summed[2],
        summed[3],
        summed[4],
        summed[5],
        summed[6],
        summed[7],
        summed[8],
    )


def solution(mesh):
    in_specs = (
        P("fsdp", "ctx", None),
        P("fsdp", "ctx", None),
        P("fsdp"),
        P("fsdp"),
        P("fsdp", None),
        P("fsdp", None),
        P("fsdp", None),
        P("fsdp", None),
        P("fsdp"),
        P("fsdp", None),
        P("fsdp", None),
        P("fsdp", None),
    )
    out_specs = (
        P("fsdp", "ctx", None),
        P("fsdp", "ctx", None),
        P("fsdp"),
        P("fsdp", None),
        P("fsdp", None),
        P("fsdp", None),
        P("fsdp", None),
        P("fsdp"),
        P("fsdp", None),
        P("fsdp", None),
        P("fsdp", None),
    )
    return jax.shard_map(
        per_device, mesh=mesh, in_specs=in_specs, out_specs=out_specs, check_vma=False
    )
```

profile of v0, /device:TPU:0, one launch (start us, length us, event | category | flops | bytes accessed | tf_op | source)
XLA Modules:
  0.0 2034.0 jit_solution(7495724767135460007)
XLA Ops:
  13.1 43.7 %all-reduce.6 = (bf16[1024]{0:T(1024)(128)(2,1)S(1)}, bf16[1024]{0:T(1024)(128)(2,1)S(1)}) all-reduce(bf16[1024]{0:T(1024)(128)(2,1)S(1)} %dynamic-update-slice, bf16[1024]{0:T(1024)(128)(2,1)S(1)} %dynamic-update-slice.1), channel_id=1, replica_groups=mesh['ctx'=2,'fsdp'=16] {'fsdp'}, use_global_device_ids=true, to_apply=%add | all-reduce | flops 2048 | bytes 8192
  59.9 14.5 all-gather.28.cloned.1.call-done
  82.4 54.1 %all-gather.24.cloned.1.call-done = bf16[1024,1024]{1,0:T(8,128)(2,1)} async-done(((bf16[64,1024]{1,0:T(8,128)(2,1)}), bf16[1024,1024]{1,0:T(8,128)(2,1)}) %all-gather.24.cloned.1.call-update) | async-done | bytes 2097168 | tf_op jit(solution)/shard_map/all_gather | solution.py:64
  171.6 38.4 %all-gather.8 = bf16[16,2,16]{2,1,0:T(2,128)(2,1)S(1)} all-gather(bf16[1,2,16]{2,1,0:T(2,128)(2,1)S(1)} %bitcast.563), channel_id=1, replica_groups=mesh['ctx'=2,'fsdp'=16] {'fsdp'}, dimensions={0}, use_global_device_ids=true | all-gather | bytes 1088 | tf_op jit(solution)/shard_map/all_gather | solution.py:69
  215.2 16.4 fusion.8
  252.8 35.3 %fusion.12 = f32[16,512,1024]{2,1,0:T(8,128)} fusion(f32[512,1024,16]{1,2,0:T(8,128)} %fusion.8, pred[1024]{0:T(1024)(128)(4,1)S(1)} %iota_compare_fusion.22, bf16[512,16,64]{0,2,1:T(8,128)(2,1)S(1)} %bitcast.514, bf16[1024,16,64]{0,2,1:T(8,128)(2,1)S(1)} %bitcast.506), kind=kOutput, calls=%fused_computation.17 | convolution fusion | flops 1090519040 | bytes 70255616 | tf_op jit(solution)/shard_map/sihd,sjhd->shij/dot_general | solution.py:83
  288.1 36.9 %fusion.300 = (f32[16,512]{1,0:T(8,128)S(1)}, f32[16,512,1024]{2,1,0:T(8,128)}) fusion(f32[16,512,1024]{2,1,0:T(8,128)} %fusion.12), kind=kOutput, calls=%fused_computation.372 | output fusion | flops 16778240 | bytes 67141632 | tf_op jit(solution)/shard_map/sub | solution.py:88
  328.0 35.1 %fusion.11 = f32[16,512,1024]{2,1,0:T(8,128)} fusion(f32[512,1024,16]{1,2,0:T(8,128)} %fusion.8, pred[1024]{0:T(1024)(128)(4,1)S(1)} %iota_compare_fusion.23, bf16[512,16,64]{0,2,1:T(8,128)(2,1)S(1)} %bitcast.518, bf16[1024,16,64]{0,2,1:T(8,128)(2,1)S(1)} %bitcast.508), kind=kOutput, calls=%fused_computation.16 | convolution fusion | flops 1090519040 | bytes 70255616 | tf_op jit(solution)/shard_map/sihd,sjhd->shij/dot_general | solution.py:83
  363.1 36.8 %fusion.301 = (f32[16,512]{1,0:T(8,128)S(1)}, f32[16,512,1024]{2,1,0:T(8,128)}) fusion(f32[16,512,1024]{2,1,0:T(8,128)} %fusion.11), kind=kOutput, calls=%fused_computation.373 | output fusion | flops 16778240 | bytes 67141632 | tf_op jit(solution)/shard_map/sub | solution.py:88
  402.8 32.3 %fusion.153 = bf16[16,64,512]{2,1,0:T(8,128)(2,1)S(1)} fusion(bf16[1024,16,64]{0,2,1:T(8,128)(2,1)S(1)} %bitcast.536, f32[16,512]{1,0:T(8,128)S(1)} %get-tuple-element.68, f32[16,512,1024]{2,1,0:T(8,128)} %fusion.12), kind=kOutput, calls=%fused_computation.239 | convolution fusion | flops 1099441152 | bytes 36732928 | tf_op jit(solution)/shard_map/shij,sjhd->sihd/dot_general | solution.py:185
  460.3 25.5 %fusion.150 = bf16[16,64,512]{2,1,0:T(8,128)(2,1)S(1)} fusion(bf16[1024,16,64]{0,2,1:T(8,128)(2,1)} %bitcast.540, f32[16,512]{1,0:T(8,128)S(1)} %get-tuple-element.72, f32[16,512,1024]{2,1,0:T(8,128)} %fusion.11), kind=kOutput, calls=%fused_computation.238 | convolution fusion | flops 1099441152 | bytes 36732928 | tf_op jit(solution)/shard_map/shij,sjhd->sihd/dot_general | solution.py:185
  490.7 35.3 %fusion.10 = f32[16,512,1024]{2,1,0:T(8,128)} fusion(f32[512,1024,16]{1,2,0:T(8,128)} %fusion.8, pred[1024]{0:T(1024)(128)(4,1)S(1)} %copy-done.76, bf16[512,16,64]{0,2,1:T(8,128)(2,1)S(1)} %bitcast.516, bf16[1024,16,64]{0,2,1:T(8,128)(2,1)S(1)} %bitcast.510), kind=kOutput, calls=%fused_computation.15 | convolution fusion | flops 1090519040 | bytes 70255616 | tf_op jit(solution)/shard_map/sihd,sjhd->shij/dot_general | solution.py:83
  526.1 37.2 %fusion.302 = (f32[16,512]{1,0:T(8,128)S(1)}, f32[16,512,1024]{2,1,0:T(8,128)}) fusion(f32[16,512,1024]{2,1,0:T(8,128)} %fusion.10), kind=kOutput, calls=%fused_computation.374 | output fusion | flops 16778240 | bytes 67141632 | tf_op jit(solution)/shard_map/sub | solution.py:88
  563.3 25.6 %fusion.147 = bf16[16,64,512]{2,1,0:T(8,128)(2,1)S(1)} fusion(bf16[1024,16,64]{0,2,1:T(8,128)(2,1)} %bitcast.538, f32[16,512]{1,0:T(8,128)S(1)} %get-tuple-element.76, f32[16,512,1024]{2,1,0:T(8,128)} %fusion.10), kind=kOutput, calls=%fused_computation.237 | convolution fusion | flops 1099441152 | bytes 36732928 | tf_op jit(solution)/shard_map/shij,sjhd->sihd/dot_general | solution.py:185
  593.8 34.5 %fusion.9 = f32[16,512,1024]{2,1,0:T(8,128)} fusion(f32[512,1024,16]{1,2,0:T(8,128)} %fusion.8, pred[1024]{0:T(1024)(128)(4,1)S(1)} %copy-done.75, bf16[512,16,64]{0,2,1:T(8,128)(2,1)S(1)} %bitcast.520, bf16[1024,16,64]{0,2,1:T(8,128)(2,1)S(1)} %bitcast.513), kind=kOutput, calls=%fused_computation.14 | convolution fusion | flops 1090519040 | bytes 70255616 | tf_op jit(solution)/shard_map/sihd,sjhd->shij/dot_general | solution.py:83
  628.2 36.8 %fusion.303 = (f32[16,512]{1,0:T(8,128)S(1)}, f32[16,512,1024]{2,1,0:T(8,128)}) fusion(f32[16,512,1024]{2,1,0:T(8,128)} %fusion.9), kind=kOutput, calls=%fused_computation.375 | output fusion | flops 16778240 | bytes 67141632 | tf_op jit(solution)/shard_map/sub | solution.py:88
  665.6 25.2 %fusion.144 = bf16[16,64,512]{2,1,0:T(8,128)(2,1)S(1)} fusion(bf16[1024,16,64]{0,2,1:T(8,128)(2,1)} %bitcast.546, f32[16,512]{1,0:T(8,128)S(1)} %get-tuple-element.80, f32[16,512,1024]{2,1,0:T(8,128)} %fusion.9), kind=kOutput, calls=%fused_computation.236 | convolution fusion | flops 1099441152 | bytes 36732928 | tf_op jit(solution)/shard_map/shij,sjhd->sihd/dot_general | solution.py:185
  707.1 14.7 fusion.37
  739.0 13.3 fusion.29
  772.5 13.1 fusion.25
  806.0 14.1 fusion.33
  820.1 16.6 multiply_reduce_fusion.5
  854.7 22.7 %multiply_reduce_fusion.3 = (f32[16,512]{1,0:T(8,128)S(1)}, f32[16,512,1024]{2,1,0:T(8,128)}) fusion(f32[16,512,1024]{2,1,0:T(8,128)} %get-tuple-element.81, f32[16,512]{1,0:T(8,128)S(1)} %copy-done.91, bf16[512,16,64]{0,2,1:T(8,128)(2,1)S(1)} %bitcast.556, bf16[1024,16,64]{0,2,1:T(8,128)(2,1)} %bitcast.547), kind=kOutput, calls=%fused_computation.25 | convolution fusion | flops 1098899456 | bytes 70320128 | tf_op jit(solution)/shard_map/sihd,sjhd->shij/dot_general | solution.py:266
  877.3 27.7 %multiply_convert_fusion.3 = bf16[16,512,1024]{2,1,0:T(8,128)(2,1)} fusion(f32[16,512,1024]{2,1,0:T(8,128)} %get-tuple-element.91, f32[16,512]{1,0:T(8,128)S(1)} %get-tuple-element.90, f32[16,512,1024]{2,1,0:T(8,128)} %get-tuple-element.81, f32[16,512]{1,0:T(8,128)S(1)} %copy-done.91), kind=kLoop, calls=%fused_computation.24 | loop fusion | flops 33554432 | bytes 83951616 | tf_op jit(solution)/shard_map/convert_element_type | solution.py:271
  919.0 22.6 %multiply_reduce_fusion.1 = (f32[16,512]{1,0:T(8,128)S(1)}, f32[16,512,1024]{2,1,0:T(8,128)}) fusion(f32[16,512,1024]{2,1,0:T(8,128)} %get-tuple-element.73, f32[16,512]{1,0:T(8,128)S(1)} %copy-done.85, bf16[512,16,64]{0,2,1:T(8,128)(2,1)S(1)} %bitcast.560, bf16[1024,16,64]{0,2,1:T(8,128)(2,1)} %bitcast.541), kind=kOutput, calls=%fused_computation.21 | convolution fusion | flops 1098899456 | bytes 70320128 | tf_op jit(solution)/shard_map/sihd,sjhd->shij/dot_general | solution.py:266
  941.6 27.6 %multiply_convert_fusion.1 = bf16[16,512,1024]{2,1,0:T(8,128)(2,1)} fusion(f32[16,512,1024]{2,1,0:T(8,128)} %get-tuple-element.93, f32[16,512]{1,0:T(8,128)S(1)} %get-tuple-element.92, f32[16,512,1024]{2,1,0:T(8,128)} %get-tuple-element.73, f32[16,512]{1,0:T(8,128)S(1)} %copy-done.85), kind=kLoop, calls=%fused_computation.20 | loop fusion | flops 33554432 | bytes 83951616 | tf_op jit(solution)/shard_map/convert_element_type | solution.py:271
  985.9 22.3 %multiply_reduce_fusion.2 = (f32[16,512]{1,0:T(8,128)S(1)}, f32[16,512,1024]{2,1,0:T(8,128)}) fusion(f32[16,512,1024]{2,1,0:T(8,128)} %get-tuple-element.77, f32[16,512]{1,0:T(8,128)S(1)} %copy-done.88, bf16[512,16,64]{0,2,1:T(8,128)(2,1)S(1)} %bitcast.554, bf16[1024,16,64]{0,2,1:T(8,128)(2,1)} %bitcast.539), kind=kOutput, calls=%fused_computation.23 | convolution fusion | flops 1098899456 | bytes 70320128 | tf_op jit(solution)/shard_map/sihd,sjhd->shij/dot_general | solution.py:266
  1008.3 28.6 %multiply_convert_fusion.2 = bf16[16,512,1024]{2,1,0:T(8,128)(2,1)} fusion(f32[16,512,1024]{2,1,0:T(8,128)} %get-tuple-element.89, f32[16,512]{1,0:T(8,128)S(1)} %get-tuple-element.88, f32[16,512,1024]{2,1,0:T(8,128)} %get-tuple-element.77, f32[16,512]{1,0:T(8,128)S(1)} %copy-done.88), kind=kLoop, calls=%fused_computation.22 | loop fusion | flops 33554432 | bytes 83951616 | tf_op jit(solution)/shard_map/convert_element_type | solution.py:271
  1047.2 23.4 %multiply_reduce_fusion = (f32[16,512]{1,0:T(8,128)S(1)}, f32[16,512,1024]{2,1,0:T(8,128)}) fusion(f32[16,512,1024]{2,1,0:T(8,128)} %get-tuple-element.69, f32[16,512]{1,0:T(8,128)S(1)} %copy-done.83, bf16[512,16,64]{0,2,1:T(8,128)(2,1)} %bitcast.558, bf16[1024,16,64]{0,2,1:T(8,128)(2,1)S(1)} %bitcast.537), kind=kOutput, calls=%fused_computation.19 | convolution fusion | flops 1098899456 | bytes 70320128 | tf_op jit(solution)/shard_map/sihd,sjhd->shij/dot_general | solution.py:266
  1070.6 27.6 %multiply_convert_fusion = bf16[16,512,1024]{2,1,0:T(8,128)(2,1)} fusion(f32[16,512,1024]{2,1,0:T(8,128)} %get-tuple-element.87, f32[16,512]{1,0:T(8,128)S(1)} %get-tuple-element.86, f32[16,512,1024]{2,1,0:T(8,128)} %get-tuple-element.69, f32[16,512]{1,0:T(8,128)S(1)} %copy-done.83), kind=kLoop, calls=%fused_computation.18 | loop fusion | flops 33554432 | bytes 83951616 | tf_op jit(solution)/shard_map/convert_element_type | solution.py:271
  1108.6 32.8 %fusion.138 = bf16[16,64,1024]{2,1,0:T(8,128)(2,1)} fusion(bf16[512,16,64]{0,2,1:T(8,128)(2,1)S(1)} %bitcast.561, f32[16,512]{1,0:T(8,128)S(1)} %copy-done.86, f32[16,512,1024]{2,1,0:T(8,128)} %fusion.11), kind=kOutput, calls=%fused_computation.234 | convolution fusion | flops 1099965440 | bytes 36732928 | tf_op jit(solution)/shard_map/shij,sihd->sjhd/dot_general | solution.py:283
  1141.4 32.5 %fusion.132 = bf16[16,64,1024]{2,1,0:T(8,128)(2,1)} fusion(bf16[512,16,64]{0,2,1:T(8,128)(2,1)S(1)} %bitcast.557, f32[16,512]{1,0:T(8,128)S(1)} %copy-done.92, f32[16,512,1024]{2,1,0:T(8,128)} %fusion.9), kind=kOutput, calls=%fused_computation.232 | convolution fusion | flops 1099965440 | bytes 36732928 | tf_op jit(solution)/shard_map/shij,sihd->sjhd/dot_general | solution.py:283
  1174.0 32.7 %fusion.135 = bf16[16,64,1024]{2,1,0:T(8,128)(2,1)} fusion(bf16[512,16,64]{0,2,1:T(8,128)(2,1)S(1)} %bitcast.555, f32[16,512]{1,0:T(8,128)S(1)} %copy-done.89, f32[16,512,1024]{2,1,0:T(8,128)} %fusion.10), kind=kOutput, calls=%fused_computation.233 | convolution fusion | flops 1099965440 | bytes 36732928 | tf_op jit(solution)/shard_map/shij,sihd->sjhd/dot_general | solution.py:283
  1206.8 33.1 %fusion.141 = bf16[16,64,1024]{2,1,0:T(8,128)(2,1)} fusion(bf16[512,16,64]{0,2,1:T(8,128)(2,1)S(1)} %bitcast.559, f32[16,512]{1,0:T(8,128)S(1)} %copy-done.83, f32[16,512,1024]{2,1,0:T(8,128)} %fusion.12), kind=kOutput, calls=%fused_computation.235 | convolution fusion | flops 1099965440 | bytes 36732928 | tf_op jit(solution)/shard_map/shij,sihd->sjhd/dot_general | solution.py:283
  1251.9 13.1 convolution_convert_fusion.6
  1386.6 13.4 fusion.266
  1400.1 22.8 %add_convert_fusion.1 = bf16[1024,4096]{1,0:T(8,128)(2,1)} fusion(f32[1024,4096]{1,0:T(8,128)} %fusion.268, f32[1024,4096]{1,0:T(8,128)} %fusion.264, f32[1024,4096]{1,0:T(8,128)} %fusion.266, bf16[512,4096]{1,0:T(8,128)(2,1)} %copy-done.50, f32[512,1024]{1,0:T(8,128)S(1)} %copy-done.19, f32[512]{0:T(512)S(1)} %copy-done.97, f32[1024]{0:T(1024)S(1)} %copy-done.81), kind=kOutput, calls=%fused_computation.41 | convolution fusion | flops 4313317376 | bytes 65017856 | tf_op jit(solution)/shard_map/rd,rf->df/dot_general | solution.py:237
  1424.6 15.6 fusion.237
  1440.3 15.4 fusion.225
  1455.6 21.5 %fusion.231 = f32[4096,1024]{1,0:T(8,128)} fusion(f32[512]{0:T(512)S(1)} %copy-done.122, bf16[4,512,1024]{2,1,0:T(8,128)(2,1)S(1)} %copy-done.49, f32[512,4096]{1,0:T(8,128)S(1)} %bitcast.565), kind=kOutput, calls=%fused_computation.315 | convolution fusion | flops 4315414528 | bytes 26216448 | tf_op jit(solution)/shard_map/rf,rd->fd/dot_general | solution.py:230
  1477.2 24.5 %add_convert_fusion = bf16[4096,1024]{1,0:T(8,128)(2,1)} fusion(f32[4096,1024]{1,0:T(8,128)} %fusion.237, f32[4096,1024]{1,0:T(8,128)} %fusion.225, f32[4096,1024]{1,0:T(8,128)} %fusion.231, f32[512]{0:T(512)S(1)} %copy-done.135, bf16[4,512,1024]{2,1,0:T(8,128)(2,1)} %param.14, f32[512,4096]{1,0:T(8,128)} %fusion.270), kind=kOutput, calls=%fused_computation.40 | convolution fusion | flops 4332191744 | bytes 68159488 | tf_op jit(solution)/shard_map/rf,rd->fd/dot_general | solution.py:230
  1558.5 15.2 fusion.160
  1573.7 18.0 fusion.178
  1591.8 16.2 fusion.175
  1608.0 17.3 fusion.181
  1645.4 72.8 %all-reduce.5 = (bf16[1024]{0:T(1024)(128)(2,1)S(1)}, bf16[1024]{0:T(1024)(128)(2,1)S(1)}, bf16[32,16]{1,0:T(8,128)(2,1)S(1)}) all-reduce(bf16[1024]{0:T(1024)(128)(2,1)S(1)} %get-tuple-element.100, bf16[1024]{0:T(1024)(128)(2,1)S(1)} %get-tuple-element.99, ...), channel_id=18, replica_groups=mesh['ctx'=2,'fsdp'=16] {'fsdp'}, use_global_device_ids=true, to_apply=%region_41.42.clone | all-reduce | flops 2560 | bytes 10240
  1718.6 89.6 %reduce-scatter.39.cloned.1.call-done = bf16[64,4096]{1,0:T(8,128)(2,1)} async-done(((bf16[1024,4096]{1,0:T(8,128)(2,1)}), bf16[64,4096]{1,0:T(8,128)(2,1)}) %reduce-scatter.39.cloned.1.call-update) | async-done | bytes 524304 | tf_op jit(solution)/shard_map/reduce_scatter | solution.py:338
  1808.2 182.4 %reduce-scatter.41.cloned.1.call-done = bf16[256,1024]{1,0:T(8,128)(2,1)} async-done(((bf16[4096,1024]{1,0:T(8,128)(2,1)}), bf16[256,1024]{1,0:T(8,128)(2,1)}) %reduce-scatter.41.cloned.1.call-update) | async-done | bytes 524304 | tf_op jit(solution)/shard_map/reduce_scatter | solution.py:341
  (552 shorter events, 508.9 us)
Async XLA Ops:
  7.2 67.2 %all-gather.28.cloned.1.call-start = ((), (), s32[]{:S(2)}) async-start(), calls=%async_computation.16 | async-start | bytes 2228224 | tf_op jit(solution)/shard_map/all_gather | solution.py:63
  7.9 128.6 %all-gather.24.cloned.1.call-start = ((), (), s32[]{:S(2)}) async-start(), calls=%async_computation.14 | async-start | bytes 2228224 | tf_op jit(solution)/shard_map/all_gather | solution.py:64
  8.7 223.0 %all-gather.26.cloned.1.call-start = ((), (), s32[]{:S(2)}) async-start(), calls=%async_computation.15 | async-start | bytes 2228224 | tf_op jit(solution)/shard_map/all_gather | solution.py:62
  9.4 240.5 %all-gather.50.cloned.1.call-start = ((), (), s32[]{:S(2)}) async-start(), calls=%async_computation.41 | async-start | bytes 3145728 | tf_op jit(solution)/shard_map/all_gather | solution.py:174
  56.8 188.4 %copy-start.77 = (f32[1024]{0:T(1024)}, f32[1024]{0:T(1024)S(1)}, u32[]{:S(2)}) copy-start(f32[1024]{0:T(1024)S(1)} %convert_element_type.658) | copy-start | bytes 12292
  59.9 84.7 %copy-start.106 = (f32[512]{0:T(512)}, f32[512]{0:T(512)S(1)}, u32[]{:S(2)}) copy-start(f32[512]{0:T(512)S(1)} %get-tuple-element.34) | copy-start | bytes 6148
  59.9 92.6 %copy-start.104 = (f32[512]{0:T(512)}, f32[512]{0:T(512)S(1)}, u32[]{:S(2)}) copy-start(f32[512]{0:T(512)S(1)} %get-tuple-element.33) | copy-start | bytes 6148
  59.9 171.8 %copy-start.93 = (f32[512]{0:T(512)}, f32[512]{0:T(512)S(1)}, u32[]{:S(2)}) copy-start(f32[512]{0:T(512)S(1)} %fusion.262) | copy-start | bytes 6148
  78.7 246.3 %all-gather.46.cloned.1.call-start = ((), (), s32[]{:S(2)}) async-start(), calls=%async_computation.39 | async-start | bytes 3145728 | tf_op jit(solution)/shard_map/all_gather | solution.py:174
  78.8 156.9 %copy-start.112 = (f32[512]{0:T(512)}, f32[512]{0:T(512)S(1)}, u32[]{:S(2)}) copy-start(f32[512]{0:T(512)S(1)} %fusion.260) | copy-start | bytes 6148
  82.4 317.5 %all-gather.48.cloned.1.call-start = ((), (), s32[]{:S(2)}) async-start(), calls=%async_computation.40 | async-start | bytes 3145728 | tf_op jit(solution)/shard_map/all_gather | solution.py:175
  140.9 294.2 %all-gather.44.cloned.1.call-start = ((), (), s32[]{:S(2)}) async-start(), calls=%async_computation.38 | async-start | bytes 3145728 | tf_op jit(solution)/shard_map/all_gather | solution.py:175
  144.5 295.0 %all-gather.40.cloned.1.call-start = ((), (), s32[]{:S(2)}) async-start(), calls=%async_computation.36 | async-start | bytes 3145728 | tf_op jit(solution)/shard_map/all_gather | solution.py:175
  144.6 96.1 %copy-start.115 = (f32[512]{0:T(512)}, f32[512]{0:T(512)S(1)}, u32[]{:S(2)}) copy-start(f32[512]{0:T(512)S(1)} %fusion.258) | copy-start | bytes 6148
  148.1 295.3 %all-gather.42.cloned.1.call-start = ((), (), s32[]{:S(2)}) async-start(), calls=%async_computation.37 | async-start | bytes 3145728 | tf_op jit(solution)/shard_map/all_gather | solution.py:174
  152.4 294.9 %all-gather.36.cloned.1.call-start = ((), (), s32[]{:S(2)}) async-start(), calls=%async_computation.34 | async-start | bytes 3145728 | tf_op jit(solution)/shard_map/all_gather | solution.py:175
  152.5 92.7 %copy-start.118 = (f32[512]{0:T(512)}, f32[512]{0:T(512)S(1)}, u32[]{:S(2)}) copy-start(f32[512]{0:T(512)S(1)} %fusion.256) | copy-start | bytes 6148
  156.0 295.3 %all-gather.38.cloned.1.call-start = ((), (), s32[]{:S(2)}) async-start(), calls=%async_computation.35 | async-start | bytes 3145728 | tf_op jit(solution)/shard_map/all_gather | solution.py:174
  160.3 50.1 %copy-start.140 = (s32[15]{0:T(128)S(1)}, s32[15]{0:T(128)}, u32[]{:S(2)}) copy-start(s32[15]{0:T(128)} %constant.52.clone) | copy-start | bytes 184
  160.4 294.9 %all-gather.30.cloned.1.call-start = ((), (), s32[]{:S(2)}) async-start(), calls=%async_computation.17 | async-start | bytes 2228224 | tf_op jit(solution)/shard_map/all_gather | solution.py:65
  160.9 534.1 %all-gather.32.cloned.1.call-start = ((), (), s32[]{:S(2)}) async-start(), calls=%async_computation.18 | async-start | bytes 8912896 | tf_op jit(solution)/shard_map/all_gather | solution.py:67
  161.7 545.4 %all-gather.34.cloned.1.call-start = ((), (), s32[]{:S(2)}) async-start(), calls=%async_computation.19 | async-start | bytes 8912896 | tf_op jit(solution)/shard_map/all_gather | solution.py:68
  162.3 1158.0 %reduce-scatter.23.cloned.1.call-start = ((), (), s32[]{:S(2)}) async-start(), calls=%async_computation.24 | async-start | bytes 3145728 | tf_op jit(solution)/shard_map/reduce_scatter | solution.py:287
  252.8 35.3 %copy-start.2 = (bf16[1024,1024]{0,1:T(8,128)(2,1)}, bf16[1024,1024]{0,1:T(8,128)(2,1)S(1)}, u32[]{:S(2)}) copy-start(bf16[1024,1024]{0,1:T(8,128)(2,1)S(1)} %copy.119) | copy-start | bytes 6291460
  325.0 77.8 %copy-start.82 = (f32[16,512]{1,0:T(8,128)}, f32[16,512]{1,0:T(8,128)S(1)}, u32[]{:S(2)}) copy-start(f32[16,512]{1,0:T(8,128)S(1)} %get-tuple-element.68) | copy-start | bytes 98308
  399.9 60.4 %copy-start.84 = (f32[16,512]{1,0:T(8,128)}, f32[16,512]{1,0:T(8,128)S(1)}, u32[]{:S(2)}) copy-start(f32[16,512]{1,0:T(8,128)S(1)} %get-tuple-element.72) | copy-start | bytes 98308
  485.8 40.3 %copy-start.42 = (bf16[16,64,512]{2,1,0:T(8,128)(2,1)}, bf16[16,64,512]{2,1,0:T(8,128)(2,1)S(1)}, u32[]{:S(2)}) copy-start(bf16[16,64,512]{2,1,0:T(8,128)(2,1)S(1)} %fusion.150) | copy-start | bytes 3145732
  589.0 39.3 %copy-start.44 = (bf16[16,64,512]{2,1,0:T(8,128)(2,1)}, bf16[16,64,512]{2,1,0:T(8,128)(2,1)S(1)}, u32[]{:S(2)}) copy-start(bf16[16,64,512]{2,1,0:T(8,128)(2,1)S(1)} %fusion.147) | copy-start | bytes 3145732
  593.2 243.5 %copy-start.127 = (f32[512]{0:T(512)}, f32[512]{0:T(512)S(1)}, u32[]{:S(2)}) copy-start(f32[512]{0:T(512)S(1)} %fusion.259) | copy-start | bytes 6148
  695.0 141.7 %copy-start.131 = (f32[512]{0:T(512)}, f32[512]{0:T(512)S(1)}, u32[]{:S(2)}) copy-start(f32[512]{0:T(512)S(1)} %fusion.257) | copy-start | bytes 6148
  979.4 345.9 %reduce-scatter.15.cloned.1.call-start = ((), (), s32[]{:S(2)}) async-start(), calls=%async_computation.20 | async-start | bytes 3145728 | tf_op jit(solution)/shard_map/reduce_scatter | solution.py:287
  1008.2 322.1 %reduce-scatter.19.cloned.1.call-start = ((), (), s32[]{:S(2)}) async-start(), calls=%async_computation.22 | async-start | bytes 3145728 | tf_op jit(solution)/shard_map/reduce_scatter | solution.py:287
  1047.1 288.4 %reduce-scatter.27.cloned.1.call-start = ((), (), s32[]{:S(2)}) async-start(), calls=%async_computation.26 | async-start | bytes 3145728 | tf_op jit(solution)/shard_map/reduce_scatter | solution.py:287
  1108.5 254.6 %reduce-scatter.25.cloned.1.call-start = ((), (), s32[]{:S(2)}) async-start(), calls=%async_computation.25 | async-start | bytes 3145728 | tf_op jit(solution)/shard_map/reduce_scatter | solution.py:290
  1141.4 226.8 %reduce-scatter.17.cloned.1.call-start = ((), (), s32[]{:S(2)}) async-start(), calls=%async_computation.21 | async-start | bytes 3145728 | tf_op jit(solution)/shard_map/reduce_scatter | solution.py:290
  1173.9 199.2 %reduce-scatter.21.cloned.1.call-start = ((), (), s32[]{:S(2)}) async-start(), calls=%async_computation.23 | async-start | bytes 3145728 | tf_op jit(solution)/shard_map/reduce_scatter | solution.py:290
  1206.7 171.4 %reduce-scatter.29.cloned.1.call-start = ((), (), s32[]{:S(2)}) async-start(), calls=%async_computation.27 | async-start | bytes 3145728 | tf_op jit(solution)/shard_map/reduce_scatter | solution.py:290
  1251.7 466.8 %reduce-scatter.31.cloned.1.call-start = ((), (), s32[]{:S(2)}) async-start(), calls=%async_computation.28 | async-start | bytes 2228224 | tf_op jit(solution)/shard_map/reduce_scatter | solution.py:323
  1311.8 406.7 %reduce-scatter.37.cloned.1.call-start = ((), (), s32[]{:S(2)}) async-start(), calls=%async_computation.31 | async-start | bytes 2228224 | tf_op jit(solution)/shard_map/reduce_scatter | solution.py:332
  1320.1 398.4 %reduce-scatter.33.cloned.1.call-start = ((), (), s32[]{:S(2)}) async-start(), calls=%async_computation.29 | async-start | bytes 2228224 | tf_op jit(solution)/shard_map/reduce_scatter | solution.py:326
  1343.8 374.8 %reduce-scatter.35.cloned.1.call-start = ((), (), s32[]{:S(2)}) async-start(), calls=%async_computation.30 | async-start | bytes 2228224 | tf_op jit(solution)/shard_map/reduce_scatter | solution.py:329
  1386.3 421.9 %reduce-scatter.39.cloned.1.call-start = ((), (), s32[]{:S(2)}) async-start(), calls=%async_computation.32 | async-start | bytes 8912896 | tf_op jit(solution)/shard_map/reduce_scatter | solution.py:338
  1422.9 567.7 %reduce-scatter.41.cloned.1.call-start = ((), (), s32[]{:S(2)}) async-start(), calls=%async_computation.33 | async-start | bytes 8912896 | tf_op jit(solution)/shard_map/reduce_scatter | solution.py:341
  1501.6 514.9 %all-reduce.11.cloned.1.call-start = ((), (), s32[]{:S(2)}) async-start(), calls=%async_computation.42 | async-start | bytes 3145728 | tf_op jit(solution)/shard_map/psum | solution.py:350
  1638.4 80.0 %copy-start.109 = (f32[512]{0:T(512)S(1)}, f32[512]{0:T(512)}, u32[]{:S(2)}) copy-start(f32[512]{0:T(512)} %copy-done.108) | copy-start | bytes 6148
  1638.4 80.0 %copy-start.111 = (f32[512]{0:T(512)S(1)}, f32[512]{0:T(512)}, u32[]{:S(2)}) copy-start(f32[512]{0:T(512)} %copy-done.110) | copy-start | bytes 6148
  1638.5 80.0 %copy-start.105 = (f32[512]{0:T(512)S(1)}, f32[512]{0:T(512)}, u32[]{:S(2)}) copy-start(f32[512]{0:T(512)} %copy-done.104) | copy-start | bytes 6148
  1638.5 80.0 %copy-start.107 = (f32[512]{0:T(512)S(1)}, f32[512]{0:T(512)}, u32[]{:S(2)}) copy-start(f32[512]{0:T(512)} %copy-done.106) | copy-start | bytes 6148
  (145 other events, 1573.9 us)
Sparse Core Ops, SparseCore 0:
  10.8 63.5 all-gather.27
  77.2 59.3 all-gather.23
  139.3 59.5 all-gather.25
  200.9 9.0 all-gather.49
  212.0 11.7 all-gather.45
  225.7 11.7 all-gather.47
  239.6 11.7 all-gather.43
  253.0 11.7 all-gather.39
  266.3 11.7 all-gather.41
  279.5 11.7 all-gather.35
  292.8 11.7 all-gather.37
  307.2 61.8 all-gather.29
  371.9 111.6 all-gather.31
  486.3 110.9 all-gather.33
  979.5 5.4 reduce-scatter.22
  1008.3 6.0 reduce-scatter.14
  1047.3 6.0 reduce-scatter.18
  1108.6 5.4 reduce-scatter.26
  1141.5 5.4 reduce-scatter.24
  1174.1 5.4 reduce-scatter.16
  1206.8 5.4 reduce-scatter.20
  1251.8 5.4 reduce-scatter.28
  1311.9 76.2 reduce-scatter.30
  1390.4 77.7 reduce-scatter.36
  1470.5 77.5 reduce-scatter.32
  1550.2 77.7 reduce-scatter.34
  1630.1 178.0 reduce-scatter.38
  1810.5 180.0 reduce-scatter.40
  1993.4 23.1 all-reduce.10
where the time goes:
time: 2040 us; the launch traced here: 2030 us
  matrix products  1140 us (56%)
  waiting for transfers between devices  355 us (17%)
  other arithmetic  312 us (15%)
  blocking collectives  158 us (8%)
  local copies, waits for them, and re-layouts  53.2 us (3%)
    reduce_scatter x1, waiting for transfers between devices, per_device(): lax.psum_scatter(totals[7].astype(jnp.bfloat16), 'fsdp', scatter_dimensio...  182 us
    sub x4, other arithmetic, attend_stats(): exp_scores = jnp.exp(scores - row_max)  148 us
    dot_general x4, matrix products, attend_stats(): jnp.einsum('sihd,sjhd->shij', query_four, key_four, preferred_element_typ...  140 us
    dot_general x4, matrix products, per_device(): jnp.einsum('shij,sihd->sjhd', probs_low, grad_mixed_four, preferred_eleme...  131 us
    unnamed x2, blocking collectives  117 us
    convert_element_type x4, other arithmetic, per_device(): scores_low = grad_scores.astype(jnp.bfloat16)  112 us
    dot_general x4, matrix products, per_device(): jnp.einsum('shij,sjhd->sihd', probs_low, value_four, preferred_element_ty...  109 us
    dot_general x4, matrix products, per_device(): jnp.einsum('sihd,sjhd->shij', grad_mixed_four, value_four, preferred_elem...  90.9 us
  transfers between devices with their start and end apart: 29, of which 5 were waited for; matrix products, arithmetic and copies ran while one was open for 59% of the time, Pallas kernels for 0%

commit v1 on v0

v1 whole, which is shorter than its diff:
```python
import functools

import jax
import jax.numpy as jnp
import numpy as np
from jax import lax
from jax.experimental import pallas as pl
from jax.experimental.pallas import tpu as pltpu
from jax.sharding import PartitionSpec as P

LOG2E = 1.4426950408889634
LN2 = 0.6931471805599453
NEG = -1e30
TILE = 256
QT = 512
HEAD_DIM = 64
EPS = 1e-6
GELU = 0.7978845608028654
CUBIC = 0.044715


def dot(a, b, ca, cb, precision=None):
    return lax.dot_general(a, b, (((ca,), (cb,)), ((), ())), precision=precision,
                           preferred_element_type=jnp.float32)

def attend_kernel(len_ref, tvec_ref, q_ref, k_ref, v_ref, o_ref, lse_ref, strip_ref, *, seq_len, head_dim):
    heads = q_ref.shape[-1] // head_dim
    blocks = seq_len // TILE
    far = seq_len - QT

    @pl.when(pl.program_id(1) == 0)
    def _():
        for h in range(heads):
            wide = jnp.broadcast_to(tvec_ref[0, h : h + 1, :], (QT, tvec_ref.shape[-1]))
            strip_ref[h] = pltpu.roll(wide, 0, 1, stride=1, stride_axis=0)

    live = len_ref[pl.program_id(1)]
    lane = lax.broadcasted_iota(jnp.int32, (1, q_ref.shape[-1]), 1) // head_dim
    column = lax.broadcasted_iota(jnp.int32, (1, TILE), 1)

    def with_blocks(used):
        top = TILE * used
        kept = [lane == h for h in range(heads)]
        keys = [jnp.where(kept[h], k_ref[0, 0:top, :], 0) for h in range(heads)]
        values = [jnp.where(kept[h], v_ref[0, 0:top, :], 1) for h in range(heads)]

        def query_tile(a, carry):
            here = pl.ds(pl.multiple_of(a * QT, QT), QT)
            q = q_ref[0, here, :]
            total = None
            for h in range(heads):
                at = pl.ds(pl.multiple_of(far - QT * a, TILE), top)
                scores = dot(q, keys[h], 1, 1) + strip_ref[h, :, at]
                last = jnp.where(column + (top - TILE) < live, scores[:, top - TILE :], NEG)
                scores = jnp.concatenate([scores[:, : top - TILE], last], axis=1) if used > 1 else last
                peak = jnp.max(scores, axis=1, keepdims=True)
                probs = jnp.exp2(scores - peak).astype(jnp.bfloat16)
                out = dot(probs, values[h], 1, 0)
                mass = pltpu.roll(out, head_dim, 1)
                out = out * (1.0 / mass)
                total = out if total is None else jnp.where(kept[h], out, total)
                lse = peak + jnp.log2(mass)
                lse_ref[0, 0, h : h + 1, here] = jnp.transpose(lse)[h * head_dim : h * head_dim + 1, :]
            o_ref[0, here, :] = total.astype(jnp.bfloat16)
            return carry

        lax.fori_loop(0, seq_len // QT, query_tile, 0, unroll=True)

    for used in range(1, blocks + 1):
        pl.when((live + TILE - 1) // TILE == used)(functools.partial(with_blocks, used))


def attend(lengths, tvec, q, k, v, head_dim):
    seqs, seq_len, width = q.shape
    pairs = width // 128
    heads = 128 // head_dim
    strip = tvec.shape[-1]
    block = pl.BlockSpec((1, seq_len, 128), lambda p, s, n: (s, 0, p))
    return pl.pallas_call(
        functools.partial(attend_kernel, seq_len=seq_len, head_dim=head_dim),
        grid_spec=pltpu.PrefetchScalarGridSpec(
            num_scalar_prefetch=1, grid=(pairs, seqs),
            in_specs=[pl.BlockSpec((1, heads, strip), lambda p, s, n: (p, 0, 0)), block, block, block],
            out_specs=[block, pl.BlockSpec((1, 1, heads, seq_len), lambda p, s, n: (p, s, 0, 0))],
            scratch_shapes=[pltpu.VMEM((heads, QT, strip), jnp.float32)]),
        out_shape=[jax.ShapeDtypeStruct(q.shape, jnp.bfloat16), jax.ShapeDtypeStruct((pairs, seqs, heads, seq_len), jnp.float32)],
        compiler_params=pltpu.CompilerParams(vmem_limit_bytes=48 << 20),
        cost_estimate=pl.CostEstimate(flops=4 * seqs * width * seq_len * seq_len, bytes_accessed=8 * seqs * seq_len * width, transcendentals=0),
        name="attend",
    )(lengths, tvec, q, k, v)


def unattend_kernel(len_ref, tvec_ref, q_ref, k_ref, v_ref, o_ref, do_ref, lse_ref, dq_ref, dk_ref, dv_ref, dt_ref,
                    strip_ref, sums_ref, dk_acc, dv_acc, *, seq_len, head_dim):
    heads = q_ref.shape[-1] // head_dim
    blocks = seq_len // TILE
    far = seq_len - TILE
    bands = (2 * blocks - 1) * TILE

    @pl.when(pl.program_id(1) == 0)
    def _():
        for h in range(heads):
            wide = jnp.broadcast_to(tvec_ref[0, h : h + 1, :], (TILE, tvec_ref.shape[-1]))
            wide = pltpu.roll(wide, 0, 1, stride=1, stride_axis=0)
            for b in range(2 * blocks - 1):
                strip_ref[TILE * b : TILE * (b + 1), TILE * h : TILE * (h + 1)] = jnp.transpose(wide[:, TILE * b : TILE * (b + 1)])
        sums_ref[...] = jnp.zeros_like(sums_ref)

    live = len_ref[pl.program_id(1)]
    lane = lax.broadcasted_iota(jnp.int32, (1, q_ref.shape[-1]), 1) // head_dim
    row = lax.broadcasted_iota(jnp.int32, (TILE, 1), 0)
    kept = [lane == h for h in range(heads)]

    def with_blocks(used):
        top = TILE * used
        dk_acc[0:top, :] = jnp.zeros((top, dk_acc.shape[1]), jnp.float32)
        dv_acc[0:top, :] = jnp.zeros((top, dv_acc.shape[1]), jnp.float32)

        def query_tile(a, carry):
            here = pl.ds(pl.multiple_of(a * TILE, TILE), TILE)
            q = q_ref[0, here, :]
            do = do_ref[0, here, :]
            product = jnp.transpose(do.astype(jnp.float32) * o_ref[0, here, :].astype(jnp.float32))
            qs = jnp.concatenate([jnp.where(kept[h], q, 0) for h in range(heads)], axis=0)
            dos = jnp.concatenate([jnp.where(kept[h], do, 0) for h in range(heads)], axis=0)
            delta = jnp.concatenate([jnp.sum(product[h * head_dim : (h + 1) * head_dim], axis=0, keepdims=True) for h in range(heads)], axis=1)
            lse = jnp.concatenate([lse_ref[0, 0, h : h + 1, here] for h in range(heads)], axis=1)
            at = pl.ds(pl.multiple_of(far - TILE * a, TILE), top)
            kb = k_ref[0, 0:top, :]
            vb = v_ref[0, 0:top, :]
            p = jnp.exp2(dot(kb, qs, 1, 1) + strip_ref[at, :] - lse)
            last = jnp.where(row + (top - TILE) < live, p[top - TILE :], 0.0)
            p = jnp.concatenate([p[: top - TILE], last], axis=0) if used > 1 else last
            ds = p * (dot(vb, dos, 1, 1) - delta)
            sums_ref[at, :] += ds
            p = p.astype(jnp.bfloat16)
            ds = ds.astype(jnp.bfloat16)
            dv_acc[0:top, :] += dot(p, dos, 1, 0)
            dk_acc[0:top, :] += dot(ds, qs, 1, 0)
            dq = dot(ds, kb, 0, 0)
            dq_total = dq[0:TILE]
            for h in range(1, heads):
                dq_total = jnp.where(kept[h], dq[TILE * h : TILE * (h + 1)], dq_total)
            dq_ref[0, here, :] = (dq_total * LN2).astype(jnp.bfloat16)
            return carry

        lax.fori_loop(0, used, query_tile, 0)
        dk_ref[0, 0:top, :] = dk_acc[0:top, :].astype(jnp.bfloat16)
        dv_ref[0, 0:top, :] = dv_acc[0:top, :].astype(jnp.bfloat16)
        if used < blocks:
            zeros = jnp.zeros((seq_len - top, q_ref.shape[-1]), jnp.bfloat16)
            dq_ref[0, top:, :] = zeros
            dk_ref[0, top:, :] = zeros
            dv_ref[0, top:, :] = zeros

    for used in range(1, blocks + 1):
        pl.when((live + TILE - 1) // TILE == used)(functools.partial(with_blocks, used))

    @pl.when(pl.program_id(1) == pl.num_programs(1) - 1)
    def _():
        wide = dt_ref.shape[-1]
        for h in range(heads):
            turned = jnp.concatenate([jnp.transpose(sums_ref[TILE * b : TILE * (b + 1), TILE * h : TILE * (h + 1)]) for b in range(2 * blocks - 1)]
                                     + [jnp.zeros((TILE, wide - bands), jnp.float32)], axis=1)
            group = turned[0:8]
            for g in range(1, TILE // 8):
                group = group + pltpu.roll(turned[8 * g : 8 * (g + 1)], wide - 8 * g, 1)
            diagonal = group[0:1]
            for s in range(1, 8):
                diagonal = diagonal + pltpu.roll(group[s : s + 1], wide - s, 1)
            dt_ref[0, h : h + 1, :] = diagonal


def unattend(lengths, tvec, q, k, v, o, do, lse, head_dim):
    seqs, seq_len, width = q.shape
    pairs = width // 128
    heads = 128 // head_dim
    strip = tvec.shape[-1]
    bands = 2 * seq_len - TILE
    block = pl.BlockSpec((1, seq_len, 128), lambda p, s, n: (s, 0, p))
    vec = pl.BlockSpec((1, heads, strip), lambda p, s, n: (p, 0, 0))
    return pl.pallas_call(
        functools.partial(unattend_kernel, seq_len=seq_len, head_dim=head_dim),
        grid_spec=pltpu.PrefetchScalarGridSpec(
            num_scalar_prefetch=1, grid=(pairs, seqs),
            in_specs=[vec, block, block, block, block, block, pl.BlockSpec((1, 1, heads, seq_len), lambda p, s, n: (p, s, 0, 0))],
            out_specs=[block, block, block, vec],
            scratch_shapes=[pltpu.VMEM((bands, heads * TILE), jnp.float32), pltpu.VMEM((bands, heads * TILE), jnp.float32),
                            pltpu.VMEM((seq_len, 128), jnp.float32), pltpu.VMEM((seq_len, 128), jnp.float32)]),
        out_shape=[jax.ShapeDtypeStruct(q.shape, jnp.bfloat16)] * 3 + [jax.ShapeDtypeStruct((pairs, heads, strip), jnp.float32)],
        compiler_params=pltpu.CompilerParams(vmem_limit_bytes=56 << 20),
        cost_estimate=pl.CostEstimate(flops=10 * seqs * width * seq_len * seq_len, bytes_accessed=16 * seqs * seq_len * width, transcendentals=0),
        name="unattend",
    )(lengths, tvec, q, k, v, o, do, lse)


def bucket_edges():
    distance = np.arange(1, 512)
    scaled = 8 + np.floor(np.log(distance / 8.0) / np.log(16.0) * 8.0)
    level = np.where(distance < 8, distance, np.minimum(15, scaled))
    return np.array([distance[level >= target][0] for target in range(1, 16)], np.int32)

def levels_of(offset):
    level = jnp.sum((jnp.abs(offset)[:, None] >= jnp.asarray(bucket_edges())).astype(jnp.int32), axis=1)
    return level + 16 * (offset > 0).astype(jnp.int32)

def bias_vectors(table, seq_len, tile=TILE):
    x = jnp.arange(2 * seq_len, dtype=jnp.int32)
    far = seq_len - tile
    offset = jnp.where(x < 2 * seq_len - tile, x - far, x - far - 2 * seq_len)
    onehot = (levels_of(offset)[:, None] == jnp.arange(table.shape[0])).astype(jnp.float32)
    return jnp.einsum("xb,bh->hx", onehot, table.astype(jnp.float32) * LOG2E, precision=lax.Precision.HIGHEST)

def table_sums(diag, buckets, seq_len):
    x = jnp.arange(2 * seq_len, dtype=jnp.int32)
    far = seq_len - TILE
    offset = jnp.where(x < 2 * seq_len - TILE, x - far, x - far - 2 * seq_len)
    onehot = ((levels_of(offset)[:, None] == jnp.arange(buckets)) & (jnp.abs(offset) < seq_len)[:, None]).astype(jnp.float32)
    return jnp.einsum("zb,hz->bh", onehot, diag, precision=lax.Precision.HIGHEST)


def inverse_root(v):
    return lax.rsqrt(jnp.mean(v * v, axis=-1, keepdims=True) + EPS)


def norm_back(v, c, gain, e):
    scaled = e * v * c
    down = c * gain * e - v * (c * c) * jnp.mean(gain * scaled, axis=-1, keepdims=True)
    return down, jnp.sum(scaled, axis=0)


def gelu_pair(u):
    square = u * u
    t = jnp.tanh(GELU * u * (1.0 + CUBIC * square))
    value = 0.5 * u * (1.0 + t)
    slope = 0.5 * (1.0 + t) + 0.5 * u * (1.0 - t * t) * (GELU * (1.0 + 3.0 * CUBIC * square))
    return value, slope


def matmul(a, b, ca=1, cb=0):
    return dot(a, b, ca, cb)


def gather_rows(shard):
    n = lax.axis_size("ctx")
    part = shard.shape[0] // n
    mine = lax.dynamic_slice_in_dim(shard, lax.axis_index("ctx") * part, part, 0)
    return lax.all_gather(mine, ("fsdp", "ctx"), axis=0, tiled=True)


def swap(x):
    return lax.ppermute(x, "ctx", [(0, 1), (1, 0)])


def scatter_rows(grad):
    part = lax.psum_scatter(grad, ("fsdp", "ctx"), scatter_dimension=0, tiled=True)
    if lax.axis_size("ctx") != 2:
        return lax.all_gather(part, "ctx", axis=0, tiled=True).astype(jnp.float32)
    other = swap(part)
    first = lax.axis_index("ctx") == 0
    return jnp.concatenate([jnp.where(first, part, other), jnp.where(first, other, part)], axis=0).astype(jnp.float32)


def to_heads(x):
    if lax.axis_size("ctx") != 2:
        return lax.all_to_all(x, "ctx", split_axis=2, concat_axis=1, tiled=True)
    c = lax.axis_index("ctx")
    width = x.shape[2] // 2
    kept = lax.dynamic_slice_in_dim(x, c * width, width, 2)
    came = swap(lax.dynamic_slice_in_dim(x, (1 - c) * width, width, 2))
    return jnp.concatenate([jnp.where(c == 0, kept, came), jnp.where(c == 0, came, kept)], axis=1)


def to_positions(x):
    if lax.axis_size("ctx") != 2:
        return lax.all_to_all(x, "ctx", split_axis=1, concat_axis=2, tiled=True)
    c = lax.axis_index("ctx")
    width = x.shape[1] // 2
    kept = lax.dynamic_slice_in_dim(x, c * width, width, 1)
    came = swap(lax.dynamic_slice_in_dim(x, (1 - c) * width, width, 1))
    return jnp.concatenate([jnp.where(c == 0, kept, came), jnp.where(c == 0, came, kept)], axis=2)


def per_device(tokens, cotangent, lengths, norm_gain, query_weight, key_weight, value_weight, output_weight,
               ffn_gain, inner_weight, outer_weight, bias_table):
    seqs, block, width = tokens.shape
    rows = seqs * block
    n_ctx = lax.axis_size("ctx")
    n_fsdp = lax.axis_size("fsdp")
    c = lax.axis_index("ctx")
    seq_len = block * n_ctx
    heads = bias_table.shape[1]
    buckets = bias_table.shape[0] * n_fsdp
    shard = query_weight.shape[0]
    own_heads = heads // n_ctx
    pairs = own_heads * HEAD_DIM // 128
    per_pair = 128 // HEAD_DIM
    small = bias_table.size
    low = jnp.bfloat16

    side = jnp.concatenate([norm_gain[:, None], ffn_gain[:, None], jnp.broadcast_to(bias_table.reshape(1, small), (shard, small)),
                            jnp.zeros((shard, 126 - small), low)], axis=1)
    first = gather_rows(jnp.concatenate([query_weight, key_weight, value_weight, side], axis=1))
    w_qkv = first[:, : 3 * width]
    gain_one = first[:, 3 * width].astype(jnp.float32)[None, :]
    gain_two = first[:, 3 * width + 1].astype(jnp.float32)[None, :]
    table = first[::shard, 3 * width + 2 : 3 * width + 2 + small].reshape(buckets, heads)
    second = gather_rows(jnp.concatenate([output_weight, inner_weight], axis=1))
    w_output = second[:, :width]
    w_inner = second[:, width:]
    w_outer = gather_rows(outer_weight)

    own_table = lax.dynamic_slice_in_dim(table, c * own_heads, own_heads, 1)
    vector_q = bias_vectors(own_table, seq_len, QT).reshape(pairs, per_pair, 2 * seq_len)
    vector_k = bias_vectors(own_table, seq_len, TILE).reshape(pairs, per_pair, 2 * seq_len)

    x = tokens.astype(jnp.float32).reshape(rows, width)
    root_one = inverse_root(x)
    normed = (x * root_one * gain_one).astype(low)
    scale = jnp.concatenate([jnp.ones((1, width)), jnp.full((1, width), LOG2E), jnp.ones((1, width))], axis=1)
    qkv = (matmul(normed, w_qkv) * scale).astype(low).reshape(seqs, block, 3 * width)
    q, k, v = (to_heads(qkv[:, :, i * width : (i + 1) * width]) for i in range(3))
    out, lse = attend(lengths, vector_q, q, k, v, HEAD_DIM)
    mixed = to_positions(out).reshape(rows, width)
    residual = x + matmul(mixed, w_output)
    root_two = inverse_root(residual)
    normed_ffn = (residual * root_two * gain_two).astype(low)
    hidden, slope = gelu_pair(matmul(normed_ffn, w_inner))
    hidden = hidden.astype(low)
    slope = slope.astype(low)
    layer_out = (residual + matmul(hidden, w_outer)).astype(low).reshape(seqs, block, width)

    position = c * block + jnp.arange(block, dtype=jnp.int32)
    live = (position[None, :] < lengths[:, None])[:, :, None]
    grad_out = jnp.where(live, cotangent, 0).reshape(rows, width)
    outer_grad = matmul(hidden, grad_out, 0, 0).astype(low)
    grad_inner = (matmul(grad_out, w_outer, 1, 1) * slope.astype(jnp.float32)).astype(low)
    inner_grad = matmul(normed_ffn, grad_inner, 0, 0).astype(low)
    down, ffn_gain_grad = norm_back(residual, root_two, gain_two, matmul(grad_inner, w_inner, 1, 1))
    grad_residual = grad_out.astype(jnp.float32) + down
    grad_residual_low = grad_residual.astype(low)
    output_grad = matmul(mixed, grad_residual_low, 0, 0).astype(low)
    grad_mixed = matmul(grad_residual_low, w_output, 1, 1).astype(low).reshape(seqs, block, width)
    grad_mixed = to_heads(grad_mixed)
    dq, dk, dv, diagonals = unattend(lengths, vector_k, q, k, v, out, grad_mixed, lse, HEAD_DIM)
    grads = jnp.concatenate([to_positions(g) for g in (dq, dk, dv)], axis=2).reshape(rows, 3 * width)
    qkv_grad = matmul(normed, grads, 0, 0).astype(low)
    down, norm_gain_grad = norm_back(x, root_one, gain_one, matmul(grads, w_qkv, 1, 1))
    token_grad = (grad_residual + down).reshape(seqs, block, width)

    own_sums = table_sums(diagonals.reshape(own_heads, 2 * seq_len), buckets, seq_len)
    sums = lax.dynamic_update_slice_in_dim(jnp.zeros((buckets, heads), jnp.float32), own_sums, c * own_heads, 1)
    sums = jnp.zeros((n_fsdp, shard, small), jnp.float32).at[:, 0, :].set(sums.reshape(n_fsdp, small)).reshape(n_fsdp * shard, small)
    side = jnp.concatenate([norm_gain_grad[:, None], ffn_gain_grad[:, None], sums, jnp.zeros((n_fsdp * shard, 126 - small), jnp.float32)], axis=1).astype(low)

    outer_grad = scatter_rows(outer_grad)
    second = scatter_rows(jnp.concatenate([output_grad, inner_grad], axis=1))
    first = scatter_rows(jnp.concatenate([qkv_grad, side], axis=1))
    table_grad = first[0, 3 * width + 2 : 3 * width + 2 + small].reshape(bias_table.shape)
    return (layer_out, token_grad, first[:, 3 * width], first[:, :width], first[:, width : 2 * width], first[:, 2 * width : 3 * width],
            second[:, :width], first[:, 3 * width + 1], second[:, width:], outer_grad, table_grad)


def solution(mesh):
    rows = P("fsdp", "ctx", None)
    in_specs = (rows, rows, P("fsdp"), P("fsdp"), P("fsdp", None), P("fsdp", None), P("fsdp", None), P("fsdp", None),
                P("fsdp"), P("fsdp", None), P("fsdp", None), P("fsdp", None))
    out_specs = (rows, rows, P("fsdp"), P("fsdp", None), P("fsdp", None), P("fsdp", None), P("fsdp", None),
                 P("fsdp"), P("fsdp", None), P("fsdp", None), P("fsdp", None))
    return jax.shard_map(per_device, mesh=mesh, in_specs=in_specs, out_specs=out_specs, check_vma=False)
```

time: 2040 us -> 869 us (0.43)
  matrix products: 1140 us -> 267 us
  other arithmetic: 312 us -> 76.7 us
  blocking collectives: 158 us -> 0 us
  Pallas kernels: 0 us -> 137 us
  waiting for transfers between devices: 355 us -> 307 us
    dot_general x101 -> x15, matrix products: 1140 us -> 267 us  [the longest x12 264 us: dot(): lax.dot_general(a, b, (((ca,), (cb,)), ((), ())), precision=precision, pr...]
    sub x4 -> x0, other arithmetic: 148 us -> none  [attend_stats(): exp_scores = jnp.exp(scores - row_max)]
    pallas_call x0 -> x2, Pallas kernels: none -> 137 us  [the longest x1 80.6 us: unattend(): pl.pallas_call(functools.partial(unattend_kernel, seq_len=seq_len, head_d...]
    convert_element_type x20 -> x5, other arithmetic: 129 us -> 7.74 us  [the longest x1 4.15 us: per_device(): normed = (x * root_one * gain_one).astype(low)]
    unnamed x2 -> x0, blocking collectives: 117 us -> none
    all_gather x1 -> x0, blocking collectives: 38.4 us -> none  [fetch_each(): lax.all_gather(bias_table, 'fsdp', axis=0, tiled=True)]
    reduce_scatter x14 -> x3, waiting for transfers between devices: 272 us -> 236 us  [scatter_rows(): lax.psum_scatter(grad, ('fsdp', 'ctx'), scatter_dimension=0, tiled=True)]
    all_gather x8 -> x0, local copies, waits for them, and re-layouts: 28.8 us -> none  [the longest x4 15.1 us: per_device(): lax.all_gather(value_blocks, 'ctx', axis=1, tiled=True)]
  transfers between devices with their start and end apart: 29 -> 17, of which waited for: 5 -> 6; matrix products, arithmetic and copies ran while one was open for 59% -> 44% of each run, Pallas kernels for 0% -> 16%
where the time goes in v1:
time: 869 us; the launch traced here: 860 us
  waiting for transfers between devices  307 us (35%)
  matrix products  267 us (31%)
  Pallas kernels  137 us (16%)
  other arithmetic  76.7 us (9%)
  local copies, waits for them, and re-layouts  53.8 us (6%)
  between operations  15.1 us (2%)
    dot_general x12, matrix products, dot(): lax.dot_general(a, b, (((ca,), (cb,)), ((), ())), precision=precision, pr...  264 us
    reduce_scatter x3, waiting for transfers between devices, scatter_rows(): lax.psum_scatter(grad, ('fsdp', 'ctx'), scatter_dimension=0, tiled=True)  236 us
    pallas_call x1, Pallas kernels, unattend(): pl.pallas_call(functools.partial(unattend_kernel, seq_len=seq_len, head_d...  80.6 us
    all_gather x3, waiting for transfers between devices, gather_rows(): return lax.all_gather(mine, ('fsdp', 'ctx'), axis=0, tiled=True)  68 us
    pallas_call x1, Pallas kernels, attend(): pl.pallas_call(functools.partial(attend_kernel, seq_len=seq_len, head_dim...  56.1 us
  transfers between devices with their start and end apart: 17, of which 6 were waited for; matrix products, arithmetic and copies ran while one was open for 44% of the time, Pallas kernels for 16%

profile of v1, /device:TPU:0, one launch (start us, length us, event | category | flops | bytes accessed | tf_op | source)
XLA Modules:
  0.0 860.2 jit_solution(767757537080046652)
XLA Ops:
  11.5 1.7 fusion.40
  13.3 3.1 fusion
  17.0 68.0 %all-gather.4.cloned.1.call-done = bf16[1024,3200]{1,0:T(8,128)(2,1)} async-done(((bf16[32,3200]{1,0:T(8,128)(2,1)}), bf16[1024,3200]{1,0:T(8,128)(2,1)}) %all-gather.4.cloned.1.call-update) | async-done | bytes 6553616 | tf_op jit(solution)/shard_map/all_gather | solution.py:248
  87.0 4.1 fusion.4
  91.1 16.5 %multiply_convert_fusion.2 = bf16[2048,3072]{1,0:T(8,128)(2,1)S(1)} fusion(bf16[2048,1024]{1,0:T(8,128)(2,1)} %fusion.4, f32[3072]{0:T(1024)S(1)} %copy-done.30, bf16[1024,3200]{1,0:T(8,128)(2,1)} %all-gather.4.cloned.1.call-done), kind=kOutput, calls=%fused_computation.4 | convolution fusion | flops 12897484800 | bytes 23080960 | tf_op jit(solution)/shard_map/dot_general | solution.py:23
  107.6 4.1 fusion.57
  111.7 2.0 copy-done.9
  113.7 1.5 constant_dynamic-slice_fusion.8
  116.3 3.1 constant_dynamic-slice_fusion.6
  119.4 3.1 constant_dynamic-slice_fusion.7
  125.9 2.6 broadcast_select_fusion.10
  128.5 2.3 pad_maximum_fusion.1.q_ref
  130.8 3.4 broadcast_select_fusion.6
  134.2 2.3 pad_maximum_fusion.3.v_ref
  136.5 2.8 pad_maximum_fusion.2.k_ref
  139.3 56.1 %attend.1 = (bf16[4,1024,512]{2,1,0:T(8,128)(2,1)S(1)}, f32[4,4,2,1024]{3,2,1,0:T(2,128)S(1)}) custom-call(s32[4]{0:T(128)S(1)} %copy-done.3, f32[4,2,2048]{2,1,0:T(2,128)S(1)} %reshape.249.tvec_ref, bf16[4,1024,512]{2,1,0:T(8,128)(2,1)} %pad_maximum_fusion.1.q_ref, bf16[4,1024,512]{2,1,0:T(8,128)(2,1)} %pad_maximum_fusion.2.k_ref, ...), custom_call_target="tpu_custom_call" | custom-call | flops 8589934592 | bytes 16777216 | tf_op jit(solution)/shard_map/attend/pallas_call | solution.py:79
  196.1 3.1 broadcast_select_fusion
  200.8 2.6 pad_maximum_fusion.4
  203.4 12.3 %multiply_reduce_fusion.2 = (f32[2048]{0:T(1024)S(1)}, f32[2048,1024]{1,0:T(8,128)}) fusion(bf16[2048,1024]{1,0:T(8,128)(2,1)} %bitcast.55, bf16[1024,5120]{1,0:T(8,128)(2,1)} %all-gather.6.cloned.1.call-done, bf16[4,512,1024]{2,1,0:T(8,128)(2,1)} %param.17), kind=kOutput, calls=%fused_computation.28 | convolution fusion | flops 4303353856 | bytes 18882560 | tf_op jit(solution)/shard_map/dot_general | solution.py:23
  216.3 26.9 %fusion.11 = f32[2048,4096]{1,0:T(8,128)} fusion(bf16[1024,5120]{1,0:T(8,128)(2,1)} %all-gather.6.cloned.1.call-done, f32[2048,1024]{1,0:T(8,128)} %get-tuple-element.72, f32[1024]{0:T(1024)S(1)} %get-tuple-element.39, f32[2048]{0:T(1024)S(1)} %get-tuple-element.70), kind=kOutput, calls=%fused_computation.33 | convolution fusion | flops 17186160640 | bytes 50343936 | tf_op jit(solution)/shard_map/dot_general | solution.py:23
  243.1 30.4 %convolution_convert_fusion = bf16[4096,1024]{1,0:T(8,128)(2,1)} fusion(bf16[2048,1024]{1,0:T(8,128)(2,1)S(1)} %bitcast.50, f32[2048,4096]{1,0:T(8,128)} %fusion.11), kind=kOutput, calls=%fused_computation.29 | convolution fusion | flops 17259560960 | bytes 46137344 | tf_op jit(solution)/shard_map/dot_general | solution.py:23
  273.7 42.4 %multiply_convert_fusion = bf16[2048,4096]{1,0:T(8,128)(2,1)} fusion(bf16[2048,1024]{1,0:T(8,128)(2,1)} %bitcast.49, bf16[4096,1024]{1,0:T(8,128)(2,1)} %all-gather.8.cloned.1.call-done, f32[2048,4096]{1,0:T(8,128)} %fusion.11), kind=kOutput, calls=%fused_computation | convolution fusion | flops 17347641344 | bytes 62914560 | tf_op jit(solution)/shard_map/dot_general | solution.py:23
  316.0 25.8 %fusion.28 = (bf16[1024]{0:T(1024)(128)(2,1)S(1)}, f32[2048]{0:T(1024)S(1)}, f32[2048,1024]{1,0:T(8,128)}) fusion(f32[2048]{0:T(1024)S(1)} %get-tuple-element.70, f32[2048,1024]{1,0:T(8,128)} %get-tuple-element.72, f32[1024]{0:T(1024)S(1)} %get-tuple-element.39, bf16[2048,4096]{1,0:T(8,128)(2,1)} %multiply_convert_fusion, ...), kind=kOutput, calls=%fused_computation.70 | convolution fusion | flops 17190352896 | bytes 41965568 | tf_op jit(solution)/shard_map/dot_general | solution.py:23
  341.9 7.1 subtract_add_fusion
  349.1 8.0 convolution_convert_fusion.2
  357.1 2.0 copy-done.16
  359.2 1.5 constant_dynamic-slice_fusion.3
  362.9 2.5 collective-permute-done.4
  365.3 2.4 broadcast_select_fusion.2
  367.8 2.3 pad_maximum_fusion.5.do_ref
  370.1 80.6 %unattend.1 = (bf16[4,1024,512]{2,1,0:T(8,128)(2,1)}, bf16[4,1024,512]{2,1,0:T(8,128)(2,1)}, bf16[4,1024,512]{2,1,0:T(8,128)(2,1)}, f32[4,2,2048]{2,1,0:T(2,128)}) custom-call(s32[4]{0:T(128)} %len_ref.3, f32[4,2,2048]{2,1,0:T(2,128)} %reshape.254.tvec_ref, bf16[4,1024,512]{2,1,0:T(8,128)(2,1)} %pad_maximum_fusion.1.q_ref, ...), custom_call_target="tpu_custom_call" | custom-call | flops 21474836480 | bytes 33554432 | tf_op jit(solution)/shard_map/unattend/pallas_call | solution.py:182
  450.7 3.2 constant_dynamic-slice_fusion.2
  454.3 3.1 constant_dynamic-slice_fusion.1
  461.5 2.5 select_dynamic-update-slice_fusion.5
  463.9 3.1 select_dynamic-update-slice_fusion.4
  467.8 2.4 select_dynamic-update-slice_fusion.2
  471.7 4.5 copy-done.17
  476.1 19.6 %fusion.16 = (bf16[1024]{0:T(1024)(128)(2,1)S(1)}, f32[2048]{0:T(1024)S(1)}, f32[2048,1024]{1,0:T(8,128)}) fusion(bf16[4,512,1024]{2,1,0:T(8,128)(2,1)S(1)} %copy-done.5, f32[2048]{0:T(1024)S(1)} %bitcast.60, f32[1024]{0:T(1024)S(1)} %copy-done.23, bf16[2048,3072]{1,0:T(8,128)(2,1)} %bitcast.58, bf16[1024,3200]{1,0:T(8,128)(2,1)} %all-gather.4.cloned.1.call-done), kind=kOutput, calls=%fused_computation.38 | convolution fusion | flops 12897481728 | bytes 31479808 | tf_op jit(solution)/shard_map/dot_general | solution.py:23
  496.0 18.9 %bitcast_convert_fusion = bf16[1024,3072]{1,0:T(8,128)(2,1)} fusion(bf16[4,512,3072]{2,1,0:T(8,128)(2,1)} %copy-done.17, bf16[4,512,1024]{2,1,0:T(8,128)(2,1)S(1)} %copy-done.5, f32[1024]{0:T(1024)S(1)} %copy-done.23, f32[4,512]{1,0:T(4,128)S(1)} %copy-done.25), kind=kOutput, calls=%fused_computation.5 | convolution fusion | flops 12896436224 | bytes 23080960 | tf_op jit(solution)/shard_map/dot_general | solution.py:23
  515.0 11.0 %concatenate.52 = bf16[1024,3200]{1,0:T(8,128)(2,1)} concatenate(bf16[1024,3072]{1,0:T(8,128)(2,1)} %bitcast_convert_fusion, bf16[1024,1]{1,0:T(8,128)(2,1)S(1)} %broadcast_in_dim.76, bf16[1024,1]{1,0:T(8,128)(2,1)S(1)} %broadcast_in_dim.77, bf16[1024,32]{1,0:T(8,128)(2,1)S(1)} %bitcast.57, bf16[1024,94]{1,0:T(8,128)(2,1)S(1)} %broadcast_in_dim.75), dimensions={1} | concatenate | bytes 13107200 | tf_op jit(solution)/shard_map/concatenate | solution.py:358
  526.0 10.5 %fusion.23 = bf16[1024,1024]{0,1:T(8,128)(2,1)} fusion(bf16[2048,1024]{1,0:T(8,128)(2,1)} %bitcast.56, f32[2048,1024]{1,0:T(8,128)} %copy-done.6), kind=kOutput, calls=%fused_computation.67 | convolution fusion | flops 4298113024 | bytes 14680064 | tf_op jit(solution)/shard_map/dot_general | solution.py:23
  536.5 3.0 copy.46
  539.6 24.2 %convolution_convert_fusion.1 = bf16[1024,4096]{1,0:T(8,128)(2,1)S(1)} fusion(bf16[2048,4096]{1,0:T(8,128)(2,1)} %multiply_convert_fusion, f32[2048,1024]{1,0:T(8,128)} %get-tuple-element.72, f32[1024]{0:T(1024)S(1)} %get-tuple-element.39, f32[2048]{0:T(1024)S(1)} %get-tuple-element.70), kind=kOutput, calls=%fused_computation.30 | convolution fusion | flops 17190354944 | bytes 33566720 | tf_op jit(solution)/shard_map/dot_general | solution.py:23
  563.8 4.7 pad_maximum_fusion
  568.5 28.8 %add_convert_fusion.1 = bf16[2048,1024]{1,0:T(8,128)(2,1)} fusion(f32[2048,1024]{1,0:T(8,128)} %get-tuple-element.72, bf16[4096,1024]{1,0:T(8,128)(2,1)} %all-gather.8.cloned.1.call-done, f32[2048,4096]{1,0:T(8,128)} %fusion.11), kind=kOutput, calls=%fused_computation.26 | convolution fusion | flops 17259560960 | bytes 54525952 | tf_op jit(solution)/shard_map/dot_general | solution.py:23
  597.5 11.9 %fusion.7 = f32[2048,1024]{1,0:T(8,128)} fusion(f32[2048,1024]{1,0:T(8,128)} %copy-done.6, bf16[4,512,1024]{2,1,0:T(8,128)(2,1)} %param.17, f32[2048,1024]{1,0:T(8,128)} %get-tuple-element.74, f32[2048]{0:T(1024)S(1)} %broadcast_multiply_fusion, f32[2048]{0:T(1024)S(1)} %mul.297, f32[1024]{0:T(1024)S(1)} %copy-done.23, f32[2048]{0:T(1024)S(1)} %bitcast.63), kind=kLoop, calls=%fused_computation.20 | loop fusion | flops 14680064 | bytes 29388800 | tf_op jit(solution)/shard_map/add | solution.py:349
  609.4 87.0 %reduce-scatter.4.cloned.1.call-done = bf16[32,3200]{1,0:T(8,128)(2,1)} async-done(((bf16[1024,3200]{1,0:T(8,128)(2,1)}), bf16[32,3200]{1,0:T(8,128)(2,1)}) %reduce-scatter.4.cloned.1.call-update) | async-done | bytes 204816 | tf_op jit(solution)/shard_map/reduce_scatter | solution.py:256
  699.1 148.8 %reduce-scatter.6.cloned.1.call-done = bf16[32,5120]{1,0:T(8,128)(2,1)} async-done(((bf16[1024,5120]{1,0:T(8,128)(2,1)}), bf16[32,5120]{1,0:T(8,128)(2,1)}) %reduce-scatter.6.cloned.1.call-update) | async-done | bytes 327696 | tf_op jit(solution)/shard_map/reduce_scatter | solution.py:256
  (149 shorter events, 31.2 us)
Async XLA Ops:
  7.2 108.3 %copy-start = (bf16[256,1024]{1,0:T(8,128)(2,1)S(1)}, bf16[256,1024]{1,0:T(8,128)(2,1)}, u32[]{:S(2)}) copy-start(bf16[256,1024]{1,0:T(8,128)(2,1)} %param.27) | copy-start | bytes 1572868
  7.2 83.9 %copy-start.30 = (f32[3072]{0:T(1024)S(1)}, f32[3072]{0:T(1024)}, u32[]{:S(2)}) copy-start(f32[3072]{0:T(1024)} %constant.93.clone.1) | copy-start | bytes 36868
  7.2 77.8 %all-gather.4.cloned.1.call-start = ((), (), s32[]{:S(2)}) async-start(), calls=%async_computation.3 | async-start | bytes 6758400 | tf_op jit(solution)/shard_map/all_gather | solution.py:248
  11.4 191.9 %all-gather.6.cloned.1.call-start = ((), (), s32[]{:S(2)}) async-start(), calls=%async_computation.4 | async-start | bytes 10813440 | tf_op jit(solution)/shard_map/all_gather | solution.py:248
  13.3 260.4 %all-gather.8.cloned.1.call-start = ((), (), s32[]{:S(2)}) async-start(), calls=%async_computation.5 | async-start | bytes 8650752 | tf_op jit(solution)/shard_map/all_gather | solution.py:248
  17.0 90.6 %copy-start.19 = (f32[1,4,4,128]{3,1,2,0:T(4,128)}, f32[1,4,4,128]{3,1,2,0:T(4,128)S(1)}, u32[]{:S(2)}) copy-start(f32[1,4,4,128]{3,1,2,0:T(4,128)S(1)} %copy.50) | copy-start | bytes 24580
  86.4 0.6 copy-start.22
  111.7 2.0 copy-start.9
  111.7 11.3 %copy-start.29 = (s32[15]{0:T(128)S(1)}, s32[15]{0:T(128)}, u32[]{:S(2)}) copy-start(s32[15]{0:T(128)} %constant.107.clone) | copy-start | bytes 184
  115.3 10.6 %collective-permute-start = (bf16[4,512,512]{2,1,0:T(8,128)(2,1)}, bf16[4,512,512]{2,1,0:T(8,128)(2,1)S(1)}, u32[]{:S(2)}, u32[]{:S(2)}) collective-permute-start(bf16[4,512,512]{2,1,0:T(8,128)(2,1)} %constant_dynamic-slice_fusion.8), channel_id=1, source_target_pairs={{0,16},{16,0},{1,17},{17,1},{2,18},{18,2},{3,19},{19,3},{4,20},{20... | collective-permute-start | bytes 6291464 | tf_op jit(solution)/shard_map/ppermute | solution.py:252
  116.3 481.1 %reduce-scatter.8.cloned.1.call-start = ((), (), s32[]{:S(2)}) async-start(), calls=%async_computation.8 | async-start | bytes 8650752 | tf_op jit(solution)/shard_map/reduce_scatter | solution.py:256
  122.5 8.3 collective-permute-start.1
  122.7 8.0 collective-permute-start.2
  124.9 5.9 copy-start.26
  125.8 5.0 copy-start.7
  125.8 4.9 copy-start.8
  134.2 5.0 copy-start.3
  139.3 56.8 %copy-start.15 = (bf16[4,512,1024]{2,1,0:T(8,128)(2,1)S(1)}, bf16[4,512,1024]{2,1,0:T(8,128)(2,1)}, u32[]{:S(2)}) copy-start(bf16[4,512,1024]{2,1,0:T(8,128)(2,1)} %param.18) | copy-start | bytes 12582916
  195.4 5.4 copy-start.2
  195.4 5.4 copy-start.4
  195.6 4.2 collective-permute-start.3
  216.3 26.9 %copy-start.10 = (bf16[4,512,1024]{2,1,0:T(8,128)(2,1)S(1)}, bf16[4,512,1024]{2,1,0:T(8,128)(2,1)}, u32[]{:S(2)}) copy-start(bf16[4,512,1024]{2,1,0:T(8,128)(2,1)} %broadcast_select_fusion) | copy-start | bytes 12582916
  273.6 422.8 %reduce-scatter.4.cloned.1.call-start = ((), (), s32[]{:S(2)}) async-start(), calls=%async_computation.6 | async-start | bytes 6758400 | tf_op jit(solution)/shard_map/reduce_scatter | solution.py:256
  316.0 25.9 %copy-start.11 = (bf16[4,512,1024]{2,1,0:T(8,128)(2,1)S(1)}, bf16[4,512,1024]{2,1,0:T(8,128)(2,1)}, u32[]{:S(2)}) copy-start(bf16[4,512,1024]{2,1,0:T(8,128)(2,1)} %broadcast_select_fusion) | copy-start | bytes 12582916
  316.0 25.9 %copy-start.24 = (f32[2048]{0:T(1024)S(1)}, f32[2048]{0:T(1024)}, u32[]{:S(2)}) copy-start(f32[2048]{0:T(1024)} %get-tuple-element.69) | copy-start | bytes 24580
  349.0 8.1 copy-start.6
  349.0 12.3 %copy-start.27 = (bf16[32,16]{1,0:T(8,128)(2,1)S(1)}, bf16[32,16]{1,0:T(8,128)(2,1)}, u32[]{:S(2)}) copy-start(bf16[32,16]{1,0:T(8,128)(2,1)} %copy-done.26) | copy-start | bytes 3076
  349.0 12.3 %copy-start.28 = (s32[2048]{0:T(1024)S(1)}, s32[2048]{0:T(1024)}, u32[]{:S(2)}) copy-start(s32[2048]{0:T(1024)} %get-tuple-element.75) | copy-start | bytes 24580
  357.1 2.1 copy-start.16
  360.7 4.6 collective-permute-start.4
  450.7 6.8 copy-start.12
  450.7 8.9 %copy-start.21 = (f32[4,2,2048]{2,1,0:T(2,128)S(1)}, f32[4,2,2048]{2,1,0:T(2,128)}, u32[]{:S(2)}) copy-start(f32[4,2,2048]{2,1,0:T(2,128)} %get-tuple-element.34) | copy-start | bytes 196612
  453.9 7.5 collective-permute-start.5
  457.4 9.7 %collective-permute-start.6 = (bf16[4,512,512]{2,1,0:T(8,128)(2,1)}, bf16[4,512,512]{2,1,0:T(8,128)(2,1)}, u32[]{:S(2)}, u32[]{:S(2)}) collective-permute-start(bf16[4,512,512]{2,1,0:T(8,128)(2,1)} %constant_dynamic-slice_fusion.1), channel_id=1, source_target_pairs={{0,16},{16,0},{1,17},{17,1},{2,18},{18,2},{3,19},{19,3},{4,20},{20... | collective-permute-start | bytes 6291464 | tf_op jit(solution)/shard_map/ppermute | solution.py:252
  459.0 11.2 %collective-permute-start.7 = (bf16[4,512,512]{2,1,0:T(8,128)(2,1)}, bf16[4,512,512]{2,1,0:T(8,128)(2,1)S(1)}, u32[]{:S(2)}, u32[]{:S(2)}) collective-permute-start(bf16[4,512,512]{2,1,0:T(8,128)(2,1)} %constant_dynamic-slice_fusion), channel_id=1, source_target_pairs={{0,16},{16,0},{1,17},{17,1},{2,18},{18,2},{3,19},{19,3},{4,20},{20... | collective-permute-start | bytes 6291464 | tf_op jit(solution)/shard_map/ppermute | solution.py:252
  461.4 5.7 copy-start.14
  463.9 6.3 copy-start.13
  467.7 8.4 copy-start.5
  467.7 8.4 copy-start.20
  467.8 8.4 copy-start.23
  471.7 4.5 copy-start.17
  476.1 19.9 %copy-start.25 = (f32[4,512]{1,0:T(4,128)S(1)}, f32[4,512]{1,0:T(4,128)}, u32[]{:S(2)}) copy-start(f32[4,512]{1,0:T(4,128)} %get-tuple-element.67) | copy-start | bytes 24580
  526.0 321.9 %reduce-scatter.6.cloned.1.call-start = ((), (), s32[]{:S(2)}) async-start(), calls=%async_computation.7 | async-start | bytes 10813440 | tf_op jit(solution)/shard_map/reduce_scatter | solution.py:256
  597.4 99.0 %collective-permute-start.10 = (bf16[128,1024]{1,0:T(8,128)(2,1)}, bf16[128,1024]{1,0:T(8,128)(2,1)S(1)}, u32[]{:S(2)}, u32[]{:S(2)}) collective-permute-start(bf16[128,1024]{1,0:T(8,128)(2,1)} %reduce-scatter.8.cloned.1.call-done), channel_id=1, source_target_pairs={{0,16},{16,0},{1,17},{17,1},{2,18},{18,2},{3,19},{19,3},{4,20},{20... | collective-permute-start | bytes 786440 | tf_op jit(solution)/shard_map/ppermute | solution.py:252
  597.5 98.9 %copy-start.18 = (bf16[128,1024]{1,0:T(8,128)(2,1)S(1)}, bf16[128,1024]{1,0:T(8,128)(2,1)}, u32[]{:S(2)}) copy-start(bf16[128,1024]{1,0:T(8,128)(2,1)} %reduce-scatter.8.cloned.1.call-done) | copy-start | bytes 786436
  597.5 255.5 %copy-start.1 = (bf16[256,1024]{1,0:T(8,128)(2,1)S(1)}, bf16[256,1024]{1,0:T(8,128)(2,1)}, u32[]{:S(2)}) copy-start(bf16[256,1024]{1,0:T(8,128)(2,1)} %param.27) | copy-start | bytes 1572868
  696.4 1.7 collective-permute-start.8
  847.8 2.4 collective-permute-start.9
Sparse Core Ops, SparseCore 0:
  11.6 73.3 all-gather.3
  88.4 85.2 all-gather.5
  177.1 75.9 all-gather.7
  273.7 153.2 reduce-scatter.7
  526.1 170.2 reduce-scatter.3
  698.6 149.2 reduce-scatter.5

commit v2 on v1

v2 whole, which is shorter than its diff:
```python
import functools

import jax
import jax.numpy as jnp
import numpy as np
from jax import lax
from jax.experimental import pallas as pl
from jax.experimental.pallas import tpu as pltpu
from jax.sharding import PartitionSpec as P

LOG2E = 1.4426950408889634
LN2 = 0.6931471805599453
NEG = -1e30
TILE = 256
QT = 512
HEAD_DIM = 64
EPS = 1e-6
GELU = 0.7978845608028654
CUBIC = 0.044715
VMEM_LIMIT = 60 << 20
CHIPS = (4, 2, 2)
PIECE = 1664


def dot(a, b, ca, cb, precision=None):
    return lax.dot_general(a, b, (((ca,), (cb,)), ((), ())), precision=precision, preferred_element_type=jnp.float32)


def offsets(c, parts, block):
    return [pl.ds(pl.multiple_of(lax.rem(c + parts - j, parts) * block, block), block) for j in range(parts)]


def attend_kernel(info_ref, tvec_ref, *refs, seq_len, head_dim, parts):
    pieces, outs = refs[:parts], refs[parts : 2 * parts]
    lse_ref, strip_ref, q_ref, k_ref, v_ref, o_ref = refs[2 * parts :]
    places = offsets(info_ref[0], parts, seq_len // parts)
    for j in range(parts):
        for t, ref in enumerate((q_ref, k_ref, v_ref)):
            ref[places[j], :] = pieces[j][t, 0]

    heads = q_ref.shape[-1] // head_dim
    blocks = seq_len // TILE
    far = seq_len - QT

    @pl.when(pl.program_id(1) == 0)
    def _():
        for h in range(heads):
            wide = jnp.broadcast_to(tvec_ref[0, h : h + 1, :], (QT, tvec_ref.shape[-1]))
            strip_ref[h] = pltpu.roll(wide, 0, 1, stride=1, stride_axis=0)

    live = info_ref[1 + pl.program_id(1)]
    lane = lax.broadcasted_iota(jnp.int32, (1, q_ref.shape[-1]), 1) // head_dim
    column = lax.broadcasted_iota(jnp.int32, (1, TILE), 1)

    def with_blocks(used):
        top = TILE * used
        kept = [lane == h for h in range(heads)]
        keys = [jnp.where(kept[h], k_ref[0:top, :], 0) for h in range(heads)]
        values = [jnp.where(kept[h], v_ref[0:top, :], 1) for h in range(heads)]

        def query_tile(a, carry):
            here = pl.ds(pl.multiple_of(a * QT, QT), QT)
            q = q_ref[here, :]
            total = None
            for h in range(heads):
                at = pl.ds(pl.multiple_of(far - QT * a, TILE), top)
                scores = dot(q, keys[h], 1, 1) + strip_ref[h, :, at]
                last = jnp.where(column + (top - TILE) < live, scores[:, top - TILE :], NEG)
                scores = jnp.concatenate([scores[:, : top - TILE], last], axis=1) if used > 1 else last
                peak = jnp.max(scores, axis=1, keepdims=True)
                probs = jnp.exp2(scores - peak).astype(jnp.bfloat16)
                out = dot(probs, values[h], 1, 0)
                mass = pltpu.roll(out, head_dim, 1)
                out = out * (1.0 / mass)
                total = out if total is None else jnp.where(kept[h], out, total)
                lse = peak + jnp.log2(mass)
                lse_ref[0, 0, h : h + 1, here] = jnp.transpose(lse)[h * head_dim : h * head_dim + 1, :]
            o_ref[here, :] = total.astype(jnp.bfloat16)
            return carry

        lax.fori_loop(0, seq_len // QT, query_tile, 0, unroll=True)

    for used in range(1, blocks + 1):
        pl.when((live + TILE - 1) // TILE == used)(functools.partial(with_blocks, used))

    for j in range(parts):
        outs[j][0] = o_ref[places[j], :]


def attend(info, tvec, pieces, head_dim):
    parts = len(pieces)
    _, seqs, block, width = pieces[0].shape
    seq_len = block * parts
    pairs = width // 128
    heads = 128 // head_dim
    strip = tvec.shape[-1]
    three = pl.BlockSpec((3, 1, block, 128), lambda p, s, n: (0, s, 0, p))
    one = pl.BlockSpec((1, block, 128), lambda p, s, n: (s, 0, p))
    return pl.pallas_call(
        functools.partial(attend_kernel, seq_len=seq_len, head_dim=head_dim, parts=parts),
        grid_spec=pltpu.PrefetchScalarGridSpec(
            num_scalar_prefetch=1, grid=(pairs, seqs),
            in_specs=[pl.BlockSpec((1, heads, strip), lambda p, s, n: (p, 0, 0))] + [three] * parts,
            out_specs=[one] * parts + [pl.BlockSpec((1, 1, heads, seq_len), lambda p, s, n: (p, s, 0, 0))],
            scratch_shapes=[pltpu.VMEM((heads, QT, strip), jnp.float32)] + [pltpu.VMEM((seq_len, 128), jnp.bfloat16)] * 4),
        out_shape=[jax.ShapeDtypeStruct((seqs, block, width), jnp.bfloat16)] * parts + [jax.ShapeDtypeStruct((pairs, seqs, heads, seq_len), jnp.float32)],
        compiler_params=pltpu.CompilerParams(vmem_limit_bytes=VMEM_LIMIT),
        cost_estimate=pl.CostEstimate(flops=16 * seqs * width * seq_len * seq_len, bytes_accessed=8 * seqs * seq_len * width, transcendentals=0),
        name="attend",
    )(info, tvec, *pieces)


def unattend_kernel(info_ref, tvec_ref, *refs, seq_len, head_dim, parts):
    pieces, out_pieces, do_pieces = refs[:parts], refs[parts : 2 * parts], refs[2 * parts : 3 * parts]
    lse_ref = refs[3 * parts]
    grads, dt_ref = refs[3 * parts + 1 : 4 * parts + 1], refs[4 * parts + 1]
    strip_ref, sums_ref, dk_acc, dv_acc, q_ref, k_ref, v_ref, o_ref, do_ref, dq_ref = refs[4 * parts + 2 :]
    places = offsets(info_ref[0], parts, seq_len // parts)
    for j in range(parts):
        for t, ref in enumerate((q_ref, k_ref, v_ref)):
            ref[places[j], :] = pieces[j][t, 0]
        o_ref[places[j], :] = out_pieces[j][0]
        do_ref[places[j], :] = do_pieces[j][0]
    heads = q_ref.shape[-1] // head_dim
    blocks = seq_len // TILE
    far = seq_len - TILE
    bands = (2 * blocks - 1) * TILE

    @pl.when(pl.program_id(1) == 0)
    def _():
        for h in range(heads):
            wide = jnp.broadcast_to(tvec_ref[0, h : h + 1, :], (TILE, tvec_ref.shape[-1]))
            wide = pltpu.roll(wide, 0, 1, stride=1, stride_axis=0)
            for b in range(2 * blocks - 1):
                strip_ref[TILE * b : TILE * (b + 1), TILE * h : TILE * (h + 1)] = jnp.transpose(wide[:, TILE * b : TILE * (b + 1)])
        sums_ref[...] = jnp.zeros_like(sums_ref)

    live = info_ref[1 + pl.program_id(1)]
    lane = lax.broadcasted_iota(jnp.int32, (1, q_ref.shape[-1]), 1) // head_dim
    row = lax.broadcasted_iota(jnp.int32, (TILE, 1), 0)
    kept = [lane == h for h in range(heads)]

    def with_blocks(used):
        top = TILE * used
        dk_acc[0:top, :] = jnp.zeros((top, dk_acc.shape[1]), jnp.float32)
        dv_acc[0:top, :] = jnp.zeros((top, dv_acc.shape[1]), jnp.float32)

        def query_tile(a, carry):
            here = pl.ds(pl.multiple_of(a * TILE, TILE), TILE)
            q = q_ref[here, :]
            do = do_ref[here, :]
            product = jnp.transpose(do.astype(jnp.float32) * o_ref[here, :].astype(jnp.float32))
            qs = jnp.concatenate([jnp.where(kept[h], q, 0) for h in range(heads)], axis=0)
            dos = jnp.concatenate([jnp.where(kept[h], do, 0) for h in range(heads)], axis=0)
            delta = jnp.concatenate([jnp.sum(product[h * head_dim : (h + 1) * head_dim], axis=0, keepdims=True) for h in range(heads)], axis=1)
            lse = jnp.concatenate([lse_ref[0, 0, h : h + 1, here] for h in range(heads)], axis=1)
            at = pl.ds(pl.multiple_of(far - TILE * a, TILE), top)
            kb = k_ref[0:top, :]
            vb = v_ref[0:top, :]
            p = jnp.exp2(dot(kb, qs, 1, 1) + strip_ref[at, :] - lse)
            last = jnp.where(row + (top - TILE) < live, p[top - TILE :], 0.0)
            p = jnp.concatenate([p[: top - TILE], last], axis=0) if used > 1 else last
            ds = p * (dot(vb, dos, 1, 1) - delta)
            sums_ref[at, :] += ds
            p = p.astype(jnp.bfloat16)
            ds = ds.astype(jnp.bfloat16)
            dv_acc[0:top, :] += dot(p, dos, 1, 0)
            dk_acc[0:top, :] += dot(ds, qs, 1, 0)
            dq = dot(ds, kb, 0, 0)
            dq_total = dq[0:TILE]
            for h in range(1, heads):
                dq_total = jnp.where(kept[h], dq[TILE * h : TILE * (h + 1)], dq_total)
            dq_ref[here, :] = (dq_total * LN2).astype(jnp.bfloat16)
            return carry

        lax.fori_loop(0, used, query_tile, 0)
        if used < blocks:
            dq_ref[top:, :] = jnp.zeros((seq_len - top, q_ref.shape[-1]), jnp.bfloat16)
            dk_acc[top:, :] = jnp.zeros((seq_len - top, q_ref.shape[-1]), jnp.float32)
            dv_acc[top:, :] = jnp.zeros((seq_len - top, q_ref.shape[-1]), jnp.float32)

    for used in range(1, blocks + 1):
        pl.when((live + TILE - 1) // TILE == used)(functools.partial(with_blocks, used))

    for j in range(parts):
        grads[j][0, 0] = dq_ref[places[j], :]
        grads[j][1, 0] = dk_acc[places[j], :].astype(jnp.bfloat16)
        grads[j][2, 0] = dv_acc[places[j], :].astype(jnp.bfloat16)

    @pl.when(pl.program_id(1) == pl.num_programs(1) - 1)
    def _():
        wide = dt_ref.shape[-1]
        for h in range(heads):
            turned = jnp.concatenate([jnp.transpose(sums_ref[TILE * b : TILE * (b + 1), TILE * h : TILE * (h + 1)]) for b in range(2 * blocks - 1)]
                                     + [jnp.zeros((TILE, wide - bands), jnp.float32)], axis=1)
            group = turned[0:8]
            for g in range(1, TILE // 8):
                group = group + pltpu.roll(turned[8 * g : 8 * (g + 1)], wide - 8 * g, 1)
            diagonal = group[0:1]
            for s in range(1, 8):
                diagonal = diagonal + pltpu.roll(group[s : s + 1], wide - s, 1)
            dt_ref[0, h : h + 1, :] = diagonal


def unattend(info, tvec, pieces, outs, do, lse, head_dim):
    parts = len(pieces)
    _, seqs, block, width = pieces[0].shape
    seq_len = block * parts
    pairs = width // 128
    heads = 128 // head_dim
    strip = tvec.shape[-1]
    bands = 2 * seq_len - TILE
    three = pl.BlockSpec((3, 1, block, 128), lambda p, s, n: (0, s, 0, p))
    one = pl.BlockSpec((1, block, 128), lambda p, s, n: (s, 0, p))
    vec = pl.BlockSpec((1, heads, strip), lambda p, s, n: (p, 0, 0))
    return pl.pallas_call(
        functools.partial(unattend_kernel, seq_len=seq_len, head_dim=head_dim, parts=parts),
        grid_spec=pltpu.PrefetchScalarGridSpec(
            num_scalar_prefetch=1, grid=(pairs, seqs),
            in_specs=[vec] + [three] * parts + [one] * (2 * parts) + [pl.BlockSpec((1, 1, heads, seq_len), lambda p, s, n: (p, s, 0, 0))],
            out_specs=[three] * parts + [vec],
            scratch_shapes=[pltpu.VMEM((bands, heads * TILE), jnp.float32), pltpu.VMEM((bands, heads * TILE), jnp.float32),
                            pltpu.VMEM((seq_len, 128), jnp.float32), pltpu.VMEM((seq_len, 128), jnp.float32)]
            + [pltpu.VMEM((seq_len, 128), jnp.bfloat16)] * 6),
        out_shape=[jax.ShapeDtypeStruct((3, seqs, block, width), jnp.bfloat16)] * parts + [jax.ShapeDtypeStruct((pairs, heads, strip), jnp.float32)],
        compiler_params=pltpu.CompilerParams(vmem_limit_bytes=VMEM_LIMIT),
        cost_estimate=pl.CostEstimate(flops=40 * seqs * width * seq_len * seq_len, bytes_accessed=16 * seqs * seq_len * width, transcendentals=0),
        name="unattend",
    )(info, tvec, *pieces, *outs, *do, lse)


def bucket_edges():
    distance = np.arange(1, 512)
    scaled = 8 + np.floor(np.log(distance / 8.0) / np.log(16.0) * 8.0)
    level = np.where(distance < 8, distance, np.minimum(15, scaled))
    return np.array([distance[level >= target][0] for target in range(1, 16)], np.int32)

def levels_of(offset):
    level = jnp.sum((jnp.abs(offset)[:, None] >= jnp.asarray(bucket_edges())).astype(jnp.int32), axis=1)
    return level + 16 * (offset > 0).astype(jnp.int32)

def bias_vectors(table, seq_len, tile=TILE):
    x = jnp.arange(2 * seq_len, dtype=jnp.int32)
    far = seq_len - tile
    offset = jnp.where(x < 2 * seq_len - tile, x - far, x - far - 2 * seq_len)
    onehot = (levels_of(offset)[:, None] == jnp.arange(table.shape[0])).astype(jnp.float32)
    return jnp.einsum("xb,bh->hx", onehot, table.astype(jnp.float32) * LOG2E, precision=lax.Precision.HIGHEST)

def table_sums(diag, buckets, seq_len):
    x = jnp.arange(2 * seq_len, dtype=jnp.int32)
    far = seq_len - TILE
    offset = jnp.where(x < 2 * seq_len - TILE, x - far, x - far - 2 * seq_len)
    onehot = ((levels_of(offset)[:, None] == jnp.arange(buckets)) & (jnp.abs(offset) < seq_len)[:, None]).astype(jnp.float32)
    return jnp.einsum("zb,hz->bh", onehot, diag, precision=lax.Precision.HIGHEST)


class Place:
    def __init__(self):
        c = lax.axis_index("ctx")
        f = lax.axis_index("fsdp")
        self.c = c
        self.other = 1 - c
        z, y, x = f // 4, (f // 2) % 2, f % 2
        self.z, self.up, self.down, self.far = z, (z + 1) % 4, (z + 3) % 4, (z + 2) % 4
        self.own = (y, x)
        self.u = ((y + c) % 2, (x + 1 - c) % 2)
        self.w = ((y + 1 - c) % 2, (x + c) % 2)
        self.uw = (1 - y, 1 - x)
        flat = lambda zz, col: {"fsdp": zz * 4 + col[0] * 2 + col[1]}
        self.to = {"u": flat(z, self.u), "w": flat(z, self.w), "up": flat(self.up, self.own),
                   "down": flat(self.down, self.own), "core": {"ctx": 1 - c}}

    def greet(self):
        barrier = pltpu.get_barrier_semaphore()
        for target in self.to.values():
            pl.semaphore_signal(barrier, inc=1, device_id=target, device_id_type=pl.DeviceIdType.MESH)
        pl.semaphore_wait(barrier, len(self.to))


class Copies:
    def __init__(self, place, send, recv):
        self.place, self.send, self.recv = place, send, recv
        self.made = {}

    def start(self, name, src, dst, to):
        i = len(self.made)
        copy = pltpu.make_async_remote_copy(src_ref=src, dst_ref=dst, send_sem=self.send.at[i], recv_sem=self.recv.at[i],
                                            device_id=self.place.to[to], device_id_type=pl.DeviceIdType.MESH)
        copy.start()
        self.made[name] = copy

    def arrived(self, name):
        self.made[name].wait_recv()

    def finish(self):
        for copy in self.made.values():
            copy.wait_send()


def windows(columns, size):
    cuts = list(range(0, columns, size))
    if len(cuts) > 1 and columns - cuts[-1] < size // 2:
        cuts.pop()
    return [(a, b - a) for a, b in zip(cuts, cuts[1:] + [columns])]


def gather_steps(i, shard, out, window, place, copies, local):
    p = place
    columns = pl.ds(*window)
    name = lambda s: (i, s)
    levels = [p.z, p.down, p.far, p.up]
    at = lambda k, col: out.at[levels[k], col[0], col[1], p.c, :, columns]
    mine = shard.at[p.c, :, columns]
    theirs = shard.at[p.other, :, columns]
    kept = [pltpu.make_async_copy(mine, at(0, p.own), local.at[2 * i]),
            pltpu.make_async_copy(theirs, out.at[p.z, p.own[0], p.own[1], p.other, :, columns], local.at[2 * i + 1])]

    def own(k):
        if k == 0:
            for copy in kept:
                copy.start()
        else:
            copies.arrived(name("z %d" % k))
        source = mine if k == 0 else at(k, p.own)
        if k < 3:
            copies.start(name("z %d" % (k + 1)), source, at(k, p.own), "up")
        copies.start(name("u %d" % k), source, at(k, p.own), "u")
        copies.start(name("w own %d" % k), source, at(k, p.own), "w")
        if k > 0:
            copies.start(name("core own %d" % k), source, at(k, p.own), "core")

    def turn(k):
        copies.arrived(name("u %d" % k))
        copies.start(name("w u %d" % k), at(k, p.u), at(k, p.u), "w")
        copies.start(name("core u %d" % k), at(k, p.u), at(k, p.u), "core")

    def across(k):
        copies.arrived(name("w own %d" % k))
        copies.start(name("core w %d" % k), at(k, p.w), at(k, p.w), "core")
        copies.arrived(name("w u %d" % k))
        copies.start(name("core uw %d" % k), at(k, p.uw), at(k, p.uw), "core")

    def end():
        for k in range(4):
            for what in ("own", "u", "w", "uw"):
                if k > 0 or what != "own":
                    copies.arrived(name("core %s %d" % (what, k)))
        for copy in kept:
            copy.wait()

    def step(n):
        if n < 4:
            own(n)
        if 0 <= n - 1 < 4:
            turn(n - 1)
        if 0 <= n - 2 < 4:
            across(n - 2)

    return [functools.partial(step, n) for n in range(6)] + [end]


GATHER_COPIES = 3 + 4 + 8 + 15


def staggered(chains):
    for step in range(len(chains) - 1 + max(len(chain) for chain in chains)):
        for i, chain in enumerate(chains):
            if 0 <= step - i < len(chain):
                chain[step - i]()


def gather_kernel(*refs, count):
    shards, outs = refs[:count], refs[count : 2 * count]
    send, recv, local = refs[2 * count :]
    place = Place()
    place.greet()
    copies = Copies(place, send, recv)
    parts = [(i, window) for i in range(count) for window in windows(shards[i].shape[-1], PIECE)]
    staggered([gather_steps(n, shards[i], outs[i], window, place, copies, local) for n, (i, window) in enumerate(parts)])
    copies.finish()


def gather_all(shards, collective_id):
    split = [s.reshape(2, s.shape[0] // 2, s.shape[1]) for s in shards]
    count = len(shards)
    parts = sum(len(windows(s.shape[-1], PIECE)) for s in split)
    anywhere = pl.BlockSpec(memory_space=pl.ANY)
    outs = pl.pallas_call(
        functools.partial(gather_kernel, count=count),
        in_specs=[anywhere] * count,
        out_specs=[anywhere] * count,
        out_shape=[jax.ShapeDtypeStruct(CHIPS + s.shape, s.dtype) for s in split],
        scratch_shapes=[pltpu.SemaphoreType.DMA((GATHER_COPIES * parts,)), pltpu.SemaphoreType.DMA((GATHER_COPIES * parts,)),
                        pltpu.SemaphoreType.DMA((2 * parts,))],
        compiler_params=pltpu.CompilerParams(collective_id=collective_id, has_side_effects=True),
        name="gather_rows",
    )(*split)
    return [o.reshape(-1, o.shape[-1]) for o in outs]


def add_into(acc, came):
    lead = acc.shape[:-2]
    total = int(np.prod(lead))
    if total == 1:
        index = (0,) * len(lead)
        acc[index] = acc[index] + came[index]
        return

    def body(n, carry):
        index = []
        for extent in reversed(lead):
            index.append(n % extent)
            n = n // extent
        index = tuple(reversed(index))
        acc[index] = acc[index] + came[index]
        return carry

    lax.fori_loop(0, total, body, 0)


def scatter_buffers(rows, columns):
    shapes = [(4, 2, 2), (4, 2, 2), (2, 4), (4,), (3,)]
    return [pltpu.VMEM(lead + (rows, columns), jnp.bfloat16) for lead in shapes]


SCATTER_BUFFERS = 5
SCATTER_COPIES = 1 + 2 + 1 + 3 + 1


def scatter_steps(i, grad, out, window, buffers, place, copies, local):
    p = place
    acc, came, by_w, by_u, by_z = buffers
    columns = pl.ds(*window)
    name = lambda s: (i, s)
    line = lambda col: acc.at[:, col[0], col[1]]
    at = lambda z: acc.at[z, p.own[0], p.own[1]]
    load = pltpu.make_async_copy(grad.at[:, :, :, p.c, :, columns], acc, local.at[i])

    def first():
        load.start()
        copies.start(name("core"), grad.at[:, :, :, p.other, :, columns], came, "core")

    def second():
        load.wait()
        copies.arrived(name("core"))
        add_into(line(p.uw), came.at[:, p.uw[0], p.uw[1]])
        copies.start(name("w 1"), line(p.uw), by_w.at[1], "w")
        add_into(line(p.w), came.at[:, p.w[0], p.w[1]])
        copies.start(name("w 0"), line(p.w), by_w.at[0], "w")
        add_into(line(p.u), came.at[:, p.u[0], p.u[1]])
        add_into(line(p.own), came.at[:, p.own[0], p.own[1]])

    def third():
        copies.arrived(name("w 1"))
        add_into(line(p.u), by_w.at[1])
        copies.start(name("u"), line(p.u), by_u, "u")
        copies.arrived(name("w 0"))
        add_into(line(p.own), by_w.at[0])

    def fourth():
        copies.arrived(name("u"))
        add_into(line(p.own), by_u)
        copies.start(name("z 0"), at(p.down), by_z.at[0], "up")

    def climb(k, level):
        def run():
            copies.arrived(name("z %d" % k))
            add_into(at(level), by_z.at[k])
            copies.start(name("z %d" % (k + 1)), at(level), by_z.at[k + 1], "up")
        return run

    def last():
        copies.arrived(name("z 2"))
        out[p.c, :, columns] = at(p.z)[...] + by_z[2]
        copies.start(name("out"), out.at[p.c, :, columns], out.at[p.c, :, columns], "core")

    def end():
        copies.arrived(name("out"))

    return [first, second, third, fourth, climb(0, p.far), climb(1, p.up), last, end]


def scatter_kernel(*refs, count):
    grads, outs = refs[:count], refs[count : 2 * count]
    parts = [(i, window) for i in range(count) for window in windows(grads[i].shape[-1], PIECE)]
    buffers = [refs[2 * count + SCATTER_BUFFERS * n : 2 * count + SCATTER_BUFFERS * (n + 1)] for n in range(len(parts))]
    send, recv, local = refs[2 * count + SCATTER_BUFFERS * len(parts) :]
    place = Place()
    place.greet()
    copies = Copies(place, send, recv)
    staggered([scatter_steps(n, grads[i], outs[i], window, buffers[n], place, copies, local) for n, (i, window) in enumerate(parts)])
    copies.finish()


def scatter_all(grads, collective_id):
    split = [g.reshape(CHIPS + (2, g.shape[0] // 32, g.shape[1])) for g in grads]
    count = len(grads)
    parts = [(g.shape[-2], window[1]) for g in split for window in windows(g.shape[-1], PIECE)]
    outs = pl.pallas_call(
        functools.partial(scatter_kernel, count=count),
        in_specs=[pl.BlockSpec(memory_space=pl.ANY)] * count,
        out_specs=[pl.BlockSpec(memory_space=pltpu.VMEM)] * count,
        out_shape=[jax.ShapeDtypeStruct(g.shape[3:], g.dtype) for g in split],
        scratch_shapes=[b for part in parts for b in scatter_buffers(*part)]
        + [pltpu.SemaphoreType.DMA((SCATTER_COPIES * len(parts),)), pltpu.SemaphoreType.DMA((SCATTER_COPIES * len(parts),)),
           pltpu.SemaphoreType.DMA((len(parts),))],
        compiler_params=pltpu.CompilerParams(collective_id=collective_id, has_side_effects=True, vmem_limit_bytes=60 << 20),
        name="scatter_rows",
    )(*split)
    return [o.reshape(-1, o.shape[-1]) for o in outs]


def inverse_root(v):
    return lax.rsqrt(jnp.mean(v * v, axis=-1, keepdims=True) + EPS)


def norm_back(v, c, gain, e):
    scaled = e * v * c
    down = c * gain * e - v * (c * c) * jnp.mean(gain * scaled, axis=-1, keepdims=True)
    return down, jnp.sum(scaled, axis=0, keepdims=True)


def gelu_pair(u):
    square = u * u
    t = jnp.tanh(u * (GELU + GELU * CUBIC * square))
    half = 0.5 * u
    slope = 0.5 + 0.5 * t + half * (1.0 - t * t) * (GELU + 3.0 * GELU * CUBIC * square)
    return half + half * t, slope


def group(c, j, parts):
    return lax.rem(c + j, parts)


def resident(shape):
    return pl.BlockSpec(shape, lambda i, n: (0,) * len(shape), pipeline_mode=pl.Buffered(1))


def tiles(shape, axis):
    at = lambda i, n: tuple(i if a == axis else 0 for a in range(len(shape)))
    return pl.BlockSpec(shape, at)


def params():
    return pltpu.CompilerParams(vmem_limit_bytes=VMEM_LIMIT)


def cost(flops, size):
    return pl.CostEstimate(flops=int(flops), bytes_accessed=int(size), transcendentals=0)


def project_kernel(info_ref, x_ref, gain_ref, w_ref, normed_ref, *outs, parts):
    c = info_ref[0]
    x = x_ref[...].astype(jnp.float32)
    width = x.shape[1]
    share = width // parts
    normed = (x * inverse_root(x) * gain_ref[...]).astype(jnp.bfloat16)
    normed_ref[...] = normed
    for j in reversed(range(parts)):
        for t in range(3):
            at = pl.ds(pl.multiple_of(t * width + group(c, j, parts) * share, 128), share)
            y = dot(normed, w_ref[:, at], 1, 0)
            outs[j][t] = (y * LOG2E if t == 1 else y).astype(jnp.bfloat16)


def project(info, x, gain, w, parts):
    rows, width = x.shape
    tile = min(512, rows)
    share = width // parts
    return pl.pallas_call(
        functools.partial(project_kernel, parts=parts),
        grid_spec=pltpu.PrefetchScalarGridSpec(
            num_scalar_prefetch=1, grid=(rows // tile,),
            in_specs=[tiles((tile, width), 0), resident((1, width)), resident(w.shape)],
            out_specs=[tiles((tile, width), 0)] + [tiles((3, tile, share), 1)] * parts),
        out_shape=[jax.ShapeDtypeStruct((rows, width), jnp.bfloat16)] + [jax.ShapeDtypeStruct((3, rows, share), jnp.bfloat16)] * parts,
        compiler_params=params(),
        cost_estimate=cost(6 * rows * width * width, 10 * rows * width + 6 * width * width),
        name="project",
    )(info, x, gain, w)


def feed_kernel(info_ref, x_ref, cot_ref, gain_ref, wo_ref, w_ref, *refs, parts, block):
    mixed = refs[:parts]
    mixed_ref, normed_ref, hidden_ref, layer_ref, inner_ref, residual_ref, low_ref, gain_grad_ref = refs[parts : parts + 8]
    grads = refs[parts + 8 : 2 * parts + 8]
    slope_ref = refs[2 * parts + 8]
    c = info_ref[0]
    tile, width = x_ref.shape
    share = width // parts
    chunk = w_ref.shape[0]
    hidden_width = w_ref.shape[1] // 2
    low = jnp.bfloat16
    rows_of = [pl.ds(pl.multiple_of(group(c, j, parts) * share, 128), share) for j in range(parts)]

    residual = x_ref[...].astype(jnp.float32)
    for j in range(parts):
        mixed_ref[:, rows_of[j]] = mixed[j][...]
        residual = residual + dot(mixed[j][...], wo_ref[rows_of[j], :], 1, 0)
    root = inverse_root(residual)
    gain = gain_ref[...]
    normed = (residual * root * gain).astype(low)
    normed_ref[...] = normed
    layer = None
    for k in range(0, hidden_width, chunk):
        value, slope = gelu_pair(dot(normed, w_ref[:, k : k + chunk], 1, 0))
        value = value.astype(low)
        hidden_ref[:, k : k + chunk] = value
        slope_ref[:, k : k + chunk] = slope.astype(slope_ref.dtype)
        part = dot(value, w_ref[:, hidden_width + k : hidden_width + k + chunk], 1, 0)
        layer = part if layer is None else layer + part
    layer_ref[...] = (residual + layer).astype(low)

    start = pl.program_id(0) * tile
    position = c * block + lax.rem(start, block) + lax.broadcasted_iota(jnp.int32, (tile, 1), 0)
    grad = jnp.where(position < info_ref[1 + start // block], cot_ref[...], 0)
    up = None
    for k in range(0, hidden_width, chunk):
        inner = (dot(grad, w_ref[:, hidden_width + k : hidden_width + k + chunk], 1, 1) * slope_ref[:, k : k + chunk].astype(jnp.float32)).astype(low)
        inner_ref[:, k : k + chunk] = inner
        part = dot(inner, w_ref[:, k : k + chunk], 1, 1)
        up = part if up is None else up + part
    down, gain_grad = norm_back(residual, root, gain, up)

    @pl.when(pl.program_id(0) == 0)
    def _():
        gain_grad_ref[...] = jnp.zeros_like(gain_grad_ref)

    gain_grad_ref[...] += gain_grad
    down = down + grad.astype(jnp.float32)
    residual_ref[...] = down
    down = down.astype(low)
    low_ref[...] = down
    for j in range(parts):
        grads[j][...] = dot(down, wo_ref[rows_of[j], :], 1, 1).astype(low)


def feed(info, x, cot, gain, wo, w, mixed, block, tile=256):
    parts = len(mixed)
    rows, width = x.shape
    hidden = w.shape[1] // 2
    tile = min(tile, block)
    share = width // parts
    t = lambda w: tiles((tile, w), 0)
    low = lambda w: jax.ShapeDtypeStruct((rows, w), jnp.bfloat16)
    return pl.pallas_call(
        functools.partial(feed_kernel, parts=parts, block=block),
        grid_spec=pltpu.PrefetchScalarGridSpec(
            num_scalar_prefetch=1, grid=(rows // tile,),
            in_specs=[t(width), t(width), resident((1, width)), resident(wo.shape), resident(w.shape)] + [t(share)] * parts,
            out_specs=[t(width), t(width), t(hidden), t(width), t(hidden), t(width), t(width), resident((1, width))] + [t(share)] * parts,
            scratch_shapes=[pltpu.VMEM((tile, hidden), jnp.bfloat16)]),
        out_shape=[low(width), low(width), low(hidden), low(width), low(hidden), jax.ShapeDtypeStruct((rows, width), jnp.float32), low(width),
                   jax.ShapeDtypeStruct((1, width), jnp.float32)] + [low(share)] * parts,
        compiler_params=params(),
        cost_estimate=cost(rows * width * (8 * hidden + 4 * width), rows * (18 * width + 4 * hidden) + 4 * width * hidden),
        name="feed",
    )(info, x, cot, gain, wo, w, *mixed)


def unproject_kernel(info_ref, x_ref, residual_ref, gain_ref, w_ref, *refs, parts):
    came = refs[:parts]
    token_ref, grads_ref, gain_grad_ref = refs[parts:]
    c = info_ref[0]
    x = x_ref[...].astype(jnp.float32)
    width = x.shape[1]
    share = width // parts
    up = None
    for j in range(parts):
        for t in range(3):
            at = pl.ds(pl.multiple_of(t * width + group(c, j, parts) * share, 128), share)
            piece = came[j][t]
            grads_ref[:, at] = piece
            part = dot(piece, w_ref[:, at], 1, 1)
            up = part if up is None else up + part
    down, gain_grad = norm_back(x, inverse_root(x), gain_ref[...], up)

    @pl.when(pl.program_id(0) == 0)
    def _():
        gain_grad_ref[...] = jnp.zeros_like(gain_grad_ref)

    gain_grad_ref[...] += gain_grad
    token_ref[...] = residual_ref[...] + down


def unproject(info, x, residual, gain, w, came):
    parts = len(came)
    rows, width = x.shape
    tile = min(512, rows)
    share = width // parts
    return pl.pallas_call(
        functools.partial(unproject_kernel, parts=parts),
        grid_spec=pltpu.PrefetchScalarGridSpec(
            num_scalar_prefetch=1, grid=(rows // tile,),
            in_specs=[tiles((tile, width), 0), tiles((tile, width), 0), resident((1, width)), resident(w.shape)] + [tiles((3, tile, share), 1)] * parts,
            out_specs=[tiles((tile, width), 0), tiles((tile, 3 * width), 0), resident((1, width))]),
        out_shape=[jax.ShapeDtypeStruct((rows, width), jnp.float32), jax.ShapeDtypeStruct((rows, 3 * width), jnp.bfloat16), jax.ShapeDtypeStruct((1, width), jnp.float32)],
        compiler_params=params(),
        cost_estimate=cost(6 * rows * width * width, 22 * rows * width + 6 * width * width),
        name="unproject",
    )(info, x, residual, gain, w, *came)


def gather_rows(shard):
    n = lax.axis_size("ctx")
    part = shard.shape[0] // n
    mine = lax.dynamic_slice_in_dim(shard, lax.axis_index("ctx") * part, part, 0)
    return lax.all_gather(mine, ("fsdp", "ctx"), axis=0, tiled=True)


def scatter_rows(grad):
    part = lax.psum_scatter(grad, ("fsdp", "ctx"), scatter_dimension=0, tiled=True)
    if lax.axis_size("ctx") != 2:
        return lax.all_gather(part, "ctx", axis=0, tiled=True)
    other = lax.ppermute(part, "ctx", [(0, 1), (1, 0)])
    first = lax.axis_index("ctx") == 0
    return jnp.concatenate([jnp.where(first, part, other), jnp.where(first, other, part)], axis=0)


def exchange(pieces):
    n = len(pieces)
    return [pieces[0]] + [lax.ppermute(pieces[j], "ctx", [(i, (i + j) % n) for i in range(n)]) for j in range(1, n)]


def give_back(pieces):
    n = len(pieces)
    return [pieces[0]] + [lax.ppermute(pieces[j], "ctx", [(i, (i - j) % n) for i in range(n)]) for j in range(1, n)]


def by_chip(shape):
    return shape == (2, 16)


def per_device(tokens, cotangent, lengths, norm_gain, query_weight, key_weight, value_weight, output_weight,
               ffn_gain, inner_weight, outer_weight, bias_table):
    seqs, block, width = tokens.shape
    rows = seqs * block
    n_ctx = lax.axis_size("ctx")
    n_fsdp = lax.axis_size("fsdp")
    c = lax.axis_index("ctx")
    seq_len = block * n_ctx
    heads = bias_table.shape[1]
    buckets = bias_table.shape[0] * n_fsdp
    shard = query_weight.shape[0]
    hidden_width = inner_weight.shape[1]
    slabs = hidden_width // width
    own_heads = heads // n_ctx
    pairs = own_heads * HEAD_DIM // 128
    per_pair = 128 // HEAD_DIM
    small = bias_table.size
    share = width // n_ctx
    low = jnp.bfloat16
    remote = by_chip((n_ctx, n_fsdp))
    info = jnp.concatenate([jnp.full((1,), c, jnp.int32), lengths])

    inner = inner_weight.reshape(shard, n_fsdp, slabs, shard).transpose(0, 2, 1, 3).reshape(shard, hidden_width)
    outer = outer_weight.reshape(slabs, shard, width).transpose(1, 0, 2).reshape(shard, slabs * width)
    w_feed = gather_rows(jnp.concatenate([inner, outer], axis=1))
    side = jnp.concatenate([norm_gain[:, None], ffn_gain[:, None], jnp.broadcast_to(bias_table.reshape(1, small), (shard, small)),
                            jnp.zeros((shard, 126 - small), low)], axis=1)
    first = jnp.concatenate([query_weight, key_weight, value_weight, side], axis=1)
    if remote:
        first, w_output = gather_all([first, output_weight], 1)
    else:
        first, w_output = gather_rows(first), gather_rows(output_weight)
    side = first[:, 3 * width :]
    gain_one = side[:, 0].astype(jnp.float32)[None, :]
    gain_two = side[:, 1].astype(jnp.float32)[None, :]
    table = side[::shard, 2 : 2 + small].reshape(buckets, heads)
    own_table = lax.dynamic_slice_in_dim(table, c * own_heads, own_heads, 1)
    vector_q = bias_vectors(own_table, seq_len, QT).reshape(pairs, per_pair, 2 * seq_len)
    vector_k = bias_vectors(own_table, seq_len, TILE).reshape(pairs, per_pair, 2 * seq_len)

    x = tokens.reshape(rows, width)
    cot = cotangent.reshape(rows, width)
    normed, *qkv = project(info, x, gain_one, first, n_ctx)
    qkv = exchange([p.reshape(3, seqs, block, share) for p in qkv])
    *out, lse = attend(info, vector_q, qkv, HEAD_DIM)
    mixed = [m.reshape(rows, share) for m in give_back(out)]
    (mixed, normed_ffn, hidden, layer_out, grad_inner, grad_residual, grad_low, ffn_gain_grad, *grad_mixed) = feed(
        info, x, cot, gain_two, w_output, w_feed, mixed, block)
    grad_mixed = exchange([g.reshape(seqs, block, share) for g in grad_mixed])

    position = c * block + jnp.arange(block, dtype=jnp.int32)
    live = (position[None, :] < lengths[:, None])[:, :, None]
    grad_out = jnp.where(live, cotangent, 0).reshape(rows, width)
    inner_grad = dot(normed_ffn, grad_inner, 0, 0).astype(low)
    outer_grad = [dot(hidden[:, q * width : (q + 1) * width], grad_out, 0, 0).astype(low) for q in range(slabs)]
    feed_grad = jnp.concatenate([inner_grad] + outer_grad, axis=1)
    feed_grad, grad_mixed = lax.optimization_barrier((feed_grad, grad_mixed))
    feed_grad = scatter_rows(feed_grad)

    *grads, diagonals = unattend(info, vector_k, qkv, out, grad_mixed, lse, HEAD_DIM)
    grads = [g.reshape(3, rows, share) for g in give_back(grads)]
    token_grad, grads, norm_gain_grad = unproject(info, x, grad_residual, gain_one, first, grads)
    output_grad = dot(mixed, grad_low, 0, 0).astype(low)
    qkv_grad = dot(normed, grads, 0, 0).astype(low)

    own_sums = table_sums(diagonals.reshape(own_heads, 2 * seq_len), buckets, seq_len)
    sums = lax.dynamic_update_slice_in_dim(jnp.zeros((buckets, heads), jnp.float32), own_sums, c * own_heads, 1)
    sums = jnp.zeros((n_fsdp, shard, small), jnp.float32).at[:, 0, :].set(sums.reshape(n_fsdp, small)).reshape(n_fsdp * shard, small)
    side = jnp.concatenate([norm_gain_grad.reshape(-1, 1), ffn_gain_grad.reshape(-1, 1), sums, jnp.zeros((n_fsdp * shard, 126 - small), jnp.float32)], axis=1)
    second = jnp.concatenate([output_grad, side.astype(low)], axis=1)
    if remote:
        second, qkv_grad = scatter_all([second, qkv_grad], 2)
    else:
        second, qkv_grad = scatter_rows(second), scatter_rows(qkv_grad)

    full = jnp.float32
    second = second.astype(full)
    qkv_grad = qkv_grad.astype(full)
    feed_grad = feed_grad.astype(full)
    inner_grad = feed_grad[:, :hidden_width].reshape(shard, slabs, n_fsdp, shard).transpose(0, 2, 1, 3).reshape(shard, hidden_width)
    outer_grad = feed_grad[:, hidden_width:].reshape(shard, slabs, width).transpose(1, 0, 2).reshape(slabs * shard, width)
    table_grad = second[0, width + 2 : width + 2 + small].reshape(bias_table.shape)
    return (layer_out.reshape(tokens.shape), token_grad.reshape(tokens.shape), second[:, width], qkv_grad[:, :width], qkv_grad[:, width : 2 * width],
            qkv_grad[:, 2 * width :], second[:, :width], second[:, width + 1], inner_grad, outer_grad, table_grad)


def solution(mesh):
    rows = P("fsdp", "ctx", None)
    in_specs = (rows, rows, P("fsdp"), P("fsdp"), P("fsdp", None), P("fsdp", None), P("fsdp", None), P("fsdp", None),
                P("fsdp"), P("fsdp", None), P("fsdp", None), P("fsdp", None))
    out_specs = (rows, rows, P("fsdp"), P("fsdp", None), P("fsdp", None), P("fsdp", None), P("fsdp", None),
                 P("fsdp"), P("fsdp", None), P("fsdp", None), P("fsdp", None))
    return jax.shard_map(per_device, mesh=mesh, in_specs=in_specs, out_specs=out_specs, check_vma=False)
```

time: 869 us -> 596 us (0.69)
  Pallas kernels: 137 us -> 442 us
  waiting for transfers between devices: 307 us -> 7.82 us
  matrix products: 267 us -> 78.3 us
  other arithmetic: 76.7 us -> 12 us
  local copies, waits for them, and re-layouts: 53.8 us -> 35.1 us
    pallas_call x0 -> x5, Pallas kernels: none -> 302 us  [the longest x1 102 us: feed(): pl.pallas_call(functools.partial(feed_kernel, parts=parts, block=block),...]
    reduce_scatter x3 -> x1, waiting for transfers between devices: 236 us -> 0.02 us  [scatter_rows(): lax.psum_scatter(grad, ('fsdp', 'ctx'), scatter_dimension=0, tiled=True)]
    dot_general x12 -> x7, matrix products: 264 us -> 75.3 us  [dot(): lax.dot_general(a, b, (((ca,), (cb,)), ((), ())), precision=precision, pr...]
    all_gather x3 -> x1, waiting for transfers between devices: 68 us -> 0.01 us  [gather_rows(): return lax.all_gather(mine, ('fsdp', 'ctx'), axis=0, tiled=True)]
    add x2 -> x0, other arithmetic: 19 us -> none  [the longest x1 11.9 us: per_device(): token_grad = (grad_residual + down).reshape(seqs, block, width)]
    dynamic_slice x10 -> x0, local copies, waits for them, and re-layouts: 18.6 us -> none  [the longest x4 9.26 us: to_heads(): came = swap(lax.dynamic_slice_in_dim(x, (1 - c) * width, width, 2))]
    concatenate x8 -> x2, other arithmetic: 19.4 us -> 1.42 us  [the longest x1 0.84 us: per_device(): w_feed = gather_rows(jnp.concatenate([inner, outer], axis=1))]
    select_n x4 -> x0, other arithmetic: 9.43 us -> none  [the longest x3 8.47 us: to_heads(): jnp.where(c == 0, kept, came)]
  transfers between devices with their start and end apart: 17 -> 7, of which waited for: 6 -> 2; matrix products, arithmetic and copies ran while one was open for 44% -> 12% of each run, Pallas kernels for 16% -> 57%
where the time goes in v2:
time: 596 us; the launch traced here: 591 us
  Pallas kernels  442 us (74%)
  matrix products  78.3 us (13%)
  local copies, waits for them, and re-layouts  35.1 us (6%)
  between operations  14.9 us (2%)
  other arithmetic  12 us (2%)
  waiting for transfers between devices  7.82 us (1%)
    pallas_call x1, Pallas kernels, feed(): pl.pallas_call(functools.partial(feed_kernel, parts=parts, block=block),...  102 us
    pallas_call x1, Pallas kernels, scatter_all(): pl.pallas_call(functools.partial(scatter_kernel, count=count), in_specs=[...  93.8 us
    pallas_call x1, Pallas kernels, unattend(): pl.pallas_call(functools.partial(unattend_kernel, seq_len=seq_len, head_d...  82.7 us
    dot_general x7, matrix products, dot(): lax.dot_general(a, b, (((ca,), (cb,)), ((), ())), precision=precision, pr...  75.3 us
    pallas_call x1, Pallas kernels, gather_all(): pl.pallas_call(functools.partial(gather_kernel, count=count), in_specs=[a...  59.9 us
    pallas_call x1, Pallas kernels, attend(): pl.pallas_call(functools.partial(attend_kernel, seq_len=seq_len, head_dim...  57 us
    pallas_call x1, Pallas kernels, unproject(): pl.pallas_call(functools.partial(unproject_kernel, parts=parts), grid_spe...  25.5 us
    pallas_call x1, Pallas kernels, project(): pl.pallas_call(functools.partial(project_kernel, parts=parts), grid_spec=...  20.3 us
  transfers between devices with their start and end apart: 7, of which 2 were waited for; matrix products, arithmetic and copies ran while one was open for 12% of the time, Pallas kernels for 57%

profile of v2, /device:TPU:0, one launch (start us, length us, event | category | flops | bytes accessed | tf_op | source)
XLA Modules:
  0.0 590.9 jit_solution(11879661814572509803)
XLA Ops:
  7.2 2.6 reshape.291
  10.2 0.8 reshape.292
  11.6 0.8 fusion.22
  13.0 0.9 concatenate.40.refs_0_
  13.8 59.9 %gather_rows.1 = (bf16[4,2,2,2,32,3200]{5,4,3,2,1,0:T(8,128)(2,1)}, bf16[4,2,2,2,32,1024]{5,4,3,2,1,0:T(8,128)(2,1)}) custom-call(bf16[2,32,3200]{2,1,0:T(8,128)(2,1)} %concatenate.40.refs_0_, bf16[2,32,1024]{2,1,0:T(8,128)(2,1)} %bitcast.76), custom_call_target="tpu_custom_call" | custom-call | tf_op jit(solution)/shard_map/gather_rows/pallas_call | solution.py:388
  73.8 0.6 pad_add_fusion.info_ref
  74.3 2.0 convert_reduce_fusion
  76.3 20.3 %project.1 = (bf16[2048,1024]{1,0:T(8,128)(2,1)}, bf16[3,2048,512]{2,1,0:T(8,128)(2,1)}, bf16[3,2048,512]{2,1,0:T(8,128)(2,1)}) custom-call(s32[5]{0:T(128)} %pad_add_fusion.info_ref, bf16[2048,1024]{1,0:T(8,128)(2,1)} %bitcast.85, f32[1,1024]{1,0:T(1,128)} %bitcast.81, bf16[1024,3200]{1,0:T(8,128)(2,1)} %bitcast.78), custom_call_target="tpu_custom_call" | custom-call | flops 12884901888 | bytes 27262976 | tf_op jit(solution)/shard_map/project/pallas_call | solution.py:570
  96.6 1.0 slice.90
  98.0 0.6 select_add_fusion
  98.6 0.8 fusion.19
  99.4 0.7 reshape.296.tvec_ref
  100.1 7.4 %collective-permute-done.refs_1_ = bf16[3,4,512,512]{3,2,1,0:T(8,128)(2,1)} collective-permute-done((bf16[3,4,512,512]{3,2,1,0:T(8,128)(2,1)}, bf16[3,4,512,512]{3,2,1,0:T(8,128)(2,1)}, u32[]{:S(2)}, u32[]{:S(2)}) %collective-permute-start) | collective-permute-done | bytes 6291488 | tf_op jit(solution)/shard_map/ppermute | solution.py:722
  107.5 57.0 %attend.1 = (bf16[4,512,512]{2,1,0:T(8,128)(2,1)}, bf16[4,512,512]{2,1,0:T(8,128)(2,1)}, f32[4,4,2,1024]{3,2,1,0:T(2,128)}) custom-call(s32[5]{0:T(128)} %pad_add_fusion.info_ref, f32[4,2,2048]{2,1,0:T(2,128)} %reshape.296.tvec_ref, bf16[3,4,512,512]{3,2,1,0:T(8,128)(2,1)} %bitcast.91, bf16[3,4,512,512]{3,2,1,0:T(8,128)(2,1)} %collective-permute-done.refs_1_), custom_call_target="tpu_custom_call" | custom-call | flops 34359738368 | bytes 16777216 | tf_op jit(solution)/shard_map/attend/pallas_call | solution.py:99
  164.8 3.8 broadcast_select_fusion
  169.0 1.3 copy-done.16
  170.3 102.5 %feed.1 = (bf16[2048,1024]{1,0:T(8,128)(2,1)}, bf16[2048,1024]{1,0:T(8,128)(2,1)}, bf16[2048,4096]{1,0:T(8,128)(2,1)}, bf16[2048,1024]{1,0:T(8,128)(2,1)}, bf16[...) custom-call(s32[5]{0:T(128)} %pad_add_fusion.info_ref, ...), custom_call_target="tpu_custom_call" | custom-call | flops 77309411328 | bytes 88080384 | tf_op jit(solution)/shard_map/feed/pallas_call | solution.py:646
  272.8 23.9 %convert_dynamic-update-slice_fusion = bf16[1024,8192]{1,0:T(8,128)(2,1)} fusion(bf16[2048,1024]{1,0:T(8,128)(2,1)} %get-tuple-element.60, bf16[2048,4096]{1,0:T(8,128)(2,1)} %get-tuple-element.61), kind=kOutput, calls=%fused_computation | convolution fusion | flops 17184063488 | bytes 29360128 | tf_op jit(solution)/shard_map/dot_general | solution.py:26
  296.7 5.8 convert_dynamic-update-slice_fusion.4
  302.5 5.8 convert_dynamic-update-slice_fusion.3
  308.4 5.7 convert_dynamic-update-slice_fusion.2
  314.1 5.8 convert_dynamic-update-slice_fusion.1
  320.0 1.3 copy-done.15
  321.3 0.8 fusion.17
  322.1 0.7 reshape.302.tvec_ref
  322.8 82.7 %unattend.1 = (bf16[3,4,512,512]{3,2,1,0:T(8,128)(2,1)}, bf16[3,4,512,512]{3,2,1,0:T(8,128)(2,1)}, f32[4,2,2048]{2,1,0:T(2,128)}) custom-call(s32[5]{0:T(128)} %pad_add_fusion.info_ref, f32[4,2,2048]{2,1,0:T(2,128)} %reshape.302.tvec_ref, bf16[3,4,512,512]{3,2,1,0:T(8,128)(2,1)} %bitcast.92, bf16[3,4,512,512]{3,2,1,0:T(8,128)(2,1)} %collective-permute-done.refs_1_, ...), custom_call_target="tpu_custom_call" | custom-call | flops 85899345920 | bytes 33554432 | tf_op jit(solution)/shard_map/unattend/pallas_call | solution.py:216
  405.5 0.4 collective-permute-start.3
  406.0 9.4 %convolution_convert_fusion.1 = bf16[1024,1024]{0,1:T(8,128)(2,1)} fusion(bf16[2048,1024]{1,0:T(8,128)(2,1)} %get-tuple-element.71, bf16[2048,1024]{1,0:T(8,128)(2,1)} %get-tuple-element.72), kind=kOutput, calls=%fused_computation.15 | convolution fusion | flops 4296015872 | bytes 10485760 | tf_op jit(solution)/shard_map/dot_general | solution.py:26
  415.4 1.3 fusion.20
  417.4 25.5 %unproject.1 = (f32[2048,1024]{1,0:T(8,128)}, bf16[2048,3072]{1,0:T(8,128)(2,1)}, f32[1,1024]{1,0:T(1,128)}) custom-call(s32[5]{0:T(128)} %pad_add_fusion.info_ref, bf16[2048,1024]{1,0:T(8,128)(2,1)} %bitcast.87, f32[2048,1024]{1,0:T(8,128)} %get-tuple-element.59.residual_ref, f32[1,1024]{1,0:T(1,128)} %bitcast.82, bf16[1024,3200]{1,0:T(8,128)(2,1)} %bitcast.80, ...), custom_call_target="tpu_custom_call" | custom-call | flops 12884901888 | bytes 52428800 | tf_op jit(solution)/shard_map/unproject/pallas_call | solution.py:691
  442.9 0.7 convert_bitcast_fusion.1
  443.6 8.1 %concatenate.43 = bf16[1024,1152]{0,1:T(8,128)(2,1)S(1)} concatenate(bf16[1024,1024]{0,1:T(8,128)(2,1)} %convolution_convert_fusion.1, bf16[1024,1]{0,1:T(2,128)(2,1)S(1)} %convert_bitcast_fusion.1, bf16[1024,1]{0,1:T(2,128)(2,1)S(1)} %convert_bitcast_fusion, bf16[1024,32]{0,1:T(8,128)(2,1)S(1)} %reshape.313, bf16[1024,94]{0,1:T(8,128)(2,1)S(1)} %broadcast_in_dim.31), dimensions={1} | concatenate | bytes 4718592 | tf_op jit(solution)/shard_map/concatenate | solution.py:803
  451.6 2.5 copy.60
  454.1 19.0 %convolution_convert_fusion = bf16[1024,3072]{1,0:T(8,128)(2,1)} fusion(bf16[2048,1024]{1,0:T(8,128)(2,1)} %get-tuple-element.76, bf16[2048,3072]{1,0:T(8,128)(2,1)} %get-tuple-element.77), kind=kOutput, calls=%fused_computation.1 | convolution fusion | flops 12888047616 | bytes 23068672 | tf_op jit(solution)/shard_map/dot_general | solution.py:26
  473.1 93.8 %scatter_rows.1 = (bf16[2,32,1152]{2,1,0:T(8,128)(2,1)}, bf16[2,32,3072]{2,1,0:T(8,128)(2,1)}) custom-call(bf16[4,2,2,2,32,1152]{5,4,3,2,1,0:T(8,128)(2,1)} %bitcast.59, bf16[4,2,2,2,32,3072]{5,4,3,2,1,0:T(8,128)(2,1)} %bitcast.61), custom_call_target="tpu_custom_call" | custom-call | tf_op jit(solution)/shard_map/scatter_rows/pallas_call | solution.py:499
  567.0 1.0 bitcast_convert_fusion
  568.2 0.9 bitcast_convert_fusion.1
  569.2 0.7 slice.96
  570.0 0.6 reshape_squeeze.3
  570.6 0.7 slice_reduce_fusion
  571.3 0.9 fusion.42
  572.2 1.1 broadcast_select_fusion.2
  573.5 1.1 fusion.41
  574.6 0.8 reshape.316
  575.5 2.3 copy.61
  577.8 3.5 reshape.317
  581.3 0.7 reshape.318
  582.0 1.6 copy.62
  (77 shorter events, 3.6 us)
Async XLA Ops:
  7.2 3.8 copy-start.2
  7.2 161.8 %all-gather.2.cloned.1.call-start = ((), (), s32[]{:S(2)}) async-start(), calls=%async_computation.1 | async-start | bytes 17301504 | tf_op jit(solution)/shard_map/all_gather | solution.py:708
  9.8 2.7 copy-start.17
  9.9 2.8 copy-start.12
  9.9 2.9 copy-start.13
  9.9 3.1 copy-start.3
  9.9 3.1 copy-start.4
  9.9 3.1 copy-start.5
  9.9 63.8 %copy-start.14 = (s32[4]{0:T(128)S(1)}, s32[4]{0:T(128)}, u32[]{:S(2)}) copy-start(s32[4]{0:T(128)} %param.19) | copy-start | bytes 52
  12.5 555.6 %reduce-scatter.2.cloned.1.call-start = ((), (), s32[]{:S(2)}) async-start(), calls=%async_computation.2 | async-start | bytes 17301504 | tf_op jit(solution)/shard_map/reduce_scatter | solution.py:712
  76.3 21.5 %copy-start.11 = (s32[15]{0:T(128)S(1)}, s32[15]{0:T(128)}, u32[]{:S(2)}) copy-start(s32[15]{0:T(128)} %constant.78.clone) | copy-start | bytes 184
  96.6 10.9 %collective-permute-start = (bf16[3,4,512,512]{3,2,1,0:T(8,128)(2,1)}, bf16[3,4,512,512]{3,2,1,0:T(8,128)(2,1)}, u32[]{:S(2)}, u32[]{:S(2)}) collective-permute-start(bf16[3,4,512,512]{3,2,1,0:T(8,128)(2,1)} %bitcast.84), channel_id=1, source_target_pairs={{0,16},{16,0},{1,17},{17,1},{2,18},{18,2},{3,19},{19,3},{4,20},{20... | collective-permute-start | bytes 18874376 | tf_op jit(solution)/shard_map/ppermute | solution.py:722
  97.8 66.7 %copy-start.7 = (bf16[32,16]{1,0:T(8,128)(2,1)}, bf16[32,16]{1,0:T(8,128)(2,1)S(1)}, u32[]{:S(2)}) copy-start(bf16[32,16]{1,0:T(8,128)(2,1)S(1)} %reshape.295) | copy-start | bytes 3076
  164.6 4.4 collective-permute-start.1
  169.0 1.3 copy-start.16
  272.8 23.9 %copy-start = (bf16[4,512,1024]{2,1,0:T(8,128)(2,1)S(1)}, bf16[4,512,1024]{2,1,0:T(8,128)(2,1)}, u32[]{:S(2)}) copy-start(bf16[4,512,1024]{2,1,0:T(8,128)(2,1)} %broadcast_select_fusion) | copy-start | bytes 12582916
  272.8 23.9 %copy-start.18 = (bf16[2048,4096]{1,0:T(8,128)(2,1)S(1)}, bf16[2048,4096]{1,0:T(8,128)(2,1)}, u32[]{:S(2)}) copy-start(bf16[2048,4096]{1,0:T(8,128)(2,1)} %get-tuple-element.62) | copy-start | bytes 50331652
  308.3 11.6 %collective-permute-start.2 = (bf16[4,512,512]{2,1,0:T(8,128)(2,1)}, bf16[4,512,512]{2,1,0:T(8,128)(2,1)S(1)}, u32[]{:S(2)}, u32[]{:S(2)}) collective-permute-start(bf16[4,512,512]{2,1,0:T(8,128)(2,1)} %bitcast.19), channel_id=1, source_target_pairs={{0,16},{16,0},{1,17},{17,1},{2,18},{18,2},{3,19},{19,3},{4,20},{20... | collective-permute-start | bytes 6291464 | tf_op jit(solution)/shard_map/ppermute | solution.py:722
  319.9 1.4 copy-start.15
  319.9 1.4 copy-start.8
  319.9 1.4 copy-start.9
  322.8 83.1 %copy-start.10 = (f32[1,1024]{1,0:T(1,128)S(1)}, f32[1,1024]{1,0:T(1,128)}, u32[]{:S(2)}) copy-start(f32[1,1024]{1,0:T(1,128)} %get-tuple-element.74) | copy-start | bytes 12292
  405.5 11.9 %collective-permute-start.3 = (bf16[3,4,512,512]{3,2,1,0:T(8,128)(2,1)}, bf16[3,4,512,512]{3,2,1,0:T(8,128)(2,1)}, u32[]{:S(2)}, u32[]{:S(2)}) collective-permute-start(bf16[3,4,512,512]{3,2,1,0:T(8,128)(2,1)} %get-tuple-element.69), channel_id=1, source_target_pairs={{0,16},{16,0},{1,17},{17,1},{2,18},{18,2},{3,19},{19,3},{4,20},{20... | collective-permute-start | bytes 18874376 | tf_op jit(solution)/shard_map/ppermute | solution.py:727
  406.0 9.4 %copy-start.6 = (f32[4,2,2048]{2,1,0:T(2,128)S(1)}, f32[4,2,2048]{2,1,0:T(2,128)}, u32[]{:S(2)}) copy-start(f32[4,2,2048]{2,1,0:T(2,128)} %get-tuple-element.75) | copy-start | bytes 196612
  568.1 4.2 collective-permute-start.4
  575.5 5.9 copy-start.1
Sparse Core Ops, SparseCore 0:
  12.6 131.2 all-gather.1
  320.1 193.2 reduce-scatter.1

commit v3 on v2

--- a/solution.py
+++ b/solution.py
@@ -12,7 +12,7 @@
 LN2 = 0.6931471805599453
 NEG = -1e30
 TILE = 256
-QT = 512
+QT = 256
 HEAD_DIM = 64
 EPS = 1e-6
 GELU = 0.7978845608028654
@@ -56,7 +56,8 @@
         top = TILE * used
         kept = [lane == h for h in range(heads)]
         keys = [jnp.where(kept[h], k_ref[0:top, :], 0) for h in range(heads)]
-        values = [jnp.where(kept[h], v_ref[0:top, :], 1) for h in range(heads)]
+        ones = jnp.ones((top, 128), jnp.bfloat16)
+        values = [jnp.concatenate([jnp.where(kept[h], v_ref[0:top, :], 0), ones], axis=1) for h in range(heads)]
 
         def query_tile(a, carry):
             here = pl.ds(pl.multiple_of(a * QT, QT), QT)
@@ -70,11 +71,14 @@
                 peak = jnp.max(scores, axis=1, keepdims=True)
                 probs = jnp.exp2(scores - peak).astype(jnp.bfloat16)
                 out = dot(probs, values[h], 1, 0)
-                mass = pltpu.roll(out, head_dim, 1)
-                out = out * (1.0 / mass)
-                total = out if total is None else jnp.where(kept[h], out, total)
+                mass = out[:, 128:]
+                out = out[:, :128] * (1.0 / mass)
+                total = out if total is None else total + out
                 lse = peak + jnp.log2(mass)
-                lse_ref[0, 0, h : h + 1, here] = jnp.transpose(lse)[h * head_dim : h * head_dim + 1, :]
+                both = lse if h == 0 else jnp.where(kept[h], lse, both)
+            both = jnp.transpose(both)
+            for h in range(heads):
+                lse_ref[0, 0, h : h + 1, here] = both[h * head_dim : h * head_dim + 1, :]
             o_ref[here, :] = total.astype(jnp.bfloat16)
             return carry
 
@@ -173,7 +177,7 @@
             dq_ref[here, :] = (dq_total * LN2).astype(jnp.bfloat16)
             return carry
 
-        lax.fori_loop(0, used, query_tile, 0)
+        lax.fori_loop(0, used, query_tile, 0, unroll=2)
         if used < blocks:
             dq_ref[top:, :] = jnp.zeros((seq_len - top, q_ref.shape[-1]), jnp.bfloat16)
             dk_acc[top:, :] = jnp.zeros((seq_len - top, q_ref.shape[-1]), jnp.float32)
@@ -565,7 +569,7 @@
 
 def project(info, x, gain, w, parts):
     rows, width = x.shape
-    tile = min(512, rows)
+    tile = min(256, rows)
     share = width // parts
     return pl.pallas_call(
         functools.partial(project_kernel, parts=parts),
@@ -582,9 +586,9 @@
 
 def feed_kernel(info_ref, x_ref, cot_ref, gain_ref, wo_ref, w_ref, *refs, parts, block):
     mixed = refs[:parts]
-    mixed_ref, normed_ref, hidden_ref, layer_ref, inner_ref, residual_ref, low_ref, gain_grad_ref = refs[parts : parts + 8]
-    grads = refs[parts + 8 : 2 * parts + 8]
-    slope_ref = refs[2 * parts + 8]
+    mixed_ref, normed_ref, hidden_ref, layer_ref, grad_ref, inner_ref, residual_ref, low_ref, gain_grad_ref = refs[parts : parts + 9]
+    grads = refs[parts + 9 : 2 * parts + 9]
+    slope_ref = refs[2 * parts + 9]
     c = info_ref[0]
     tile, width = x_ref.shape
     share = width // parts
@@ -614,6 +618,7 @@
     start = pl.program_id(0) * tile
     position = c * block + lax.rem(start, block) + lax.broadcasted_iota(jnp.int32, (tile, 1), 0)
     grad = jnp.where(position < info_ref[1 + start // block], cot_ref[...], 0)
+    grad_ref[...] = grad
     up = None
     for k in range(0, hidden_width, chunk):
         inner = (dot(grad, w_ref[:, hidden_width + k : hidden_width + k + chunk], 1, 1) * slope_ref[:, k : k + chunk].astype(jnp.float32)).astype(low)
@@ -648,9 +653,9 @@
         grid_spec=pltpu.PrefetchScalarGridSpec(
             num_scalar_prefetch=1, grid=(rows // tile,),
             in_specs=[t(width), t(width), resident((1, width)), resident(wo.shape), resident(w.shape)] + [t(share)] * parts,
-            out_specs=[t(width), t(width), t(hidden), t(width), t(hidden), t(width), t(width), resident((1, width))] + [t(share)] * parts,
+            out_specs=[t(width), t(width), t(hidden), t(width), t(width), t(hidden), t(width), t(width), resident((1, width))] + [t(share)] * parts,
             scratch_shapes=[pltpu.VMEM((tile, hidden), jnp.bfloat16)]),
-        out_shape=[low(width), low(width), low(hidden), low(width), low(hidden), jax.ShapeDtypeStruct((rows, width), jnp.float32), low(width),
+        out_shape=[low(width), low(width), low(hidden), low(width), low(width), low(hidden), jax.ShapeDtypeStruct((rows, width), jnp.float32), low(width),
                    jax.ShapeDtypeStruct((1, width), jnp.float32)] + [low(share)] * parts,
         compiler_params=params(),
         cost_estimate=cost(rows * width * (8 * hidden + 4 * width), rows * (18 * width + 4 * hidden) + 4 * width * hidden),
@@ -686,7 +691,7 @@
 def unproject(info, x, residual, gain, w, came):
     parts = len(came)
     rows, width = x.shape
-    tile = min(512, rows)
+    tile = min(256, rows)
     share = width // parts
     return pl.pallas_call(
         functools.partial(unproject_kernel, parts=parts),
@@ -701,6 +706,60 @@
     )(info, x, residual, gain, w, *came)
 
 
+def weigh_kernel(mixed_ref, low_ref, normed_ref, grad_ref, inner_ref, hidden_ref, out_ref, made_ref, came_ref, send, recv, *, slabs):
+    s = pl.program_id(0)
+    c = lax.axis_index("ctx")
+    other = {"ctx": 1 - c}
+    total = 2 * slabs + 1
+
+    def copy(k):
+        return pltpu.make_async_remote_copy(src_ref=made_ref.at[lax.rem(k, 2), :, 1 - c], dst_ref=came_ref.at[k], send_sem=send.at[k], recv_sem=recv.at[k],
+                                            device_id=other, device_id_type=pl.DeviceIdType.MESH)
+
+    @pl.when(s == 0)
+    def _():
+        barrier = pltpu.get_barrier_semaphore()
+        pl.semaphore_signal(barrier, inc=1, device_id=other, device_id_type=pl.DeviceIdType.MESH)
+        pl.semaphore_wait(barrier, 1)
+
+    def make(left, right):
+        slab = dot(left[...], right[...], 0, 0).astype(jnp.bfloat16)
+        made_ref[lax.rem(s, 2)] = slab.reshape(made_ref.shape[1:])
+        copy(s).start()
+
+    pl.when(s == 0)(lambda: make(mixed_ref, low_ref))
+    pl.when((s > 0) & (s <= slabs))(lambda: make(normed_ref, inner_ref))
+    pl.when((s > slabs) & (s < total))(lambda: make(hidden_ref, grad_ref))
+
+    @pl.when(s > 0)
+    def _():
+        earlier = copy(s - 1)
+        earlier.wait_recv()
+        out_ref[...] = made_ref[lax.rem(s - 1, 2), :, c] + came_ref[s - 1]
+        earlier.wait_send()
+
+
+def weigh(mixed, low, normed, grad, inner, hidden, chips, collective_id):
+    rows, width = mixed.shape
+    slabs = hidden.shape[1] // width
+    total = 2 * slabs + 1
+    part = width // chips // 2
+    whole = pl.BlockSpec((rows, width), lambda s: (0, 0), pipeline_mode=pl.Buffered(1))
+    slab = lambda first: pl.BlockSpec((rows, width), lambda s: (0, jnp.clip(s - first, 0, slabs - 1)))
+    return pl.pallas_call(
+        functools.partial(weigh_kernel, slabs=slabs),
+        grid=(total + 1,),
+        in_specs=[whole, whole, whole, whole, slab(1), slab(1 + slabs)],
+        out_specs=pl.BlockSpec((chips, part, width), lambda s: (0, 0, jnp.maximum(s - 1, 0))),
+        out_shape=jax.ShapeDtypeStruct((chips, part, total * width), jnp.bfloat16),
+        scratch_shapes=[pltpu.VMEM((2, chips, 2, part, width), jnp.bfloat16), pltpu.VMEM((total, chips, part, width), jnp.bfloat16),
+                        pltpu.SemaphoreType.DMA((total,)), pltpu.SemaphoreType.DMA((total,))],
+        compiler_params=pltpu.CompilerParams(collective_id=collective_id, has_side_effects=True, vmem_limit_bytes=VMEM_LIMIT),
+        cost_estimate=cost(2 * rows * width * width * total, 2 * rows * width * 13),
+        name="weigh",
+    )(mixed, low, normed, grad, inner, hidden)
+
+
 def gather_rows(shard):
     n = lax.axis_size("ctx")
     part = shard.shape[0] // n
@@ -710,8 +769,10 @@
 
 def scatter_rows(grad):
     part = lax.psum_scatter(grad, ("fsdp", "ctx"), scatter_dimension=0, tiled=True)
-    if lax.axis_size("ctx") != 2:
-        return lax.all_gather(part, "ctx", axis=0, tiled=True)
+    return lax.all_gather(part, "ctx", axis=0, tiled=True)
+
+
+def both_halves(part):
     other = lax.ppermute(part, "ctx", [(0, 1), (1, 0)])
     first = lax.axis_index("ctx") == 0
     return jnp.concatenate([jnp.where(first, part, other), jnp.where(first, other, part)], axis=0)
@@ -725,6 +786,10 @@
 def give_back(pieces):
     n = len(pieces)
     return [pieces[0]] + [lax.ppermute(pieces[j], "ctx", [(i, (i - j) % n) for i in range(n)]) for j in range(1, n)]
+
+
+def wide(x):
+    return jnp.pad(x, [(0, 0)] * (x.ndim - 1) + [(0, 128 - x.shape[-1])])
 
 
 def by_chip(shape):
@@ -756,17 +821,17 @@
     inner = inner_weight.reshape(shard, n_fsdp, slabs, shard).transpose(0, 2, 1, 3).reshape(shard, hidden_width)
     outer = outer_weight.reshape(slabs, shard, width).transpose(1, 0, 2).reshape(shard, slabs * width)
     w_feed = gather_rows(jnp.concatenate([inner, outer], axis=1))
-    side = jnp.concatenate([norm_gain[:, None], ffn_gain[:, None], jnp.broadcast_to(bias_table.reshape(1, small), (shard, small)),
-                            jnp.zeros((shard, 126 - small), low)], axis=1)
+    side = jnp.stack([wide(norm_gain), wide(ffn_gain), wide(bias_table.reshape(small))])
+    side = jnp.pad(side, ((0, shard - 3), (0, 0)))
     first = jnp.concatenate([query_weight, key_weight, value_weight, side], axis=1)
     if remote:
         first, w_output = gather_all([first, output_weight], 1)
     else:
         first, w_output = gather_rows(first), gather_rows(output_weight)
-    side = first[:, 3 * width :]
-    gain_one = side[:, 0].astype(jnp.float32)[None, :]
-    gain_two = side[:, 1].astype(jnp.float32)[None, :]
-    table = side[::shard, 2 : 2 + small].reshape(buckets, heads)
+    side = first[:, 3 * width :].reshape(n_fsdp, shard, 128)
+    gain_one = side[:, 0, :shard].reshape(1, width).astype(jnp.float32)
+    gain_two = side[:, 1, :shard].reshape(1, width).astype(jnp.float32)
+    table = side[:, 2, :small].reshape(buckets, heads)
     own_table = lax.dynamic_slice_in_dim(table, c * own_heads, own_heads, 1)
     vector_q = bias_vectors(own_table, seq_len, QT).reshape(pairs, per_pair, 2 * seq_len)
     vector_k = bias_vectors(own_table, seq_len, TILE).reshape(pairs, per_pair, 2 * seq_len)
@@ -777,44 +842,42 @@
     qkv = exchange([p.reshape(3, seqs, block, share) for p in qkv])
     *out, lse = attend(info, vector_q, qkv, HEAD_DIM)
     mixed = [m.reshape(rows, share) for m in give_back(out)]
-    (mixed, normed_ffn, hidden, layer_out, grad_inner, grad_residual, grad_low, ffn_gain_grad, *grad_mixed) = feed(
+    (mixed, normed_ffn, hidden, layer_out, grad_out, grad_inner, grad_residual, grad_low, ffn_gain_grad, *grad_mixed) = feed(
         info, x, cot, gain_two, w_output, w_feed, mixed, block)
     grad_mixed = exchange([g.reshape(seqs, block, share) for g in grad_mixed])
 
-    position = c * block + jnp.arange(block, dtype=jnp.int32)
-    live = (position[None, :] < lengths[:, None])[:, :, None]
-    grad_out = jnp.where(live, cotangent, 0).reshape(rows, width)
-    inner_grad = dot(normed_ffn, grad_inner, 0, 0).astype(low)
-    outer_grad = [dot(hidden[:, q * width : (q + 1) * width], grad_out, 0, 0).astype(low) for q in range(slabs)]
-    feed_grad = jnp.concatenate([inner_grad] + outer_grad, axis=1)
-    feed_grad, grad_mixed = lax.optimization_barrier((feed_grad, grad_mixed))
-    feed_grad = scatter_rows(feed_grad)
+    if remote:
+        feed_grad = weigh(mixed, grad_low, normed_ffn, grad_out, grad_inner, hidden, n_fsdp, 3)
+        feed_grad, grad_mixed = lax.optimization_barrier((feed_grad, grad_mixed))
+        feed_grad = lax.psum_scatter(feed_grad, "fsdp", scatter_dimension=0, tiled=False)
+        feed_grad = both_halves(feed_grad)
+    else:
+        outer_grad = [dot(hidden[:, q * width : (q + 1) * width], grad_out, 0, 0) for q in range(slabs)]
+        feed_grad = jnp.concatenate([dot(mixed, grad_low, 0, 0), dot(normed_ffn, grad_inner, 0, 0)] + outer_grad, axis=1).astype(low)
+        feed_grad = scatter_rows(feed_grad)
 
     *grads, diagonals = unattend(info, vector_k, qkv, out, grad_mixed, lse, HEAD_DIM)
     grads = [g.reshape(3, rows, share) for g in give_back(grads)]
     token_grad, grads, norm_gain_grad = unproject(info, x, grad_residual, gain_one, first, grads)
-    output_grad = dot(mixed, grad_low, 0, 0).astype(low)
     qkv_grad = dot(normed, grads, 0, 0).astype(low)
 
     own_sums = table_sums(diagonals.reshape(own_heads, 2 * seq_len), buckets, seq_len)
     sums = lax.dynamic_update_slice_in_dim(jnp.zeros((buckets, heads), jnp.float32), own_sums, c * own_heads, 1)
-    sums = jnp.zeros((n_fsdp, shard, small), jnp.float32).at[:, 0, :].set(sums.reshape(n_fsdp, small)).reshape(n_fsdp * shard, small)
-    side = jnp.concatenate([norm_gain_grad.reshape(-1, 1), ffn_gain_grad.reshape(-1, 1), sums, jnp.zeros((n_fsdp * shard, 126 - small), jnp.float32)], axis=1)
-    second = jnp.concatenate([output_grad, side.astype(low)], axis=1)
+    side = jnp.stack([wide(norm_gain_grad.reshape(n_fsdp, shard)), wide(ffn_gain_grad.reshape(n_fsdp, shard)), wide(sums.reshape(n_fsdp, small))], axis=1)
+    side = jnp.pad(side.astype(low), ((0, 0), (0, shard - 3), (0, 0))).reshape(n_fsdp * shard, 128)
     if remote:
-        second, qkv_grad = scatter_all([second, qkv_grad], 2)
+        side, qkv_grad = scatter_all([side, qkv_grad], 2)
     else:
-        second, qkv_grad = scatter_rows(second), scatter_rows(qkv_grad)
+        side, qkv_grad = scatter_rows(side), scatter_rows(qkv_grad)
 
     full = jnp.float32
-    second = second.astype(full)
+    side = side.astype(full)
     qkv_grad = qkv_grad.astype(full)
     feed_grad = feed_grad.astype(full)
-    inner_grad = feed_grad[:, :hidden_width].reshape(shard, slabs, n_fsdp, shard).transpose(0, 2, 1, 3).reshape(shard, hidden_width)
-    outer_grad = feed_grad[:, hidden_width:].reshape(shard, slabs, width).transpose(1, 0, 2).reshape(slabs * shard, width)
-    table_grad = second[0, width + 2 : width + 2 + small].reshape(bias_table.shape)
-    return (layer_out.reshape(tokens.shape), token_grad.reshape(tokens.shape), second[:, width], qkv_grad[:, :width], qkv_grad[:, width : 2 * width],
-            qkv_grad[:, 2 * width :], second[:, :width], second[:, width + 1], inner_grad, outer_grad, table_grad)
+    inner_grad = feed_grad[:, width : width + hidden_width].reshape(shard, slabs, n_fsdp, shard).transpose(0, 2, 1, 3).reshape(shard, hidden_width)
+    outer_grad = feed_grad[:, width + hidden_width :].reshape(shard, slabs, width).transpose(1, 0, 2).reshape(slabs * shard, width)
+    return (layer_out.reshape(tokens.shape), token_grad.reshape(tokens.shape), side[0, :shard], qkv_grad[:, :width], qkv_grad[:, width : 2 * width],
+            qkv_grad[:, 2 * width :], feed_grad[:, :width], side[1, :shard], inner_grad, outer_grad, side[2, :small].reshape(bias_table.shape))
 
 
 def solution(mesh):

time: 596 us -> 547 us (0.918)
  matrix products: 78.3 us -> 20.8 us
  Pallas kernels: 442 us -> 455 us
  waiting for transfers between devices: 7.82 us -> 19.5 us
  local copies, waits for them, and re-layouts: 35.1 us -> 25 us
    dot_general x7 -> x1, matrix products: 75.3 us -> 18.6 us  [dot(): lax.dot_general(a, b, (((ca,), (cb,)), ((), ())), precision=precision, pr...]
    pallas_call x0 -> x1, Pallas kernels: none -> 54.7 us  [weigh(): pl.pallas_call(functools.partial(weigh_kernel, slabs=slabs), grid=(total...]
    pallas_call x1, Pallas kernels: 57 us -> 41.4 us  [attend(): pl.pallas_call(functools.partial(attend_kernel, seq_len=seq_len, head_dim...]
    pallas_call x1, Pallas kernels: 93.8 us -> 79.9 us  [scatter_all(): pl.pallas_call(functools.partial(scatter_kernel, count=count), in_specs=[...]
    pallas_call x1, Pallas kernels: 82.7 us -> 70.1 us  [unattend(): pl.pallas_call(functools.partial(unattend_kernel, seq_len=seq_len, head_d...]
    concatenate x5 -> x0, local copies, waits for them, and re-layouts: 11.7 us -> none  [the longest x2 10.5 us: per_device(): second = jnp.concatenate([output_grad, side.astype(low)], axis=1)]
    ppermute x2, waiting for transfers between devices: 0.37 us -> 11.3 us  [give_back(): lax.ppermute(pieces[j], 'ctx', [(i, (i - j) % n) for i in range(n)])]
  transfers between devices with their start and end apart: 7 -> 7, of which waited for: 2 -> 3; matrix products, arithmetic and copies ran while one was open for 12% -> 6% of each run, Pallas kernels for 57% -> 65%
where the time goes in v3:
time: 547 us; the launch traced here: 544 us
  Pallas kernels  455 us (83%)
  local copies, waits for them, and re-layouts  25 us (5%)
  matrix products  20.8 us (4%)
  waiting for transfers between devices  19.5 us (4%)
  between operations  14.6 us (3%)
  other arithmetic  7.94 us (1%)
    pallas_call x1, Pallas kernels, feed(): pl.pallas_call(functools.partial(feed_kernel, parts=parts, block=block),...  103 us
    pallas_call x1, Pallas kernels, scatter_all(): pl.pallas_call(functools.partial(scatter_kernel, count=count), in_specs=[...  79.9 us
    pallas_call x1, Pallas kernels, unattend(): pl.pallas_call(functools.partial(unattend_kernel, seq_len=seq_len, head_d...  70.1 us
    pallas_call x1, Pallas kernels, gather_all(): pl.pallas_call(functools.partial(gather_kernel, count=count), in_specs=[a...  59.6 us
    pallas_call x1, Pallas kernels, weigh(): pl.pallas_call(functools.partial(weigh_kernel, slabs=slabs), grid=(total...  54.7 us
    pallas_call x1, Pallas kernels, attend(): pl.pallas_call(functools.partial(attend_kernel, seq_len=seq_len, head_dim...  41.4 us
    pallas_call x1, Pallas kernels, unproject(): pl.pallas_call(functools.partial(unproject_kernel, parts=parts), grid_spe...  25.6 us
    pallas_call x1, Pallas kernels, project(): pl.pallas_call(functools.partial(project_kernel, parts=parts), grid_spec=...  21.1 us
  transfers between devices with their start and end apart: 7, of which 3 were waited for; matrix products, arithmetic and copies ran while one was open for 6% of the time, Pallas kernels for 65%

profile of v3, /device:TPU:0, one launch (start us, length us, event | category | flops | bytes accessed | tf_op | source)
XLA Modules:
  0.0 543.9 jit_solution(14929418454775784022)
XLA Ops:
  7.3 2.7 reshape.199
  10.0 0.3 copy.50
  10.2 0.8 reshape.200
  11.1 1.5 copy.39
  12.5 0.2 copy.48
  12.7 0.8 fusion.5
  13.8 0.8 pad_maximum_fusion.1
  14.6 59.6 %gather_rows.1 = (bf16[4,2,2,2,32,3200]{5,4,3,2,1,0:T(8,128)(2,1)}, bf16[4,2,2,2,32,1024]{5,4,3,2,1,0:T(8,128)(2,1)}) custom-call(bf16[2,32,3200]{2,1,0:T(8,128)(2,1)} %bitcast.68, bf16[2,32,1024]{2,1,0:T(8,128)(2,1)} %bitcast.75), custom_call_target="tpu_custom_call" | custom-call | tf_op jit(solution)/shard_map/gather_rows/pallas_call | solution.py:392
  74.2 1.0 slice.52
  75.2 0.7 reshape.225.gain_ref
  75.9 0.6 pad_add_fusion.info_ref
  76.5 21.1 %project.1 = (bf16[2048,1024]{1,0:T(8,128)(2,1)}, bf16[3,2048,512]{2,1,0:T(8,128)(2,1)}, bf16[3,2048,512]{2,1,0:T(8,128)(2,1)}) custom-call(s32[5]{0:T(128)} %pad_add_fusion.info_ref, bf16[2048,1024]{1,0:T(8,128)(2,1)} %bitcast.81, f32[1,1024]{1,0:T(1,128)} %reshape.225.gain_ref, bf16[1024,3200]{1,0:T(8,128)(2,1)} %bitcast.77), custom_call_target="tpu_custom_call" | custom-call | flops 12884901888 | bytes 27262976 | tf_op jit(solution)/shard_map/project/pallas_call | solution.py:574
  97.9 0.6 copy-done.4
  98.4 0.8 fusion.1
  99.3 0.7 reshape.203.tvec_ref
  100.0 8.2 %collective-permute-done.refs_1_ = bf16[3,4,512,512]{3,2,1,0:T(8,128)(2,1)} collective-permute-done((bf16[3,4,512,512]{3,2,1,0:T(8,128)(2,1)}, bf16[3,4,512,512]{3,2,1,0:T(8,128)(2,1)}, u32[]{:S(2)}, u32[]{:S(2)}) %collective-permute-start) | collective-permute-done | bytes 6291488 | tf_op jit(solution)/shard_map/ppermute | solution.py:783
  108.1 41.4 %attend.1 = (bf16[4,512,512]{2,1,0:T(8,128)(2,1)}, bf16[4,512,512]{2,1,0:T(8,128)(2,1)}, f32[4,4,2,1024]{3,2,1,0:T(2,128)}) custom-call(s32[5]{0:T(128)} %pad_add_fusion.info_ref, f32[4,2,2048]{2,1,0:T(2,128)} %reshape.203.tvec_ref, bf16[3,4,512,512]{3,2,1,0:T(8,128)(2,1)} %bitcast.88, bf16[3,4,512,512]{3,2,1,0:T(8,128)(2,1)} %collective-permute-done.refs_1_), custom_call_target="tpu_custom_call" | custom-call | flops 34359738368 | bytes 16777216 | tf_op jit(solution)/shard_map/attend/pallas_call | solution.py:103
  149.5 0.7 reshape.224.gain_ref
  150.2 3.7 collective-permute-done.1
  153.9 1.4 copy-done.10
  155.3 102.6 %feed.1 = (bf16[2048,1024]{1,0:T(8,128)(2,1)}, bf16[2048,1024]{1,0:T(8,128)(2,1)}, bf16[2048,4096]{1,0:T(8,128)(2,1)}, bf16[2048,1024]{1,0:T(8,128)(2,1)}, bf16[...) custom-call(s32[5]{0:T(128)} %pad_add_fusion.info_ref, ...), custom_call_target="tpu_custom_call" | custom-call | flops 77309411328 | bytes 88080384 | tf_op jit(solution)/shard_map/feed/pallas_call | solution.py:651
  257.9 0.2 collective-permute-start.2
  258.1 54.7 %weigh.1 = bf16[16,32,9216]{2,1,0:T(8,128)(2,1)} custom-call(bf16[2048,1024]{1,0:T(8,128)(2,1)} %get-tuple-element.49.mixed_ref, bf16[2048,1024]{1,0:T(8,128)(2,1)} %get-tuple-element.50.low_ref, bf16[2048,1024]{1,0:T(8,128)(2,1)} %get-tuple-element.51.normed_ref, bf16[2048,1024]{1,0:T(8,128)(2,1)} %get-tuple-element.52.grad_ref, ...), custom_call_target="tpu_custom_call" | custom-call | flops 38654705664 | bytes 54525952 | tf_op jit(solution)/shard_map/weigh/pallas_call | solution.py:749
  312.8 1.3 copy-done.9
  314.2 70.1 %unattend.1 = (bf16[3,4,512,512]{3,2,1,0:T(8,128)(2,1)}, bf16[3,4,512,512]{3,2,1,0:T(8,128)(2,1)}, f32[4,2,2048]{2,1,0:T(2,128)}) custom-call(s32[5]{0:T(128)} %pad_add_fusion.info_ref, f32[4,2,2048]{2,1,0:T(2,128)} %reshape.203.tvec_ref, bf16[3,4,512,512]{3,2,1,0:T(8,128)(2,1)} %bitcast.89, bf16[3,4,512,512]{3,2,1,0:T(8,128)(2,1)} %collective-permute-done.refs_1_, ...), custom_call_target="tpu_custom_call" | custom-call | flops 85899345920 | bytes 33554432 | tf_op jit(solution)/shard_map/unattend/pallas_call | solution.py:220
  384.2 0.4 collective-permute-start.3
  384.7 0.9 reshape.217
  385.6 1.3 fusion.3
  387.2 7.6 %collective-permute-done.3 = bf16[3,4,512,512]{3,2,1,0:T(8,128)(2,1)} collective-permute-done((bf16[3,4,512,512]{3,2,1,0:T(8,128)(2,1)}, bf16[3,4,512,512]{3,2,1,0:T(8,128)(2,1)}, u32[]{:S(2)}, u32[]{:S(2)}) %collective-permute-start.3) | collective-permute-done | bytes 6291488 | tf_op jit(solution)/shard_map/ppermute | solution.py:788
  394.8 25.6 %unproject.1 = (f32[2048,1024]{1,0:T(8,128)}, bf16[2048,3072]{1,0:T(8,128)(2,1)}, f32[1,1024]{1,0:T(1,128)}) custom-call(s32[5]{0:T(128)} %pad_add_fusion.info_ref, bf16[2048,1024]{1,0:T(8,128)(2,1)} %bitcast.83, f32[2048,1024]{1,0:T(8,128)} %get-tuple-element.48.residual_ref, f32[1,1024]{1,0:T(1,128)} %reshape.225.gain_ref, bf16[1024,3200]{1,0:T(8,128)(2,1)} %bitcast.78, ...), custom_call_target="tpu_custom_call" | custom-call | flops 12884901888 | bytes 52428800 | tf_op jit(solution)/shard_map/unproject/pallas_call | solution.py:696
  420.3 0.7 convert_reduce_fusion.2
  421.1 0.8 pad.40.clone
  421.9 18.6 %convolution_convert_fusion = bf16[1024,3072]{1,0:T(8,128)(2,1)} fusion(bf16[2048,1024]{1,0:T(8,128)(2,1)} %get-tuple-element.66, bf16[2048,3072]{1,0:T(8,128)(2,1)} %get-tuple-element.67), kind=kOutput, calls=%fused_computation | convolution fusion | flops 12888047616 | bytes 23068672 | tf_op jit(solution)/shard_map/dot_general | solution.py:26
  440.5 79.9 %scatter_rows.1 = (bf16[2,32,128]{2,1,0:T(8,128)(2,1)}, bf16[2,32,3072]{2,1,0:T(8,128)(2,1)}) custom-call(bf16[4,2,2,2,32,128]{5,4,3,2,1,0:T(8,128)(2,1)} %bitcast.69, bf16[4,2,2,2,32,3072]{5,4,3,2,1,0:T(8,128)(2,1)} %bitcast.63), custom_call_target="tpu_custom_call" | custom-call | tf_op jit(solution)/shard_map/scatter_rows/pallas_call | solution.py:503
  520.5 1.0 bitcast_convert_fusion
  521.6 0.5 collective-permute-start.4
  522.0 0.7 bitcast_convert_fusion.1
  522.8 0.6 reshape_squeeze.9
  523.4 0.5 slice_bitcast_fusion
  523.9 0.9 fusion.26
  524.8 1.1 broadcast_select_fusion.1
  526.0 1.2 fusion.6
  527.2 0.7 maximum_convert_fusion.1
  527.9 0.8 reshape.220
  528.7 2.3 copy.43
  531.0 3.5 reshape.221
  534.6 0.7 reshape.222
  535.3 1.6 copy.44
  (59 shorter events, 1.2 us)
Async XLA Ops:
  7.2 6.4 %copy-start.11 = (bf16[2,16]{1,0:T(2,128)(2,1)S(1)}, bf16[2,16]{1,0:T(2,128)(2,1)}, u32[]{:S(2)}) copy-start(bf16[2,16]{1,0:T(2,128)(2,1)} %param.26) | copy-start | bytes 196
  7.2 6.5 %copy-start.12 = (bf16[64]{0:T(256)(128)(2,1)S(1)}, bf16[64]{0:T(256)(128)(2,1)}, u32[]{:S(2)}) copy-start(bf16[64]{0:T(256)(128)(2,1)} %param.18) | copy-start | bytes 388
  7.2 6.5 %copy-start.8 = (bf16[64]{0:T(256)(128)(2,1)S(1)}, bf16[64]{0:T(256)(128)(2,1)}, u32[]{:S(2)}) copy-start(bf16[64]{0:T(256)(128)(2,1)} %param.23) | copy-start | bytes 388
  7.2 6.6 %copy-start.3 = (bf16[64,1024]{1,0:T(8,128)(2,1)S(1)}, bf16[64,1024]{1,0:T(8,128)(2,1)}, u32[]{:S(2)}) copy-start(bf16[64,1024]{1,0:T(8,128)(2,1)} %param.19) | copy-start | bytes 393220
  7.2 6.6 %copy-start.2 = (bf16[64,1024]{1,0:T(8,128)(2,1)S(1)}, bf16[64,1024]{1,0:T(8,128)(2,1)}, u32[]{:S(2)}) copy-start(bf16[64,1024]{1,0:T(8,128)(2,1)} %param.20) | copy-start | bytes 393220
  7.2 6.6 %copy-start.1 = (bf16[64,1024]{1,0:T(8,128)(2,1)S(1)}, bf16[64,1024]{1,0:T(8,128)(2,1)}, u32[]{:S(2)}) copy-start(bf16[64,1024]{1,0:T(8,128)(2,1)} %param.21) | copy-start | bytes 393220
  7.2 68.6 %copy-start.13 = (s32[4]{0:T(128)S(1)}, s32[4]{0:T(128)}, u32[]{:S(2)}) copy-start(s32[4]{0:T(128)} %param.17) | copy-start | bytes 52
  7.2 146.6 %all-gather.2.cloned.1.call-start = ((), (), s32[]{:S(2)}) async-start(), calls=%async_computation.1 | async-start | bytes 17301504 | tf_op jit(solution)/shard_map/all_gather | solution.py:767
  13.6 508.0 %reduce-scatter.2.cloned.1.call-start = ((), (), s32[]{:S(2)}) async-start(), calls=%async_computation.2 | async-start | bytes 10027008 | tf_op jit(solution)/shard_map/reduce_scatter | solution.py:852
  76.5 21.3 %copy-start.7 = (s32[15]{0:T(128)S(1)}, s32[15]{0:T(128)}, u32[]{:S(2)}) copy-start(s32[15]{0:T(128)} %constant.40.clone) | copy-start | bytes 184
  97.5 10.6 %collective-permute-start = (bf16[3,4,512,512]{3,2,1,0:T(8,128)(2,1)}, bf16[3,4,512,512]{3,2,1,0:T(8,128)(2,1)}, u32[]{:S(2)}, u32[]{:S(2)}) collective-permute-start(bf16[3,4,512,512]{3,2,1,0:T(8,128)(2,1)} %bitcast.79), channel_id=1, source_target_pairs={{0,16},{16,0},{1,17},{17,1},{2,18},{18,2},{3,19},{19,3},{4,20},{20... | collective-permute-start | bytes 18874376 | tf_op jit(solution)/shard_map/ppermute | solution.py:783
  97.8 0.6 copy-start.4
  149.5 4.4 collective-permute-start.1
  153.9 1.4 copy-start.10
  257.9 54.9 %collective-permute-start.2 = (bf16[4,512,512]{2,1,0:T(8,128)(2,1)}, bf16[4,512,512]{2,1,0:T(8,128)(2,1)S(1)}, u32[]{:S(2)}, u32[]{:S(2)}) collective-permute-start(bf16[4,512,512]{2,1,0:T(8,128)(2,1)} %bitcast.86), channel_id=1, source_target_pairs={{0,16},{16,0},{1,17},{17,1},{2,18},{18,2},{3,19},{19,3},{4,20},{20... | collective-permute-start | bytes 6291464 | tf_op jit(solution)/shard_map/ppermute | solution.py:783
  312.8 1.4 copy-start.9
  314.2 70.5 %copy-start.6 = (f32[1,1024]{1,0:T(1,128)S(1)}, f32[1,1024]{1,0:T(1,128)}, u32[]{:S(2)}) copy-start(f32[1,1024]{1,0:T(1,128)} %get-tuple-element.64) | copy-start | bytes 12292
  314.2 71.5 %copy-start.5 = (s32[2048]{0:T(1024)S(1)}, s32[2048]{0:T(1024)}, u32[]{:S(2)}) copy-start(s32[2048]{0:T(1024)} %copy-done.4) | copy-start | bytes 24580
  384.2 10.6 %collective-permute-start.3 = (bf16[3,4,512,512]{3,2,1,0:T(8,128)(2,1)}, bf16[3,4,512,512]{3,2,1,0:T(8,128)(2,1)}, u32[]{:S(2)}, u32[]{:S(2)}) collective-permute-start(bf16[3,4,512,512]{3,2,1,0:T(8,128)(2,1)} %get-tuple-element.61), channel_id=1, source_target_pairs={{0,16},{16,0},{1,17},{17,1},{2,18},{18,2},{3,19},{19,3},{4,20},{20... | collective-permute-start | bytes 18874376 | tf_op jit(solution)/shard_map/ppermute | solution.py:788
  521.6 3.3 collective-permute-start.4
  528.7 5.9 %copy-start = (f32[64,4096]{1,0:T(8,128)S(1)}, f32[64,4096]{1,0:T(8,128)}, u32[]{:S(2)}) copy-start(f32[64,4096]{1,0:T(8,128)} %get-tuple-element.73) | copy-start | bytes 3145732
Sparse Core Ops, SparseCore 0:
  13.7 130.9 all-gather.1
  313.0 178.8 reduce-scatter.1

commit v4 on v3

--- a/solution.py
+++ b/solution.py
@@ -286,19 +286,22 @@
         self.place, self.send, self.recv = place, send, recv
         self.made = {}
 
-    def start(self, name, src, dst, to):
-        i = len(self.made)
-        copy = pltpu.make_async_remote_copy(src_ref=src, dst_ref=dst, send_sem=self.send.at[i], recv_sem=self.recv.at[i],
+    def start(self, name, ends, to):
+        self.made[name] = (len(self.made), ends, to)
+        self.copy(name).start()
+
+    def copy(self, name):
+        i, ends, to = self.made[name]
+        src, dst = ends()
+        return pltpu.make_async_remote_copy(src_ref=src, dst_ref=dst, send_sem=self.send.at[i], recv_sem=self.recv.at[i],
                                             device_id=self.place.to[to], device_id_type=pl.DeviceIdType.MESH)
-        copy.start()
-        self.made[name] = copy
 
     def arrived(self, name):
-        self.made[name].wait_recv()
+        self.copy(name).wait_recv()
 
     def finish(self):
-        for copy in self.made.values():
-            copy.wait_send()
+        for name in self.made:
+            self.copy(name).wait_send()
 
 
 def windows(columns, size):
@@ -327,22 +330,22 @@
             copies.arrived(name("z %d" % k))
         source = mine if k == 0 else at(k, p.own)
         if k < 3:
-            copies.start(name("z %d" % (k + 1)), source, at(k, p.own), "up")
-        copies.start(name("u %d" % k), source, at(k, p.own), "u")
-        copies.start(name("w own %d" % k), source, at(k, p.own), "w")
+            copies.start(name("z %d" % (k + 1)), lambda: (source, at(k, p.own)), "up")
+        copies.start(name("u %d" % k), lambda: (source, at(k, p.own)), "u")
+        copies.start(name("w own %d" % k), lambda: (source, at(k, p.own)), "w")
         if k > 0:
-            copies.start(name("core own %d" % k), source, at(k, p.own), "core")
+            copies.start(name("core own %d" % k), lambda: (source, at(k, p.own)), "core")
 
     def turn(k):
         copies.arrived(name("u %d" % k))
-        copies.start(name("w u %d" % k), at(k, p.u), at(k, p.u), "w")
-        copies.start(name("core u %d" % k), at(k, p.u), at(k, p.u), "core")
+        copies.start(name("w u %d" % k), lambda: (at(k, p.u), at(k, p.u)), "w")
+        copies.start(name("core u %d" % k), lambda: (at(k, p.u), at(k, p.u)), "core")
 
     def across(k):
         copies.arrived(name("w own %d" % k))
-        copies.start(name("core w %d" % k), at(k, p.w), at(k, p.w), "core")
+        copies.start(name("core w %d" % k), lambda: (at(k, p.w), at(k, p.w)), "core")
         copies.arrived(name("w u %d" % k))
-        copies.start(name("core uw %d" % k), at(k, p.uw), at(k, p.uw), "core")
+        copies.start(name("core uw %d" % k), lambda: (at(k, p.uw), at(k, p.uw)), "core")
 
     def end():
         for k in range(4):
@@ -366,11 +369,18 @@
 GATHER_COPIES = 3 + 4 + 8 + 15
 
 
-def staggered(chains):
-    for step in range(len(chains) - 1 + max(len(chain) for chain in chains)):
+def lockstep(chains):
+    def run(step):
         for i, chain in enumerate(chains):
             if 0 <= step - i < len(chain):
                 chain[step - i]()
+
+    return [functools.partial(run, step) for step in range(len(chains) - 1 + max(len(chain) for chain in chains))]
+
+
+def staggered(chains):
+    for step in lockstep(chains):
+        step()
 
 
 def gather_kernel(*refs, count):
@@ -438,80 +448,50 @@
     name = lambda s: (i, s)
     line = lambda col: acc.at[:, col[0], col[1]]
     at = lambda z: acc.at[z, p.own[0], p.own[1]]
-    load = pltpu.make_async_copy(grad.at[:, :, :, p.c, :, columns], acc, local.at[i])
+    load = lambda: pltpu.make_async_copy(grad.at[:, :, :, p.c, :, columns], acc, local.at[i])
 
     def first():
-        load.start()
-        copies.start(name("core"), grad.at[:, :, :, p.other, :, columns], came, "core")
+        load().start()
+        copies.start(name("core"), lambda: (grad.at[:, :, :, p.other, :, columns], came), "core")
 
     def second():
-        load.wait()
+        load().wait()
         copies.arrived(name("core"))
         add_into(line(p.uw), came.at[:, p.uw[0], p.uw[1]])
-        copies.start(name("w 1"), line(p.uw), by_w.at[1], "w")
+        copies.start(name("w 1"), lambda: (line(p.uw), by_w.at[1]), "w")
         add_into(line(p.w), came.at[:, p.w[0], p.w[1]])
-        copies.start(name("w 0"), line(p.w), by_w.at[0], "w")
+        copies.start(name("w 0"), lambda: (line(p.w), by_w.at[0]), "w")
         add_into(line(p.u), came.at[:, p.u[0], p.u[1]])
         add_into(line(p.own), came.at[:, p.own[0], p.own[1]])
 
     def third():
         copies.arrived(name("w 1"))
         add_into(line(p.u), by_w.at[1])
-        copies.start(name("u"), line(p.u), by_u, "u")
+        copies.start(name("u"), lambda: (line(p.u), by_u), "u")
         copies.arrived(name("w 0"))
         add_into(line(p.own), by_w.at[0])
 
     def fourth():
         copies.arrived(name("u"))
         add_into(line(p.own), by_u)
-        copies.start(name("z 0"), at(p.down), by_z.at[0], "up")
+        copies.start(name("z 0"), lambda: (at(p.down), by_z.at[0]), "up")
 
     def climb(k, level):
         def run():
             copies.arrived(name("z %d" % k))
             add_into(at(level), by_z.at[k])
-            copies.start(name("z %d" % (k + 1)), at(level), by_z.at[k + 1], "up")
+            copies.start(name("z %d" % (k + 1)), lambda: (at(level), by_z.at[k + 1]), "up")
         return run
 
     def last():
         copies.arrived(name("z 2"))
         out[p.c, :, columns] = at(p.z)[...] + by_z[2]
-        copies.start(name("out"), out.at[p.c, :, columns], out.at[p.c, :, columns], "core")
+        copies.start(name("out"), lambda: (out.at[p.c, :, columns], out.at[p.c, :, columns]), "core")
 
     def end():
         copies.arrived(name("out"))
 
     return [first, second, third, fourth, climb(0, p.far), climb(1, p.up), last, end]
-
-
-def scatter_kernel(*refs, count):
-    grads, outs = refs[:count], refs[count : 2 * count]
-    parts = [(i, window) for i in range(count) for window in windows(grads[i].shape[-1], PIECE)]
-    buffers = [refs[2 * count + SCATTER_BUFFERS * n : 2 * count + SCATTER_BUFFERS * (n + 1)] for n in range(len(parts))]
-    send, recv, local = refs[2 * count + SCATTER_BUFFERS * len(parts) :]
-    place = Place()
-    place.greet()
-    copies = Copies(place, send, recv)
-    staggered([scatter_steps(n, grads[i], outs[i], window, buffers[n], place, copies, local) for n, (i, window) in enumerate(parts)])
-    copies.finish()
-
-
-def scatter_all(grads, collective_id):
-    split = [g.reshape(CHIPS + (2, g.shape[0] // 32, g.shape[1])) for g in grads]
-    count = len(grads)
-    parts = [(g.shape[-2], window[1]) for g in split for window in windows(g.shape[-1], PIECE)]
-    outs = pl.pallas_call(
-        functools.partial(scatter_kernel, count=count),
-        in_specs=[pl.BlockSpec(memory_space=pl.ANY)] * count,
-        out_specs=[pl.BlockSpec(memory_space=pltpu.VMEM)] * count,
-        out_shape=[jax.ShapeDtypeStruct(g.shape[3:], g.dtype) for g in split],
-        scratch_shapes=[b for part in parts for b in scatter_buffers(*part)]
-        + [pltpu.SemaphoreType.DMA((SCATTER_COPIES * len(parts),)), pltpu.SemaphoreType.DMA((SCATTER_COPIES * len(parts),)),
-           pltpu.SemaphoreType.DMA((len(parts),))],
-        compiler_params=pltpu.CompilerParams(collective_id=collective_id, has_side_effects=True, vmem_limit_bytes=60 << 20),
-        name="scatter_rows",
-    )(*split)
-    return [o.reshape(-1, o.shape[-1]) for o in outs]
 
 
 def inverse_root(v):
@@ -584,7 +564,7 @@
     )(info, x, gain, w)
 
 
-def feed_kernel(info_ref, x_ref, cot_ref, gain_ref, wo_ref, w_ref, *refs, parts, block):
+def feed_kernel(info_ref, x_ref, cot_ref, gain_ref, w_ref, *refs, parts, block):
     mixed = refs[:parts]
     mixed_ref, normed_ref, hidden_ref, layer_ref, grad_ref, inner_ref, residual_ref, low_ref, gain_grad_ref = refs[parts : parts + 9]
     grads = refs[parts + 9 : 2 * parts + 9]
@@ -593,14 +573,15 @@
     tile, width = x_ref.shape
     share = width // parts
     chunk = w_ref.shape[0]
-    hidden_width = w_ref.shape[1] // 2
+    hidden_width = (w_ref.shape[1] - chunk) // 2
+    wo = slice(2 * hidden_width, w_ref.shape[1])
     low = jnp.bfloat16
     rows_of = [pl.ds(pl.multiple_of(group(c, j, parts) * share, 128), share) for j in range(parts)]
 
     residual = x_ref[...].astype(jnp.float32)
     for j in range(parts):
         mixed_ref[:, rows_of[j]] = mixed[j][...]
-        residual = residual + dot(mixed[j][...], wo_ref[rows_of[j], :], 1, 0)
+        residual = residual + dot(mixed[j][...], w_ref[rows_of[j], wo], 1, 0)
     root = inverse_root(residual)
     gain = gain_ref[...]
     normed = (residual * root * gain).astype(low)
@@ -637,13 +618,13 @@
     down = down.astype(low)
     low_ref[...] = down
     for j in range(parts):
-        grads[j][...] = dot(down, wo_ref[rows_of[j], :], 1, 1).astype(low)
-
-
-def feed(info, x, cot, gain, wo, w, mixed, block, tile=256):
+        grads[j][...] = dot(down, w_ref[rows_of[j], wo], 1, 1).astype(low)
+
+
+def feed(info, x, cot, gain, w, mixed, block, tile=256):
     parts = len(mixed)
     rows, width = x.shape
-    hidden = w.shape[1] // 2
+    hidden = (w.shape[1] - width) // 2
     tile = min(tile, block)
     share = width // parts
     t = lambda w: tiles((tile, w), 0)
@@ -652,7 +633,7 @@
         functools.partial(feed_kernel, parts=parts, block=block),
         grid_spec=pltpu.PrefetchScalarGridSpec(
             num_scalar_prefetch=1, grid=(rows // tile,),
-            in_specs=[t(width), t(width), resident((1, width)), resident(wo.shape), resident(w.shape)] + [t(share)] * parts,
+            in_specs=[t(width), t(width), resident((1, width)), resident(w.shape)] + [t(share)] * parts,
             out_specs=[t(width), t(width), t(hidden), t(width), t(width), t(hidden), t(width), t(width), resident((1, width))] + [t(share)] * parts,
             scratch_shapes=[pltpu.VMEM((tile, hidden), jnp.bfloat16)]),
         out_shape=[low(width), low(width), low(hidden), low(width), low(width), low(hidden), jax.ShapeDtypeStruct((rows, width), jnp.float32), low(width),
@@ -660,13 +641,39 @@
         compiler_params=params(),
         cost_estimate=cost(rows * width * (8 * hidden + 4 * width), rows * (18 * width + 4 * hidden) + 4 * width * hidden),
         name="feed",
-    )(info, x, cot, gain, wo, w, *mixed)
-
-
-def unproject_kernel(info_ref, x_ref, residual_ref, gain_ref, w_ref, *refs, parts):
-    came = refs[:parts]
-    token_ref, grads_ref, gain_grad_ref = refs[parts:]
-    c = info_ref[0]
+    )(info, x, cot, gain, w, *mixed)
+
+
+def weigh_qkv_kernel(info_ref, normed_ref, *refs, parts):
+    came, out_ref = refs[:parts], refs[parts]
+    for j in range(parts):
+
+        @pl.when(pl.program_id(0) // 3 == j)
+        def _():
+            out_ref[...] = dot(normed_ref[...], came[j][0], 0, 0).astype(jnp.bfloat16)
+
+
+def weigh_qkv(info, normed, came):
+    parts = len(came)
+    rows, width = normed.shape
+    share = width // parts
+    piece = pl.BlockSpec((1, rows, share), lambda i, n: (i % 3, 0, 0))
+    return pl.pallas_call(
+        functools.partial(weigh_qkv_kernel, parts=parts),
+        grid_spec=pltpu.PrefetchScalarGridSpec(
+            num_scalar_prefetch=1, grid=(3 * parts,),
+            in_specs=[resident((rows, width))] + [piece] * parts,
+            out_specs=pl.BlockSpec((width, share), lambda i, n: (0, (i % 3) * parts + (n[0] + i // 3) % parts))),
+        out_shape=jax.ShapeDtypeStruct((width, 3 * width), jnp.bfloat16),
+        compiler_params=params(),
+        cost_estimate=cost(6 * rows * width * width, 8 * rows * width + 6 * width * width),
+        name="weigh_qkv",
+    )(info, normed, *came)
+
+
+def settle_tile(x_ref, residual_ref, gain_ref, w_ref, came, token_ref):
+    parts = len(came)
+    c = lax.axis_index("ctx")
     x = x_ref[...].astype(jnp.float32)
     width = x.shape[1]
     share = width // parts
@@ -674,36 +681,68 @@
     for j in range(parts):
         for t in range(3):
             at = pl.ds(pl.multiple_of(t * width + group(c, j, parts) * share, 128), share)
-            piece = came[j][t]
-            grads_ref[:, at] = piece
-            part = dot(piece, w_ref[:, at], 1, 1)
+            part = dot(came[j][t], w_ref[:, at], 1, 1)
             up = part if up is None else up + part
-    down, gain_grad = norm_back(x, inverse_root(x), gain_ref[...], up)
-
-    @pl.when(pl.program_id(0) == 0)
+    down, _ = norm_back(x, inverse_root(x), gain_ref[...], up)
+    token_ref[...] = residual_ref[...] + down
+
+
+def settle_kernel(x_ref, residual_ref, gain_ref, w_ref, *refs, parts, count, tiled):
+    came, grads, token_ref, outs = refs[:parts], refs[parts : parts + count], refs[parts + count], refs[parts + count + 1 : parts + 2 * count + 1]
+    scratch = refs[parts + 2 * count + 1 :]
+    sums, buffers, (send, recv, local) = scratch[:count], scratch[count:-3], scratch[-3:]
+    i = pl.program_id(0)
+    if count:
+        place = Place()
+        copies = Copies(place, send, recv)
+        windows_of = [(n, window) for n in range(count) for window in windows(grads[n].shape[-1], PIECE)]
+        chains = [scatter_steps(k, grads[n], sums[n], window, buffers[SCATTER_BUFFERS * k : SCATTER_BUFFERS * (k + 1)], place, copies, local)
+                  for k, (n, window) in enumerate(windows_of)]
+        pl.when(i == 0)(place.greet)
+        for n, step in enumerate(lockstep(chains)):
+            pl.when(i == n)(step)
+
+    @pl.when(i < tiled)
     def _():
-        gain_grad_ref[...] = jnp.zeros_like(gain_grad_ref)
-
-    gain_grad_ref[...] += gain_grad
-    token_ref[...] = residual_ref[...] + down
-
-
-def unproject(info, x, residual, gain, w, came):
-    parts = len(came)
+        settle_tile(x_ref, residual_ref, gain_ref, w_ref, came, token_ref)
+
+    if count:
+
+        @pl.when(i == pl.num_programs(0) - 1)
+        def _():
+            copies.finish()
+            for n in range(count):
+                outs[n][...] = sums[n][...]
+
+
+def settle(x, residual, gain, w, came, grads, collective_id):
+    parts, count = len(came), len(grads)
     rows, width = x.shape
     tile = min(256, rows)
+    tiled = rows // tile
     share = width // parts
-    return pl.pallas_call(
-        functools.partial(unproject_kernel, parts=parts),
-        grid_spec=pltpu.PrefetchScalarGridSpec(
-            num_scalar_prefetch=1, grid=(rows // tile,),
-            in_specs=[tiles((tile, width), 0), tiles((tile, width), 0), resident((1, width)), resident(w.shape)] + [tiles((3, tile, share), 1)] * parts,
-            out_specs=[tiles((tile, width), 0), tiles((tile, 3 * width), 0), resident((1, width))]),
-        out_shape=[jax.ShapeDtypeStruct((rows, width), jnp.float32), jax.ShapeDtypeStruct((rows, 3 * width), jnp.bfloat16), jax.ShapeDtypeStruct((1, width), jnp.float32)],
-        compiler_params=params(),
-        cost_estimate=cost(6 * rows * width * width, 22 * rows * width + 6 * width * width),
-        name="unproject",
-    )(info, x, residual, gain, w, *came)
+    split = [g.reshape(CHIPS + (2, g.shape[0] // 32, g.shape[1])) for g in grads]
+    pieces = [(g.shape[-2], window[1]) for g in split for window in windows(g.shape[-1], PIECE)]
+    steps = max(tiled, len(pieces) + 7) if count else tiled
+    at = lambda i: jnp.minimum(i, tiled - 1)
+    row = pl.BlockSpec((tile, width), lambda i: (at(i), 0))
+    fixed = lambda shape: pl.BlockSpec(shape, lambda i: (0,) * len(shape), pipeline_mode=pl.Buffered(1))
+    copied = SCATTER_COPIES * len(pieces)
+    semaphores = [pltpu.SemaphoreType.DMA((max(n, 1),)) for n in (copied, copied, len(pieces))]
+    extra = dict(collective_id=collective_id, has_side_effects=True) if count else {}
+    token, *outs = pl.pallas_call(
+        functools.partial(settle_kernel, parts=parts, count=count, tiled=tiled),
+        grid=(steps,),
+        in_specs=[row, row, fixed((1, width)), fixed(w.shape)] + [pl.BlockSpec((3, tile, share), lambda i: (0, at(i), 0))] * parts
+        + [pl.BlockSpec(memory_space=pl.ANY)] * count,
+        out_specs=[row] + [fixed(g.shape[3:]) for g in split],
+        out_shape=[jax.ShapeDtypeStruct((rows, width), jnp.float32)] + [jax.ShapeDtypeStruct(g.shape[3:], g.dtype) for g in split],
+        scratch_shapes=[pltpu.VMEM(g.shape[3:], g.dtype) for g in split] + [b for p in pieces for b in scatter_buffers(*p)] + semaphores,
+        compiler_params=pltpu.CompilerParams(vmem_limit_bytes=VMEM_LIMIT, **extra),
+        cost_estimate=cost(6 * rows * width * width, 16 * rows * width + 6 * width * width),
+        name="settle",
+    )(x, residual, gain, w, *came, *split)
+    return token, [o.reshape(-1, o.shape[-1]) for o in outs]
 
 
 def weigh_kernel(mixed_ref, low_ref, normed_ref, grad_ref, inner_ref, hidden_ref, out_ref, made_ref, came_ref, send, recv, *, slabs):
@@ -820,14 +859,11 @@
 
     inner = inner_weight.reshape(shard, n_fsdp, slabs, shard).transpose(0, 2, 1, 3).reshape(shard, hidden_width)
     outer = outer_weight.reshape(slabs, shard, width).transpose(1, 0, 2).reshape(shard, slabs * width)
-    w_feed = gather_rows(jnp.concatenate([inner, outer], axis=1))
+    w_feed = gather_rows(jnp.concatenate([inner, outer, output_weight], axis=1))
     side = jnp.stack([wide(norm_gain), wide(ffn_gain), wide(bias_table.reshape(small))])
     side = jnp.pad(side, ((0, shard - 3), (0, 0)))
     first = jnp.concatenate([query_weight, key_weight, value_weight, side], axis=1)
-    if remote:
-        first, w_output = gather_all([first, output_weight], 1)
-    else:
-        first, w_output = gather_rows(first), gather_rows(output_weight)
+    first = gather_all([first], 1)[0] if remote else gather_rows(first)
     side = first[:, 3 * width :].reshape(n_fsdp, shard, 128)
     gain_one = side[:, 0, :shard].reshape(1, width).astype(jnp.float32)
     gain_two = side[:, 1, :shard].reshape(1, width).astype(jnp.float32)
@@ -843,7 +879,7 @@
     *out, lse = attend(info, vector_q, qkv, HEAD_DIM)
     mixed = [m.reshape(rows, share) for m in give_back(out)]
     (mixed, normed_ffn, hidden, layer_out, grad_out, grad_inner, grad_residual, grad_low, ffn_gain_grad, *grad_mixed) = feed(
-        info, x, cot, gain_two, w_output, w_feed, mixed, block)
+        info, x, cot, gain_two, w_feed, mixed, block)
     grad_mixed = exchange([g.reshape(seqs, block, share) for g in grad_mixed])
 
     if remote:
@@ -858,26 +894,28 @@
 
     *grads, diagonals = unattend(info, vector_k, qkv, out, grad_mixed, lse, HEAD_DIM)
     grads = [g.reshape(3, rows, share) for g in give_back(grads)]
-    token_grad, grads, norm_gain_grad = unproject(info, x, grad_residual, gain_one, first, grads)
-    qkv_grad = dot(normed, grads, 0, 0).astype(low)
+    qkv_grad = weigh_qkv(info, normed, grads)
 
     own_sums = table_sums(diagonals.reshape(own_heads, 2 * seq_len), buckets, seq_len)
     sums = lax.dynamic_update_slice_in_dim(jnp.zeros((buckets, heads), jnp.float32), own_sums, c * own_heads, 1)
-    side = jnp.stack([wide(norm_gain_grad.reshape(n_fsdp, shard)), wide(ffn_gain_grad.reshape(n_fsdp, shard)), wide(sums.reshape(n_fsdp, small))], axis=1)
-    side = jnp.pad(side.astype(low), ((0, 0), (0, shard - 3), (0, 0))).reshape(n_fsdp * shard, 128)
+    side = jnp.stack([wide(ffn_gain_grad.reshape(n_fsdp, shard)), wide(sums.reshape(n_fsdp, small))], axis=1)
+    side = jnp.pad(side.astype(low), ((0, 0), (0, shard - 2), (0, 0))).reshape(n_fsdp * shard, 128)
     if remote:
-        side, qkv_grad = scatter_all([side, qkv_grad], 2)
+        token_grad, (side, qkv_grad) = settle(x, grad_residual, gain_one, first, grads, [side, qkv_grad], 2)
     else:
+        token_grad, _ = settle(x, grad_residual, gain_one, first, grads, [], 2)
         side, qkv_grad = scatter_rows(side), scatter_rows(qkv_grad)
 
     full = jnp.float32
     side = side.astype(full)
     qkv_grad = qkv_grad.astype(full)
     feed_grad = feed_grad.astype(full)
+    weights = jnp.concatenate([query_weight, key_weight, value_weight], axis=1).astype(full)
+    norm_gain_grad = jnp.sum(weights * qkv_grad, axis=1) / norm_gain.astype(full)
     inner_grad = feed_grad[:, width : width + hidden_width].reshape(shard, slabs, n_fsdp, shard).transpose(0, 2, 1, 3).reshape(shard, hidden_width)
     outer_grad = feed_grad[:, width + hidden_width :].reshape(shard, slabs, width).transpose(1, 0, 2).reshape(slabs * shard, width)
-    return (layer_out.reshape(tokens.shape), token_grad.reshape(tokens.shape), side[0, :shard], qkv_grad[:, :width], qkv_grad[:, width : 2 * width],
-            qkv_grad[:, 2 * width :], feed_grad[:, :width], side[1, :shard], inner_grad, outer_grad, side[2, :small].reshape(bias_table.shape))
+    return (layer_out.reshape(tokens.shape), token_grad.reshape(tokens.shape), norm_gain_grad, qkv_grad[:, :width], qkv_grad[:, width : 2 * width],
+            qkv_grad[:, 2 * width :], feed_grad[:, :width], side[0, :shard], inner_grad, outer_grad, side[1, :small].reshape(bias_table.shape))
 
 
 def solution(mesh):

time: 547 us -> 538 us (0.984)
  matrix products: 20.8 us -> 2.13 us
  local copies, waits for them, and re-layouts: 25 us -> 31.4 us
    dot_general x1 -> x0, matrix products: 18.6 us -> none  [dot(): lax.dot_general(a, b, (((ca,), (cb,)), ((), ())), precision=precision, pr...]
    pallas_call x1, Pallas kernels: 59.6 us -> 47.7 us  [gather_all(): pl.pallas_call(functools.partial(gather_kernel, count=count), in_specs=[a...]
    pallas_call x1, Pallas kernels: 70.1 us -> 78.4 us  [unattend(): pl.pallas_call(functools.partial(unattend_kernel, seq_len=seq_len, head_d...]
    unnamed x31 -> x44, local copies, waits for them, and re-layouts: 3.52 us -> 10 us
  transfers between devices with their start and end apart: 7 -> 7, of which waited for: 3 -> 4; matrix products, arithmetic and copies ran while one was open for 6% -> 3% of each run, Pallas kernels for 65% -> 66%
where the time goes in v4:
time: 538 us; the launch traced here: 532 us
  Pallas kernels  452 us (84%)
  local copies, waits for them, and re-layouts  31.4 us (6%)
  waiting for transfers between devices  21.7 us (4%)
  between operations  14.6 us (3%)
  other arithmetic  7.92 us (1%)
    pallas_call x1, Pallas kernels, feed(): pl.pallas_call(functools.partial(feed_kernel, parts=parts, block=block),...  102 us
    pallas_call x1, Pallas kernels, settle(): pl.pallas_call(functools.partial(settle_kernel, parts=parts, count=count,...  83.6 us
    pallas_call x1, Pallas kernels, unattend(): pl.pallas_call(functools.partial(unattend_kernel, seq_len=seq_len, head_d...  78.4 us
    pallas_call x1, Pallas kernels, weigh(): pl.pallas_call(functools.partial(weigh_kernel, slabs=slabs), grid=(total...  54.7 us
    pallas_call x1, Pallas kernels, gather_all(): pl.pallas_call(functools.partial(gather_kernel, count=count), in_specs=[a...  47.7 us
    pallas_call x1, Pallas kernels, attend(): pl.pallas_call(functools.partial(attend_kernel, seq_len=seq_len, head_dim...  44 us
    pallas_call x1, Pallas kernels, project(): pl.pallas_call(functools.partial(project_kernel, parts=parts), grid_spec=...  21 us
    pallas_call x1, Pallas kernels, weigh_qkv(): pl.pallas_call(functools.partial(weigh_qkv_kernel, parts=parts), grid_spe...  20.5 us
  transfers between devices with their start and end apart: 7, of which 4 were waited for; matrix products, arithmetic and copies ran while one was open for 3% of the time, Pallas kernels for 66%

profile of v4, /device:TPU:0, one launch (start us, length us, event | category | flops | bytes accessed | tf_op | source)
XLA Modules:
  0.0 532.2 jit_solution(639611968419599159)
XLA Ops:
  7.2 2.6 reshape.191
  9.9 0.3 copy.50
  10.2 0.8 reshape.192
  11.0 0.4 copy.39
  11.6 0.9 fusion.4
  12.7 0.8 pad_maximum_fusion.1
  13.5 47.7 %gather_rows.1 = bf16[4,2,2,2,32,3200]{5,4,3,2,1,0:T(8,128)(2,1)} custom-call(bf16[2,32,3200]{2,1,0:T(8,128)(2,1)} %bitcast.66), custom_call_target="tpu_custom_call" | custom-call | tf_op jit(solution)/shard_map/gather_rows/pallas_call | solution.py:402
  61.3 1.0 slice.48
  62.3 0.7 reshape.216.gain_ref
  63.0 0.6 pad_add_fusion.info_ref
  63.6 21.0 %project.1 = (bf16[2048,1024]{1,0:T(8,128)(2,1)}, bf16[3,2048,512]{2,1,0:T(8,128)(2,1)}, bf16[3,2048,512]{2,1,0:T(8,128)(2,1)}) custom-call(s32[5]{0:T(128)} %pad_add_fusion.info_ref, bf16[2048,1024]{1,0:T(8,128)(2,1)} %bitcast.78, f32[1,1024]{1,0:T(1,128)} %reshape.216.gain_ref, bf16[1024,3200]{1,0:T(8,128)(2,1)} %bitcast.59), custom_call_target="tpu_custom_call" | custom-call | flops 12884901888 | bytes 27262976 | tf_op jit(solution)/shard_map/project/pallas_call | solution.py:554
  84.5 0.5 collective-permute-start
  85.3 0.9 fusion.1
  86.2 0.7 reshape.195.tvec_ref
  86.8 8.3 %collective-permute-done.refs_1_ = bf16[3,4,512,512]{3,2,1,0:T(8,128)(2,1)} collective-permute-done((bf16[3,4,512,512]{3,2,1,0:T(8,128)(2,1)}, bf16[3,4,512,512]{3,2,1,0:T(8,128)(2,1)}, u32[]{:S(2)}, u32[]{:S(2)}) %collective-permute-start) | collective-permute-done | bytes 6291488 | tf_op jit(solution)/shard_map/ppermute | solution.py:822
  95.2 44.0 %attend.1 = (bf16[4,512,512]{2,1,0:T(8,128)(2,1)}, bf16[4,512,512]{2,1,0:T(8,128)(2,1)}, f32[4,4,2,1024]{3,2,1,0:T(2,128)}) custom-call(s32[5]{0:T(128)} %pad_add_fusion.info_ref, f32[4,2,2048]{2,1,0:T(2,128)} %reshape.195.tvec_ref, bf16[3,4,512,512]{3,2,1,0:T(8,128)(2,1)} %bitcast.83, bf16[3,4,512,512]{3,2,1,0:T(8,128)(2,1)} %collective-permute-done.refs_1_), custom_call_target="tpu_custom_call" | custom-call | flops 34359738368 | bytes 16777216 | tf_op jit(solution)/shard_map/attend/pallas_call | solution.py:103
  139.2 0.4 collective-permute-start.1
  139.7 0.7 reshape.215.gain_ref
  140.3 4.5 collective-permute-done.1
  144.8 2.0 all-gather.2.cloned.1.call-done.w_ref
  146.8 102.5 %feed.1 = (bf16[2048,1024]{1,0:T(8,128)(2,1)}, bf16[2048,1024]{1,0:T(8,128)(2,1)}, bf16[2048,4096]{1,0:T(8,128)(2,1)}, bf16[2048,1024]{1,0:T(8,128)(2,1)}, bf16[...) custom-call(s32[5]{0:T(128)} %pad_add_fusion.info_ref, ...), custom_call_target="tpu_custom_call" | custom-call | flops 77309411328 | bytes 88080384 | tf_op jit(solution)/shard_map/feed/pallas_call | solution.py:632
  249.2 0.3 collective-permute-start.2
  249.6 54.7 %weigh.1 = bf16[16,32,9216]{2,1,0:T(8,128)(2,1)} custom-call(bf16[2048,1024]{1,0:T(8,128)(2,1)} %get-tuple-element.43.mixed_ref, bf16[2048,1024]{1,0:T(8,128)(2,1)} %get-tuple-element.44.low_ref, bf16[2048,1024]{1,0:T(8,128)(2,1)} %get-tuple-element.45.normed_ref, bf16[2048,1024]{1,0:T(8,128)(2,1)} %get-tuple-element.46.grad_ref, ...), custom_call_target="tpu_custom_call" | custom-call | flops 38654705664 | bytes 54525952 | tf_op jit(solution)/shard_map/weigh/pallas_call | solution.py:788
  304.3 1.3 copy-done.14
  305.6 78.4 %unattend.1 = (bf16[3,4,512,512]{3,2,1,0:T(8,128)(2,1)}, bf16[3,4,512,512]{3,2,1,0:T(8,128)(2,1)}, f32[4,2,2048]{2,1,0:T(2,128)}) custom-call(s32[5]{0:T(128)} %pad_add_fusion.info_ref, f32[4,2,2048]{2,1,0:T(2,128)} %reshape.195.tvec_ref, bf16[3,4,512,512]{3,2,1,0:T(8,128)(2,1)} %bitcast.84, bf16[3,4,512,512]{3,2,1,0:T(8,128)(2,1)} %collective-permute-done.refs_1_, ...), custom_call_target="tpu_custom_call" | custom-call | flops 85899345920 | bytes 33554432 | tf_op jit(solution)/shard_map/unattend/pallas_call | solution.py:220
  383.9 0.3 collective-permute-start.3
  384.4 0.9 reshape.207
  385.3 1.3 fusion.5
  386.8 0.8 pad.35.clone
  387.6 6.9 %collective-permute-done.3 = bf16[3,4,512,512]{3,2,1,0:T(8,128)(2,1)} collective-permute-done((bf16[3,4,512,512]{3,2,1,0:T(8,128)(2,1)}, bf16[3,4,512,512]{3,2,1,0:T(8,128)(2,1)}, u32[]{:S(2)}, u32[]{:S(2)}) %collective-permute-start.3) | collective-permute-done | bytes 6291488 | tf_op jit(solution)/shard_map/ppermute | solution.py:827
  394.5 20.5 %weigh_qkv.1 = bf16[1024,3072]{1,0:T(8,128)(2,1)} custom-call(s32[5]{0:T(128)} %pad_add_fusion.info_ref, bf16[2048,1024]{1,0:T(8,128)(2,1)} %get-tuple-element.58.normed_ref, bf16[3,2048,512]{2,1,0:T(8,128)(2,1)} %bitcast.85, bf16[3,2048,512]{2,1,0:T(8,128)(2,1)} %bitcast.20.refs_1_), custom_call_target="tpu_custom_call" | custom-call | flops 12884901888 | bytes 23068672 | tf_op jit(solution)/shard_map/weigh_qkv/pallas_call | solution.py:661
  415.0 83.6 %settle.1 = (f32[2048,1024]{1,0:T(8,128)}, bf16[2,32,128]{2,1,0:T(8,128)(2,1)}, bf16[2,32,3072]{2,1,0:T(8,128)(2,1)}) custom-call(bf16[2048,1024]{1,0:T(8,128)(2,1)} %bitcast.80, f32[2048,1024]{1,0:T(8,128)} %get-tuple-element.42.residual_ref, f32[1,1024]{1,0:T(1,128)} %reshape.216.gain_ref, bf16[1024,3200]{1,0:T(8,128)(2,1)} %bitcast.60, ...), custom_call_target="tpu_custom_call" | custom-call | flops 12884901888 | bytes 39845888 | tf_op jit(solution)/shard_map/settle/pallas_call | solution.py:733
  498.6 0.7 bitcast_convert_fusion
  499.3 0.6 reshape_squeeze.9
  500.0 1.2 multiply_reduce_fusion
  501.3 0.4 collective-permute-start.4
  501.7 0.5 convert_divide_fusion
  502.2 0.5 slice_bitcast_fusion
  502.7 1.9 fusion.27
  504.6 1.1 broadcast_select_fusion.1
  505.8 1.2 fusion.7
  507.0 0.7 maximum_convert_fusion.1
  507.7 0.8 reshape.211
  508.5 2.3 copy.43
  510.8 3.5 reshape.212
  514.4 0.7 reshape.213
  515.1 1.6 copy.44
  516.6 8.4 %copy.53 = f32[4,512,1024]{2,1,0:T(8,128)} copy(f32[4,512,1024]{2,1,0:T(8,128)} %bitcast.56) | data formatting | bytes 16777216
  (70 shorter events, 1.2 us)
Async XLA Ops:
  7.2 3.8 copy-start.1
  7.2 4.4 copy-start.8
  7.2 139.6 %all-gather.2.cloned.1.call-start = ((), (), s32[]{:S(2)}) async-start(), calls=%async_computation.1 | async-start | bytes 19464192 | tf_op jit(solution)/shard_map/all_gather | solution.py:806
  9.9 2.7 copy-start.16
  9.9 2.8 copy-start.18
  9.9 2.8 copy-start.13
  9.9 2.8 copy-start.2
  9.9 2.8 copy-start.4
  9.9 2.8 copy-start.6
  12.5 50.4 %copy-start.17 = (s32[4]{0:T(128)S(1)}, s32[4]{0:T(128)}, u32[]{:S(2)}) copy-start(s32[4]{0:T(128)} %param.17) | copy-start | bytes 52
  12.5 488.7 %reduce-scatter.2.cloned.1.call-start = ((), (), s32[]{:S(2)}) async-start(), calls=%async_computation.2 | async-start | bytes 10027008 | tf_op jit(solution)/shard_map/reduce_scatter | solution.py:888
  63.5 21.6 %copy-start.12 = (s32[15]{0:T(128)S(1)}, s32[15]{0:T(128)}, u32[]{:S(2)}) copy-start(s32[15]{0:T(128)} %constant.41.clone) | copy-start | bytes 184
  84.5 10.6 %collective-permute-start = (bf16[3,4,512,512]{3,2,1,0:T(8,128)(2,1)}, bf16[3,4,512,512]{3,2,1,0:T(8,128)(2,1)}, u32[]{:S(2)}, u32[]{:S(2)}) collective-permute-start(bf16[3,4,512,512]{3,2,1,0:T(8,128)(2,1)} %bitcast.76), channel_id=1, source_target_pairs={{0,16},{16,0},{1,17},{17,1},{2,18},{18,2},{3,19},{19,3},{4,20},{20... | collective-permute-start | bytes 18874376 | tf_op jit(solution)/shard_map/ppermute | solution.py:822
  85.3 53.9 %copy-start.9 = (s32[2048]{0:T(1024)}, s32[2048]{0:T(1024)S(1)}, u32[]{:S(2)}) copy-start(s32[2048]{0:T(1024)S(1)} %select_add_fusion) | copy-start | bytes 24580
  139.2 5.6 %collective-permute-start.1 = (bf16[4,512,512]{2,1,0:T(8,128)(2,1)}, bf16[4,512,512]{2,1,0:T(8,128)(2,1)S(1)}, u32[]{:S(2)}, u32[]{:S(2)}) collective-permute-start(bf16[4,512,512]{2,1,0:T(8,128)(2,1)} %get-tuple-element.40.refs_3_), channel_id=1, source_target_pairs={{0,16},{16,0},{1,17},{17,1},{2,18},{18,2},{3,19},{19,3},{4,20},{20... | collective-permute-start | bytes 6291464 | tf_op jit(solution)/shard_map/ppermute | solution.py:827
  144.8 2.0 copy-start.15
  249.2 55.0 %collective-permute-start.2 = (bf16[4,512,512]{2,1,0:T(8,128)(2,1)}, bf16[4,512,512]{2,1,0:T(8,128)(2,1)S(1)}, u32[]{:S(2)}, u32[]{:S(2)}) collective-permute-start(bf16[4,512,512]{2,1,0:T(8,128)(2,1)} %bitcast.82), channel_id=1, source_target_pairs={{0,16},{16,0},{1,17},{17,1},{2,18},{18,2},{3,19},{19,3},{4,20},{20... | collective-permute-start | bytes 6291464 | tf_op jit(solution)/shard_map/ppermute | solution.py:822
  304.2 1.3 copy-start.14
  305.5 78.7 %copy-start.11 = (f32[1,1024]{1,0:T(1,128)S(1)}, f32[1,1024]{1,0:T(1,128)}, u32[]{:S(2)}) copy-start(f32[1,1024]{1,0:T(1,128)} %get-tuple-element.56) | copy-start | bytes 12292
  305.6 79.7 %copy-start.10 = (s32[2048]{0:T(1024)S(1)}, s32[2048]{0:T(1024)}, u32[]{:S(2)}) copy-start(s32[2048]{0:T(1024)} %copy-done.9) | copy-start | bytes 24580
  383.9 10.6 %collective-permute-start.3 = (bf16[3,4,512,512]{3,2,1,0:T(8,128)(2,1)}, bf16[3,4,512,512]{3,2,1,0:T(8,128)(2,1)}, u32[]{:S(2)}, u32[]{:S(2)}) collective-permute-start(bf16[3,4,512,512]{3,2,1,0:T(8,128)(2,1)} %get-tuple-element.55), channel_id=1, source_target_pairs={{0,16},{16,0},{1,17},{17,1},{2,18},{18,2},{3,19},{19,3},{4,20},{20... | collective-permute-start | bytes 18874376 | tf_op jit(solution)/shard_map/ppermute | solution.py:827
  415.0 85.0 %copy-start.3 = (bf16[64,1024]{1,0:T(8,128)(2,1)S(1)}, bf16[64,1024]{1,0:T(8,128)(2,1)}, u32[]{:S(2)}) copy-start(bf16[64,1024]{1,0:T(8,128)(2,1)} %param.21) | copy-start | bytes 393220
  415.0 85.0 %copy-start.5 = (bf16[64,1024]{1,0:T(8,128)(2,1)S(1)}, bf16[64,1024]{1,0:T(8,128)(2,1)}, u32[]{:S(2)}) copy-start(bf16[64,1024]{1,0:T(8,128)(2,1)} %param.20) | copy-start | bytes 393220
  415.0 85.0 %copy-start.7 = (bf16[64,1024]{1,0:T(8,128)(2,1)S(1)}, bf16[64,1024]{1,0:T(8,128)(2,1)}, u32[]{:S(2)}) copy-start(bf16[64,1024]{1,0:T(8,128)(2,1)} %param.19) | copy-start | bytes 393220
  415.0 86.7 %copy-start.19 = (bf16[64]{0:T(256)(128)(2,1)S(1)}, bf16[64]{0:T(256)(128)(2,1)}, u32[]{:S(2)}) copy-start(bf16[64]{0:T(256)(128)(2,1)} %param.18) | copy-start | bytes 388
  501.3 3.4 collective-permute-start.4
  508.5 5.8 %copy-start = (f32[64,4096]{1,0:T(8,128)S(1)}, f32[64,4096]{1,0:T(8,128)}, u32[]{:S(2)}) copy-start(f32[64,4096]{1,0:T(8,128)} %get-tuple-element.65) | copy-start | bytes 3145732
Sparse Core Ops, SparseCore 0:
  12.6 134.0 all-gather.1
  304.4 178.1 reduce-scatter.1
